TPU v7x, 32 devices: a whole 2x2x4 slice. The times are simulated.
32 devices in a mesh: wide: 8 (over z, y), narrow: 4 (over x, core).
Axes of the slice: x: 2, y: 2, z: 4, core: 2. Of those that a mesh axis runs over, the one named last changes fastest.
Arguments:
- trace_parts: float32 [16384, 384], P(('wide', 'narrow')), may hold values from -6 to 6
- node_slab: int32 [16384, 1], P(('wide', 'narrow')), may hold values from 0 to 7; in each aligned block of 512 rows (0 to 511, 512 to 1023, ...) at most 160 rows name the same one
- node_local: int32 [16384], P(('wide', 'narrow')), may hold values from 0 to 255
- solid_fraction: float32 [4, 2048], P('narrow', 'wide'), may hold values from 0.3 to 0.7
- influence: bfloat16 [4, 2048, 4, 2048], P(None, 'wide', 'narrow'), may hold values from -0.0625 to 0.0625
Outputs:
- boundary_potential: float32 [4, 2048, 384], P('narrow', 'wide')
- dirichlet: float32 [16384, 384], P(('wide', 'narrow'))
Inputs may be any that keep to these rules, and one draw needn't show every extreme that they name: `node_slab`: in the slots of one partition at most 160 name one target slab; some partition reaches 160.
All inputs are finite; a program needn't handle non-finite values.
Results may differ from a plain program's by a relative error of at most 0.0026.
Values may be sent and summed in bfloat16 or wider, within the bound.
No kernel may reach another device: no remote copies, remote signals or barrier semaphores. Data moves between devices by JAX's collectives and lax.ppermute only.
A program may use at most 128 MiB of HBM per device.

v0:
```python
import jax
import jax.numpy as jnp
from jax import lax
from jax.sharding import PartitionSpec as P


def on_device(trace_parts, node_slab, node_local, solid_fraction, influence):
    node_dev = solid_fraction.shape[1]
    images = trace_parts.shape[1]
    wide_count = lax.axis_size("wide")
    narrow_count = lax.axis_size("narrow")
    dest_slab = node_slab[:, 0]
    spread = (
        jnp.zeros((wide_count, node_dev, images), jnp.float32)
        .at[dest_slab, node_local]
        .add(trace_parts)
    )
    arrived = lax.all_to_all(spread, "wide", split_axis=0, concat_axis=0, tiled=True)
    first_trace = jnp.sum(arrived, axis=0)
    trace_round = first_trace.astype(jnp.bfloat16)
    matrix_block = influence.reshape(narrow_count * node_dev, wide_count * node_dev)
    partial_sum = jnp.dot(
        matrix_block,
        lax.all_gather(trace_round, "wide", axis=0, tiled=True),
        preferred_element_type=jnp.float32,
    )
    layer = lax.psum_scatter(
        partial_sum.reshape(narrow_count, node_dev, images),
        "narrow",
        scatter_dimension=0,
        tiled=True,
    )
    boundary_potential = layer + (solid_fraction[:, :, None] - 1.0) * first_trace[None, :, :]
    gathered_all = lax.all_gather(boundary_potential[0], "wide", axis=0, tiled=True)
    dirichlet = gathered_all[dest_slab * node_dev + node_local]
    return (boundary_potential, dirichlet)


def solution(mesh):
    placed = (
        P(("wide", "narrow"), None),
        P(("wide", "narrow"), None),
        P(("wide", "narrow")),
        P("narrow", "wide"),
        P(None, "wide", "narrow", None),
    )
    return jax.shard_map(
        on_device,
        mesh=mesh,
        in_specs=placed,
        out_specs=(P("narrow", "wide", None), P(("wide", "narrow"), None)),
        check_vma=False,
    )
```

profile of v0, /device:TPU:0, one launch (start us, length us, event | category | flops | bytes accessed | tf_op | source)
XLA Modules:
  0.0 281.2 jit_solution(3625069149958038650)
XLA Ops:
  7.2 0.0 all-gather.4.cloned.1.call-start
  7.2 0.7 broadcast_multiply_fusion
  7.9 0.7 compare_select_fusion.1
  8.6 0.7 or_select_fusion
  9.3 0.2 broadcast_in_dim.12
  9.5 39.9 %scatter_fusion = f32[8,256,384]{2,1,0:T(8,128)S(1)} fusion(f32[8,256,384]{2,1,0:T(8,128)S(1)} %broadcast_in_dim.12, s32[512]{0:T(512)S(1)} %bitcast.15, f32[512,384]{1,0:T(8,128)} %param.5), kind=kCustom, calls=%fused_computation.1 | custom fusion | flops 196608 | bytes 2363392 | tf_op jit(solution)/shard_map/scatter-add | solution.py:16
  49.4 77.9 %all_to_all.5 = f32[8,256,384]{2,1,0:T(8,128)} all-to-all(f32[8,256,384]{2,1,0:T(8,128)S(1)} %scatter_fusion), channel_id=1, replica_groups=mesh['wide'=8,'narrow'=4] {'wide'}, dimensions={0} | all-to-all | bytes 6291456 | tf_op jit(solution)/shard_map/all_to_all | solution.py:18
  127.3 2.1 reduce_sum.11
  129.4 0.7 convert_element_type.3
  130.1 0.0 all-gather.4.cloned.1.call-update
  130.1 0.0 reduce-scatter.2.cloned.1.call-start
  130.1 43.3 %all-gather.4.cloned.1.call-done = bf16[2048,384]{1,0:T(8,128)(2,1)} async-done(((bf16[256,384]{1,0:T(8,128)(2,1)}), bf16[2048,384]{1,0:T(8,128)(2,1)}) %all-gather.4.cloned.1.call-update) | async-done | bytes 1572880 | tf_op jit(solution)/shard_map/all_gather | solution.py:24
  173.4 4.5 %convolution_bitcast_fusion = f32[1024,384]{0,1:T(8,128)S(1)} fusion(bf16[2048,384]{1,0:T(8,128)(2,1)} %all-gather.4.cloned.1.call-done, bf16[1024,2048]{1,0:T(8,128)(2,1)} %bitcast.21), kind=kOutput, calls=%fused_computation.2 | convolution fusion | flops 1610612736 | bytes 7340032 | tf_op jit(solution)/shard_map/dot_general | solution.py:22
  177.9 0.0 copy-start
  178.0 1.6 copy.9
  179.6 0.0 reduce-scatter.2.cloned.1.call-update
  179.6 0.0 all-gather.6.cloned.1.call-start
  179.7 0.0 copy-done
  179.7 27.1 %reduce-scatter.2.cloned.1.call-done = f32[1,256,384]{2,1,0:T(8,128)} async-done(((f32[4,256,384]{2,1,0:T(8,128)}), f32[1,256,384]{2,1,0:T(8,128)}) %reduce-scatter.2.cloned.1.call-update) | async-done | bytes 393232 | tf_op jit(solution)/shard_map/reduce_scatter | solution.py:27
  206.8 1.8 fusion
  208.6 0.0 all-gather.6.cloned.1.call-update
  208.6 61.6 %all-gather.6.cloned.1.call-done = f32[1,2048,384]{2,1,0:T(8,128)} async-done(((f32[1,256,384]{2,1,0:T(8,128)}), f32[1,2048,384]{2,1,0:T(8,128)}) %all-gather.6.cloned.1.call-update) | async-done | bytes 3145744 | tf_op jit(solution)/shard_map/all_gather | solution.py:34
  270.3 4.4 %gather_fusion = f32[512,384]{1,0:T(8,128)} fusion(f32[2048,384]{1,0:T(8,128)} %bitcast.16, s32[1024]{0:T(1024)S(1)} %pad_clamp_fusion), kind=kCustom, calls=%fused_computation | custom fusion | bytes 1574912 | tf_op jit(solution)/shard_map/gather | solution.py:35
  (2 shorter events, 0.0 us)
Async XLA Ops:
  7.2 166.3 %all-gather.4.cloned.1.call-start = ((), (), s32[]{:S(2)}) async-start(), calls=%async_computation.2 | async-start | bytes 1769472 | tf_op jit(solution)/shard_map/all_gather | solution.py:24
  130.1 76.7 %reduce-scatter.2.cloned.1.call-start = ((), (), s32[]{:S(2)}) async-start(), calls=%async_computation.3 | async-start | bytes 1966080 | tf_op jit(solution)/shard_map/reduce_scatter | solution.py:27
  177.9 1.7 copy-start
  179.6 90.6 %all-gather.6.cloned.1.call-start = ((), (), s32[]{:S(2)}) async-start(), calls=%async_computation.4 | async-start | bytes 3538944 | tf_op jit(solution)/shard_map/all_gather | solution.py:34
Sparse Core Ops, SparseCore 0:
  130.2 43.1 all-gather.3
  179.7 26.9 reduce-scatter.1
  209.8 60.4 all-gather.5
where the time goes:
time: 283 us; the launch traced here: 281 us
  waiting for transfers between devices  132 us (47%)
  blocking collectives  77.9 us (28%)
  other arithmetic  46.6 us (16%)
  between operations  13.8 us (5%)
  local copies, waits for them, and re-layouts  6.24 us (2%)
  matrix products  4.5 us (2%)
    all_to_all x1, blocking collectives, on_device(): lax.all_to_all(spread, 'wide', split_axis=0, concat_axis=0, tiled=True)  77.9 us
    all_gather x1, waiting for transfers between devices, on_device(): lax.all_gather(boundary_potential[0], 'wide', axis=0, tiled=True)  61.6 us
    all_gather x1, waiting for transfers between devices, on_device(): lax.all_gather(trace_round, 'wide', axis=0, tiled=True)  43.3 us
    scatter-add x1, other arithmetic, on_device(): spread = jnp.zeros((wide_count, node_dev, images), jnp.float32).at[dest_s...  39.9 us
    reduce_scatter x1, waiting for transfers between devices, on_device(): lax.psum_scatter(partial_sum.reshape(narrow_count, node_dev, images), 'na...  27.1 us
  transfers between devices with their start and end apart: 3, of which 3 were waited for; matrix products, arithmetic and copies ran while one was open for 0% of the time, Pallas kernels for 0%

commit v1 on v0

v1 whole, which is shorter than its diff:
```python
import jax
import jax.numpy as jnp
from jax import lax
from jax.experimental import pallas as pl
from jax.experimental.pallas import tpu as pltpu
from jax.sharding import PartitionSpec as P

TRACE_SCALE = 2.0**13
RESULT_SCALE = 2.0
VMEM = 56 * 2**20
GROUP = 8


def exchange(block, axis, offset):
    count = lax.axis_size(axis)
    return lax.ppermute(block, axis, [(i, i ^ offset) for i in range(count)])


def gather_blocks(block):
    count = lax.axis_size("wide")
    held = {0: block}
    for offset in (2, 4, 6):
        if offset < count:
            held[offset] = exchange(block, "wide", offset)
    step = 1
    while step < count:
        if step not in held:
            for offset in sorted(held):
                held[offset ^ step] = exchange(held[offset], "wide", step)
        step *= 2
    return held


def halves(values):
    high = lax.reduce_precision(values, 8, 7)
    return jnp.concatenate([high, values - high], axis=-1).astype(jnp.bfloat16)


def scatter_tile(ids_ref, blocks, first_node, node_dev):
    slots = blocks[0].shape[0]
    node = first_node + lax.broadcasted_iota(jnp.int32, (node_dev, slots), 0)
    total = None
    for row, block in enumerate(blocks):
        pick = jnp.where(ids_ref[row : row + 1, :] == node, 1.0, 0.0).astype(jnp.bfloat16)
        term = jnp.dot(pick, block[...], preferred_element_type=jnp.float32)
        total = term if total is None else total + term
    images = total.shape[1] // 2
    return total[:, :images] + total[:, images:]


def scatter(ids, blocks, before, nodes, node_dev):
    slots, images = blocks[0].shape[0], blocks[0].shape[1] // 2

    def body(*refs):
        ids_ref, rest = refs[0], refs[1:]
        out = rest[-1]
        total = scatter_tile(ids_ref, rest[: len(blocks)], pl.program_id(0) * node_dev, node_dev)
        if before is not None:
            total = total + rest[len(blocks)][...]
        out[...] = total

    tile = pl.BlockSpec((node_dev, images), lambda s: (s, 0))
    whole = pl.BlockSpec((slots, 2 * images), lambda s: (0, 0))
    more = [] if before is None else [before]
    return pl.pallas_call(
        body,
        grid=(nodes // node_dev,),
        in_specs=[pl.BlockSpec(ids.shape, lambda s: (0, 0))] + [whole] * len(blocks) + [tile] * len(more),
        out_specs=tile,
        out_shape=jax.ShapeDtypeStruct((nodes, images), jnp.float32),
        compiler_params=pltpu.CompilerParams(vmem_limit_bytes=VMEM),
        name="scatter_traces",
    )(ids, *blocks, *more)


def scatter_and_layer(place, ids, blocks, before, matrix, nodes, node_dev):
    slots, images = blocks[0].shape[0], blocks[0].shape[1] // 2
    rows = matrix.shape[0]

    def body(place_ref, ids_ref, *rest):
        before_ref, matrix_ref, layer_ref, own_ref = rest[len(blocks) :]
        step = pl.program_id(0)
        total = scatter_tile(ids_ref, rest[: len(blocks)], step * node_dev, node_dev)
        total = (total + before_ref[...]) * (1.0 / TRACE_SCALE)

        @pl.when(step == place_ref[0])
        def _():
            own_ref[...] = total

        term = jnp.dot(matrix_ref[...], total.astype(jnp.bfloat16), preferred_element_type=jnp.float32)

        @pl.when(step == 0)
        def _():
            layer_ref[...] = term

        @pl.when(step != 0)
        def _():
            layer_ref[...] += term

    whole = pl.BlockSpec((slots, 2 * images), lambda s, p: (0, 0))
    return pl.pallas_call(
        body,
        grid_spec=pltpu.PrefetchScalarGridSpec(
            num_scalar_prefetch=1,
            grid=(nodes // node_dev,),
            in_specs=[pl.BlockSpec(ids.shape, lambda s, p: (0, 0))]
            + [whole] * len(blocks)
            + [
                pl.BlockSpec((node_dev, images), lambda s, p: (s, 0)),
                pl.BlockSpec((rows, node_dev), lambda s, p: (0, s)),
            ],
            out_specs=[
                pl.BlockSpec((rows, images), lambda s, p: (0, 0)),
                pl.BlockSpec((node_dev, images), lambda s, p: (0, 0)),
            ],
        ),
        out_shape=[
            jax.ShapeDtypeStruct((rows, images), jnp.float32),
            jax.ShapeDtypeStruct((node_dev, images), jnp.float32),
        ],
        compiler_params=pltpu.CompilerParams(vmem_limit_bytes=VMEM),
        name="scatter_and_layer",
    )(place, ids, *blocks, before, matrix)


def read_back(place, ids, table, count, node_dev):
    slots, images = ids.shape[0], table.shape[1] // 2

    def body(place_ref, ids_ref, table_ref, out_ref):
        total = jnp.zeros((slots, 2 * images), jnp.float32)
        lane = lax.broadcasted_iota(jnp.int32, (slots, node_dev), 1)
        for k in range(count):
            node = (place_ref[0] ^ k) * node_dev + lane
            pick = jnp.where(ids_ref[...] == node, 1.0, 0.0).astype(jnp.bfloat16)
            total += jnp.dot(
                pick, table_ref[k * node_dev : (k + 1) * node_dev, :], preferred_element_type=jnp.float32
            )
        out_ref[...] = (total[:, :images] + total[:, images:]) * (1.0 / RESULT_SCALE)

    return pl.pallas_call(
        body,
        in_specs=[
            pl.BlockSpec(memory_space=pltpu.SMEM),
            pl.BlockSpec(memory_space=pltpu.VMEM),
            pl.BlockSpec(memory_space=pltpu.VMEM),
        ],
        out_shape=jax.ShapeDtypeStruct((slots, images), jnp.float32),
        compiler_params=pltpu.CompilerParams(vmem_limit_bytes=VMEM),
        name="read_back",
    )(place, ids, table)


def on_device(trace_parts, node_slab, node_local, solid_fraction, influence):
    node_dev = solid_fraction.shape[1]
    images = trace_parts.shape[1]
    wide_count = lax.axis_size("wide")
    narrow_count = lax.axis_size("narrow")
    nodes = wide_count * node_dev
    me = lax.axis_index("wide")
    place = me.astype(jnp.int32).reshape(1)

    ids = node_slab[:, 0] * node_dev + node_local
    ids_all = lax.all_gather(ids, "wide", axis=0, tiled=False)
    order = sorted(range(wide_count), key=lambda k: (k & 1) + 2 * (k >> 2) if wide_count == 8 else k)
    ids_order = ids_all[me ^ jnp.array(order, jnp.int32)]

    sent = (trace_parts * TRACE_SCALE).astype(jnp.float16)
    held = gather_blocks(sent)
    blocks = [halves(held[k].astype(jnp.float32)) for k in order]

    last = min(GROUP, wide_count) // 2
    before = None
    done = 0
    while done < wide_count - last:
        size = min(GROUP, wide_count - last - done)
        before = scatter(ids_order[done : done + size], blocks[done : done + size], before, nodes, node_dev)
        done += size
    matrix = influence.reshape(narrow_count * node_dev, nodes)
    partial, own_trace = scatter_and_layer(
        place, ids_order[done:], blocks[done:], before, matrix, nodes, node_dev
    )

    parts = partial.reshape(narrow_count, node_dev, images)
    column = lax.axis_index("narrow")
    layer = lax.dynamic_index_in_dim(parts, column, 0, keepdims=False)
    for k in range(1, narrow_count):
        share = lax.dynamic_index_in_dim(parts, column ^ k, 0, keepdims=False)
        share = (share * RESULT_SCALE).astype(jnp.float16)
        layer = layer + exchange(share, "narrow", k).astype(jnp.float32) * (1.0 / RESULT_SCALE)
    potential = layer + (solid_fraction[0, :, None] - 1.0) * own_trace

    spread = gather_blocks((potential * RESULT_SCALE).astype(jnp.float16))
    table = halves(jnp.concatenate([spread[k] for k in range(wide_count)], axis=0).astype(jnp.float32))
    dirichlet = read_back(place, ids.reshape(-1, 1), table, wide_count, node_dev)
    return (potential[None], dirichlet)


def solution(mesh):
    placed = (
        P(("wide", "narrow"), None),
        P(("wide", "narrow"), None),
        P(("wide", "narrow")),
        P("narrow", "wide"),
        P(None, "wide", "narrow", None),
    )
    return jax.shard_map(
        on_device,
        mesh=mesh,
        in_specs=placed,
        out_specs=(P("narrow", "wide", None), P(("wide", "narrow"), None)),
        check_vma=False,
    )
```

time: 283 us -> 166 us (0.59)
  waiting for transfers between devices: 132 us -> 41.3 us
  Pallas kernels: 0 us -> 35.7 us
  other arithmetic: 46.6 us -> 13.8 us
  blocking collectives: 77.9 us -> 52.3 us
  starting transfers between devices: 0.12 us -> 19.7 us
  between operations: 13.8 us -> 0.86 us
  matrix products: 4.5 us -> 0 us
  local copies, waits for them, and re-layouts: 6.24 us -> 2.38 us
    all_gather x2 -> x0, waiting for transfers between devices: 105 us -> none  [the longest x1 61.6 us: on_device(): lax.all_gather(boundary_potential[0], 'wide', axis=0, tiled=True)]
    all_to_all x1 -> x0, blocking collectives: 77.9 us -> none  [on_device(): lax.all_to_all(spread, 'wide', split_axis=0, concat_axis=0, tiled=True)]
    all_gather x0 -> x1, blocking collectives: none -> 52.3 us  [on_device(): ids_all = lax.all_gather(ids, 'wide', axis=0, tiled=False)]
    ppermute x0 -> x17, waiting for transfers between devices: none -> 41.3 us  [exchange(): return lax.ppermute(block, axis, [(i, i ^ offset) for i in range(count)])]
    scatter-add x1 -> x0, other arithmetic: 39.9 us -> none  [on_device(): spread = jnp.zeros((wide_count, node_dev, images), jnp.float32).at[dest_s...]
    pallas_call x0 -> x3, Pallas kernels: none -> 35.7 us  [the longest x1 20.3 us: scatter_and_layer(): pl.pallas_call(body, grid_spec=pltpu.PrefetchScalarGridSpec(num_scalar_pr...]
    reduce_scatter x1 -> x0, waiting for transfers between devices: 27.1 us -> none  [on_device(): lax.psum_scatter(partial_sum.reshape(narrow_count, node_dev, images), 'na...]
    ppermute x0 -> x17, starting transfers between devices: none -> 19.7 us  [exchange(): return lax.ppermute(block, axis, [(i, i ^ offset) for i in range(count)])]
  transfers between devices with their start and end apart: 3 -> 17, of which waited for: 3 -> 9; matrix products, arithmetic and copies ran while one was open for 0% -> 5% of each run, Pallas kernels for 0% -> 0%
where the time goes in v1:
time: 166 us
  blocking collectives  52.3 us (32%)
  waiting for transfers between devices  41.3 us (25%)
  Pallas kernels  35.7 us (22%)
  starting transfers between devices  19.7 us (12%)
  other arithmetic  13.8 us (8%)
  local copies, waits for them, and re-layouts  2.38 us (1%)
    all_gather x1, blocking collectives, on_device(): ids_all = lax.all_gather(ids, 'wide', axis=0, tiled=False)  52.3 us
    ppermute x17, waiting for transfers between devices, exchange(): return lax.ppermute(block, axis, [(i, i ^ offset) for i in range(count)])  41.3 us
    pallas_call x1, Pallas kernels, scatter_and_layer(): pl.pallas_call(body, grid_spec=pltpu.PrefetchScalarGridSpec(num_scalar_pr...  20.3 us
    ppermute x17, starting transfers between devices, exchange(): return lax.ppermute(block, axis, [(i, i ^ offset) for i in range(count)])  19.7 us
    pallas_call x1, Pallas kernels, scatter(): pl.pallas_call(body, grid=(nodes // node_dev,), in_specs=[pl.BlockSpec(id...  10.7 us
    concatenate x6, other arithmetic, halves(): return jnp.concatenate([high, values - high], axis=-1).astype(jnp.bfloat16)  7.77 us
    pallas_call x1, Pallas kernels, read_back(): pl.pallas_call(body, in_specs=[pl.BlockSpec(memory_space=pltpu.SMEM), pl....  4.71 us
  transfers between devices with their start and end apart: 17, of which 9 were waited for; matrix products, arithmetic and copies ran while one was open for 5% of the time, Pallas kernels for 0%

profile of v1, /device:TPU:0, one launch (start us, length us, event | category | flops | bytes accessed | tf_op | source)
XLA Modules:
  0.0 166.0 jit_solution(291649819717512821)
XLA Ops:
  1.9 3.1 %collective-permute-start.4 = (f16[512,384]{1,0:T(8,128)(2,1)S(1)}, f16[512,384]{1,0:T(8,128)(2,1)S(1)}, u32[]{:S(2)}, u32[]{:S(2)}) collective-permute-start(f16[512,384]{1,0:T(8,128)(2,1)S(1)} %get-tuple-element.10), channel_id=1, source_target_pairs={{0,8},{4,12},{8,0},{12,4},{16,24},{20,28},{24,16},{28,20},{1,9},{5... | collective-permute-start | bytes 1179656 | tf_op jit(solution)/shard_map/ppermute | solution.py:16
  5.0 1.5 collective-permute-start.5
  6.5 2.5 %collective-permute-start.1 = (f16[512,384]{1,0:T(8,128)(2,1)S(1)}, f16[512,384]{1,0:T(8,128)(2,1)S(1)}, u32[]{:S(2)}, u32[]{:S(2)}) collective-permute-start(f16[512,384]{1,0:T(8,128)(2,1)S(1)} %get-tuple-element.10), channel_id=1, source_target_pairs={{0,24},{4,28},{8,16},{12,20},{16,8},{20,12},{24,0},{28,4},{1,25},{... | collective-permute-start | bytes 1179656 | tf_op jit(solution)/shard_map/ppermute | solution.py:16
  9.3 52.3 %all-gather.1 = s32[8,1,512]{2,1,0:T(1,128)S(1)} all-gather(s32[1,1,512]{2,1,0:T(1,128)S(1)} %bitcast.31), channel_id=2, replica_groups=mesh['wide'=8,'narrow'=4] {'wide'}, dimensions={0}, use_global_device_ids=true | all-gather | bytes 18432 | tf_op jit(solution)/shard_map/all_gather | solution.py:163
  64.0 2.1 %collective-permute-start.3 = (f16[512,384]{1,0:T(8,128)(2,1)S(1)}, f16[512,384]{1,0:T(8,128)(2,1)S(1)}, u32[]{:S(2)}, u32[]{:S(2)}) collective-permute-start(f16[512,384]{1,0:T(8,128)(2,1)S(1)} %collective-permute-done.1), channel_id=1, source_target_pairs={{0,4},{4,0},{8,12},{12,8},{16,20},{20,16},{24,28},{28,24},{1,5},{5... | collective-permute-start | bytes 1179656 | tf_op jit(solution)/shard_map/ppermute | solution.py:16
  69.0 6.8 %collective-permute-done.6 = f16[512,384]{1,0:T(8,128)(2,1)S(1)} collective-permute-done((f16[512,384]{1,0:T(8,128)(2,1)S(1)}, f16[512,384]{1,0:T(8,128)(2,1)S(1)}, u32[]{:S(2)}, u32[]{:S(2)}) %collective-permute-start.6) | collective-permute-done | bytes 393248 | tf_op jit(solution)/shard_map/ppermute | solution.py:16
  76.9 3.9 %collective-permute-done.3 = f16[512,384]{1,0:T(8,128)(2,1)S(1)} collective-permute-done((f16[512,384]{1,0:T(8,128)(2,1)S(1)}, f16[512,384]{1,0:T(8,128)(2,1)S(1)}, u32[]{:S(2)}, u32[]{:S(2)}) %collective-permute-start.3) | collective-permute-done | bytes 393248 | tf_op jit(solution)/shard_map/ppermute | solution.py:16
  81.0 4.1 %collective-permute-done.2 = f16[512,384]{1,0:T(8,128)(2,1)S(1)} collective-permute-done((f16[512,384]{1,0:T(8,128)(2,1)S(1)}, f16[512,384]{1,0:T(8,128)(2,1)S(1)}, u32[]{:S(2)}, u32[]{:S(2)}) %collective-permute-start.2) | collective-permute-done | bytes 393248 | tf_op jit(solution)/shard_map/ppermute | solution.py:16
  86.5 10.7 %scatter_traces.1.rest_4_ = f32[2048,384]{1,0:T(8,128)} custom-call(s32[4,512]{1,0:T(4,128)} %get-tuple-element.30.refs_0_, bf16[512,768]{1,0:T(8,128)(2,1)} %pad_maximum_fusion.5.refs_1_, bf16[512,768]{1,0:T(8,128)(2,1)} %get-tuple-element.32.refs_2_, bf16[512,768]{1,0:T(8,128)(2,1)} %get-tuple-element.33.refs_3_, bf16[512,768]{1,0:T(8,128)(2,1)} %pad_maximum_fusion.8.refs_4_), custom_call_target="tpu_custom_call" | custom-call | tf_op jit(solution)/shard_map/scatter_traces/pallas_call | solution.py:65
  97.1 20.3 %scatter_and_layer.1 = (f32[1024,384]{1,0:T(8,128)}, f32[256,384]{1,0:T(8,128)}) custom-call(s32[1]{0:T(128)} %bitcast.place_ref, s32[4,512]{1,0:T(4,128)} %get-tuple-element.31.ids_ref, bf16[512,768]{1,0:T(8,128)(2,1)} %get-tuple-element.34.rest_0_, bf16[512,768]{1,0:T(8,128)(2,1)} %get-tuple-element.35.rest_1_, ...), custom_call_target="tpu_custom_call" | custom-call | tf_op jit(solution)/shard_map/scatter_and_layer/pallas_call | solution.py:101
  117.4 1.4 fusion.12
  118.9 1.6 collective-permute-start.8
  120.8 5.9 %collective-permute-done.8 = f16[256,384]{1,0:T(8,128)(2,1)S(1)} collective-permute-done((f16[256,384]{1,0:T(8,128)(2,1)S(1)}, f16[256,384]{1,0:T(8,128)(2,1)S(1)}, u32[]{:S(2)}, u32[]{:S(2)}) %collective-permute-start.8) | collective-permute-done | bytes 196640 | tf_op jit(solution)/shard_map/ppermute | solution.py:16
  126.7 3.3 %collective-permute-done.9 = f16[256,384]{1,0:T(8,128)(2,1)S(1)} collective-permute-done((f16[256,384]{1,0:T(8,128)(2,1)S(1)}, f16[256,384]{1,0:T(8,128)(2,1)S(1)}, u32[]{:S(2)}, u32[]{:S(2)}) %collective-permute-start.9) | collective-permute-done | bytes 196640 | tf_op jit(solution)/shard_map/ppermute | solution.py:16
  130.0 1.9 %constant_dynamic-update-slice_fusion.7 = (f16[2048,384]{1,0:T(8,128)(2,1)S(1)}, f16[256,384]{1,0:T(8,128)(2,1)S(1)}, f32[256,384]{1,0:T(8,128)}) fusion(f32[256,384]{1,0:T(8,128)S(1)} %copy-done, f32[256]{0:T(256)S(1)} %bitcast.34, f16[256,384]{1,0:T(8,128)(2,1)S(1)} %collective-permute-done.9, f16[256,384]{1,0:T(8,128)(2,1)S(1)} %collective-permute-done.8, ...), kind=kLoop, calls=%fused_computation.56 | loop fusion | flops 1277951 | bytes 2163716
  132.2 4.1 %collective-permute-start.15 = (f16[256,384]{1,0:T(8,128)(2,1)S(1)}, f16[256,384]{1,0:T(8,128)(2,1)S(1)}, u32[]{:S(2)}, u32[]{:S(2)}) collective-permute-start(f16[256,384]{1,0:T(8,128)(2,1)S(1)} %get-tuple-element.7), channel_id=1, source_target_pairs={{0,24},{4,28},{8,16},{12,20},{16,8},{20,12},{24,0},{28,4},{1,25},{... | collective-permute-start | bytes 589832 | tf_op jit(solution)/shard_map/ppermute | solution.py:16
  137.4 2.9 %collective-permute-done.11 = f16[256,384]{1,0:T(8,128)(2,1)S(1)} collective-permute-done((f16[256,384]{1,0:T(8,128)(2,1)S(1)}, f16[256,384]{1,0:T(8,128)(2,1)S(1)}, u32[]{:S(2)}, u32[]{:S(2)}) %collective-permute-start.11) | collective-permute-done | bytes 196640 | tf_op jit(solution)/shard_map/ppermute | solution.py:16
  140.4 1.7 %collective-permute-start.12 = (f16[256,384]{1,0:T(8,128)(2,1)S(1)}, f16[256,384]{1,0:T(8,128)(2,1)S(1)}, u32[]{:S(2)}, u32[]{:S(2)}) collective-permute-start(f16[256,384]{1,0:T(8,128)(2,1)S(1)} %collective-permute-done.11), channel_id=1, source_target_pairs={{0,4},{4,0},{8,12},{12,8},{16,20},{20,16},{24,28},{28,24},{1,5},{5... | collective-permute-start | bytes 589832 | tf_op jit(solution)/shard_map/ppermute | solution.py:16
  142.1 6.9 %collective-permute-done.13 = f16[256,384]{1,0:T(8,128)(2,1)S(1)} collective-permute-done((f16[256,384]{1,0:T(8,128)(2,1)S(1)}, f16[256,384]{1,0:T(8,128)(2,1)S(1)}, u32[]{:S(2)}, u32[]{:S(2)}) %collective-permute-start.13) | collective-permute-done | bytes 196640 | tf_op jit(solution)/shard_map/ppermute | solution.py:16
  149.3 1.7 %collective-permute-start.16 = (f16[256,384]{1,0:T(8,128)(2,1)S(1)}, f16[256,384]{1,0:T(8,128)(2,1)S(1)}, u32[]{:S(2)}, u32[]{:S(2)}) collective-permute-start(f16[256,384]{1,0:T(8,128)(2,1)S(1)} %collective-permute-done.15), channel_id=1, source_target_pairs={{0,4},{4,0},{8,12},{12,8},{16,20},{20,16},{24,28},{28,24},{1,5},{5... | collective-permute-start | bytes 589832 | tf_op jit(solution)/shard_map/ppermute | solution.py:16
  151.3 5.5 %collective-permute-done.14 = f16[256,384]{1,0:T(8,128)(2,1)S(1)} collective-permute-done((f16[256,384]{1,0:T(8,128)(2,1)S(1)}, f16[256,384]{1,0:T(8,128)(2,1)S(1)}, u32[]{:S(2)}, u32[]{:S(2)}) %collective-permute-start.14) | collective-permute-done | bytes 196640 | tf_op jit(solution)/shard_map/ppermute | solution.py:16
  156.9 2.0 %collective-permute-done.16 = f16[256,384]{1,0:T(8,128)(2,1)S(1)} collective-permute-done((f16[256,384]{1,0:T(8,128)(2,1)S(1)}, f16[256,384]{1,0:T(8,128)(2,1)S(1)}, u32[]{:S(2)}, u32[]{:S(2)}) %collective-permute-start.16) | collective-permute-done | bytes 196640 | tf_op jit(solution)/shard_map/ppermute | solution.py:16
  159.4 1.9 %pad_maximum_fusion.table_ref = bf16[2048,768]{1,0:T(8,128)(2,1)} fusion(bf16[2048,384]{1,0:T(8,128)(2,1)S(1)} %get-tuple-element.12, bf16[2048,384]{1,0:T(8,128)(2,1)S(1)} %get-tuple-element.11), kind=kLoop, calls=%fused_computation.4 | loop fusion | flops 6291456 | bytes 6291456 | tf_op jit(solution)/shard_map/concatenate | solution.py:36
  161.3 4.7 %read_back.1 = f32[512,384]{1,0:T(8,128)} custom-call(s32[1]{0:T(128)} %bitcast.place_ref, s32[512,1]{1,0:T(8,128)} %copy.9.ids_ref, bf16[2048,768]{1,0:T(8,128)(2,1)} %pad_maximum_fusion.table_ref), custom_call_target="tpu_custom_call" | custom-call | tf_op jit(solution)/shard_map/read_back/pallas_call | solution.py:140
  (58 shorter events, 12.3 us)
Async XLA Ops:
  0.6 8.6 %copy-start.4 = (s32[8]{0:T(128)S(1)}, s32[8]{0:T(128)}, u32[]{:S(2)}) copy-start(s32[8]{0:T(128)} %constant.43.clone) | copy-start | bytes 100
  0.6 8.6 %copy-start.2 = (s32[512,1]{0,1:T(1,128)S(1)}, s32[512,1]{0,1:T(1,128)}, u32[]{:S(2)}) copy-start(s32[512,1]{0,1:T(1,128)} %param.7) | copy-start | bytes 6148
  0.7 8.6 %copy-start.1 = (s32[512]{0:T(512)S(1)}, s32[512]{0:T(512)}, u32[]{:S(2)}) copy-start(s32[512]{0:T(512)} %param.8) | copy-start | bytes 6148
  1.9 61.9 %collective-permute-start.4 = (f16[512,384]{1,0:T(8,128)(2,1)S(1)}, f16[512,384]{1,0:T(8,128)(2,1)S(1)}, u32[]{:S(2)}, u32[]{:S(2)}) collective-permute-start(f16[512,384]{1,0:T(8,128)(2,1)S(1)} %get-tuple-element.10), channel_id=1, source_target_pairs={{0,8},{4,12},{8,0},{12,4},{16,24},{20,28},{24,16},{28,20},{1,9},{5... | collective-permute-start | bytes 1179656 | tf_op jit(solution)/shard_map/ppermute | solution.py:16
  5.0 58.9 %collective-permute-start.5 = (f16[512,384]{1,0:T(8,128)(2,1)S(1)}, f16[512,384]{1,0:T(8,128)(2,1)S(1)}, u32[]{:S(2)}, u32[]{:S(2)}) collective-permute-start(f16[512,384]{1,0:T(8,128)(2,1)S(1)} %get-tuple-element.10), channel_id=1, source_target_pairs={{0,4},{4,0},{8,12},{12,8},{16,20},{20,16},{24,28},{28,24},{1,5},{5... | collective-permute-start | bytes 1179656 | tf_op jit(solution)/shard_map/ppermute | solution.py:16
  6.5 57.5 %collective-permute-start.1 = (f16[512,384]{1,0:T(8,128)(2,1)S(1)}, f16[512,384]{1,0:T(8,128)(2,1)S(1)}, u32[]{:S(2)}, u32[]{:S(2)}) collective-permute-start(f16[512,384]{1,0:T(8,128)(2,1)S(1)} %get-tuple-element.10), channel_id=1, source_target_pairs={{0,24},{4,28},{8,16},{12,20},{16,8},{20,12},{24,0},{28,4},{1,25},{... | collective-permute-start | bytes 1179656 | tf_op jit(solution)/shard_map/ppermute | solution.py:16
  9.0 58.6 %collective-permute-start = (f16[512,384]{1,0:T(8,128)(2,1)S(1)}, f16[512,384]{1,0:T(8,128)(2,1)S(1)}, u32[]{:S(2)}, u32[]{:S(2)}) collective-permute-start(f16[512,384]{1,0:T(8,128)(2,1)S(1)} %get-tuple-element.10), channel_id=1, source_target_pairs={{0,16},{4,20},{8,24},{12,28},{16,0},{20,4},{24,8},{28,12},{1,17},{... | collective-permute-start | bytes 1179656 | tf_op jit(solution)/shard_map/ppermute | solution.py:16
  63.8 12.1 %collective-permute-start.6 = (f16[512,384]{1,0:T(8,128)(2,1)S(1)}, f16[512,384]{1,0:T(8,128)(2,1)S(1)}, u32[]{:S(2)}, u32[]{:S(2)}) collective-permute-start(f16[512,384]{1,0:T(8,128)(2,1)S(1)} %collective-permute-done.4), channel_id=1, source_target_pairs={{0,4},{4,0},{8,12},{12,8},{16,20},{20,16},{24,28},{28,24},{1,5},{5... | collective-permute-start | bytes 1179656 | tf_op jit(solution)/shard_map/ppermute | solution.py:16
  64.0 16.8 %collective-permute-start.3 = (f16[512,384]{1,0:T(8,128)(2,1)S(1)}, f16[512,384]{1,0:T(8,128)(2,1)S(1)}, u32[]{:S(2)}, u32[]{:S(2)}) collective-permute-start(f16[512,384]{1,0:T(8,128)(2,1)S(1)} %collective-permute-done.1), channel_id=1, source_target_pairs={{0,4},{4,0},{8,12},{12,8},{16,20},{20,16},{24,28},{28,24},{1,5},{5... | collective-permute-start | bytes 1179656 | tf_op jit(solution)/shard_map/ppermute | solution.py:16
  69.0 16.0 %collective-permute-start.2 = (f16[512,384]{1,0:T(8,128)(2,1)S(1)}, f16[512,384]{1,0:T(8,128)(2,1)S(1)}, u32[]{:S(2)}, u32[]{:S(2)}) collective-permute-start(f16[512,384]{1,0:T(8,128)(2,1)S(1)} %collective-permute-done), channel_id=1, source_target_pairs={{0,4},{4,0},{8,12},{12,8},{16,20},{20,16},{24,28},{28,24},{1,5},{5... | collective-permute-start | bytes 1179656 | tf_op jit(solution)/shard_map/ppermute | solution.py:16
  117.4 3.4 %copy-start.3 = (f32[1,256]{1,0:T(1,128)S(1)}, f32[1,256]{1,0:T(1,128)}, u32[]{:S(2)}) copy-start(f32[1,256]{1,0:T(1,128)} %param.9) | copy-start | bytes 3076
  117.4 12.6 %copy-start = (f32[256,384]{1,0:T(8,128)S(1)}, f32[256,384]{1,0:T(8,128)}, u32[]{:S(2)}) copy-start(f32[256,384]{1,0:T(8,128)} %get-tuple-element.5) | copy-start | bytes 1179652
  118.9 1.9 %collective-permute-start.7 = (f16[256,384]{1,0:T(8,128)(2,1)S(1)}, f16[256,384]{1,0:T(8,128)(2,1)S(1)}, u32[]{:S(2)}, u32[]{:S(2)}) collective-permute-start(f16[256,384]{1,0:T(8,128)(2,1)S(1)} %get-tuple-element.13), channel_id=1, source_target_pairs={{0,1},{1,0},{2,3},{3,2},{4,5},{5,4},{6,7},{7,6},{8,9},{9,8},{10,11... | collective-permute-start | bytes 589832 | tf_op jit(solution)/shard_map/ppermute | solution.py:16
  118.9 7.8 %collective-permute-start.8 = (f16[256,384]{1,0:T(8,128)(2,1)S(1)}, f16[256,384]{1,0:T(8,128)(2,1)S(1)}, u32[]{:S(2)}, u32[]{:S(2)}) collective-permute-start(f16[256,384]{1,0:T(8,128)(2,1)S(1)} %get-tuple-element.15), channel_id=1, source_target_pairs={{0,2},{1,3},{2,0},{3,1},{4,6},{5,7},{6,4},{7,5},{8,10},{9,11},{10,... | collective-permute-start | bytes 589832 | tf_op jit(solution)/shard_map/ppermute | solution.py:16
  120.5 9.5 %collective-permute-start.9 = (f16[256,384]{1,0:T(8,128)(2,1)S(1)}, f16[256,384]{1,0:T(8,128)(2,1)S(1)}, u32[]{:S(2)}, u32[]{:S(2)}) collective-permute-start(f16[256,384]{1,0:T(8,128)(2,1)S(1)} %get-tuple-element.14), channel_id=1, source_target_pairs={{0,3},{1,2},{2,1},{3,0},{4,7},{5,6},{6,5},{7,4},{8,11},{9,10},{10,... | collective-permute-start | bytes 589832 | tf_op jit(solution)/shard_map/ppermute | solution.py:16
  131.9 8.4 %collective-permute-start.11 = (f16[256,384]{1,0:T(8,128)(2,1)S(1)}, f16[256,384]{1,0:T(8,128)(2,1)S(1)}, u32[]{:S(2)}, u32[]{:S(2)}) collective-permute-start(f16[256,384]{1,0:T(8,128)(2,1)S(1)} %get-tuple-element.7), channel_id=1, source_target_pairs={{0,8},{4,12},{8,0},{12,4},{16,24},{20,28},{24,16},{28,20},{1,9},{5... | collective-permute-start | bytes 589832 | tf_op jit(solution)/shard_map/ppermute | solution.py:16
  131.9 17.1 %collective-permute-start.13 = (f16[256,384]{1,0:T(8,128)(2,1)S(1)}, f16[256,384]{1,0:T(8,128)(2,1)S(1)}, u32[]{:S(2)}, u32[]{:S(2)}) collective-permute-start(f16[256,384]{1,0:T(8,128)(2,1)S(1)} %get-tuple-element.7), channel_id=1, source_target_pairs={{0,16},{4,20},{8,24},{12,28},{16,0},{20,4},{24,8},{28,12},{1,17},{... | collective-permute-start | bytes 589832 | tf_op jit(solution)/shard_map/ppermute | solution.py:16
  132.2 17.1 %collective-permute-start.15 = (f16[256,384]{1,0:T(8,128)(2,1)S(1)}, f16[256,384]{1,0:T(8,128)(2,1)S(1)}, u32[]{:S(2)}, u32[]{:S(2)}) collective-permute-start(f16[256,384]{1,0:T(8,128)(2,1)S(1)} %get-tuple-element.7), channel_id=1, source_target_pairs={{0,24},{4,28},{8,16},{12,20},{16,8},{20,12},{24,0},{28,4},{1,25},{... | collective-permute-start | bytes 589832 | tf_op jit(solution)/shard_map/ppermute | solution.py:16
  136.3 14.8 %collective-permute-start.10 = (f16[256,384]{1,0:T(8,128)(2,1)S(1)}, f16[256,384]{1,0:T(8,128)(2,1)S(1)}, u32[]{:S(2)}, u32[]{:S(2)}) collective-permute-start(f16[256,384]{1,0:T(8,128)(2,1)S(1)} %get-tuple-element.7), channel_id=1, source_target_pairs={{0,4},{4,0},{8,12},{12,8},{16,20},{20,16},{24,28},{28,24},{1,5},{5... | collective-permute-start | bytes 589832 | tf_op jit(solution)/shard_map/ppermute | solution.py:16
  140.4 10.8 %collective-permute-start.12 = (f16[256,384]{1,0:T(8,128)(2,1)S(1)}, f16[256,384]{1,0:T(8,128)(2,1)S(1)}, u32[]{:S(2)}, u32[]{:S(2)}) collective-permute-start(f16[256,384]{1,0:T(8,128)(2,1)S(1)} %collective-permute-done.11), channel_id=1, source_target_pairs={{0,4},{4,0},{8,12},{12,8},{16,20},{20,16},{24,28},{28,24},{1,5},{5... | collective-permute-start | bytes 589832 | tf_op jit(solution)/shard_map/ppermute | solution.py:16
  149.0 7.7 %collective-permute-start.14 = (f16[256,384]{1,0:T(8,128)(2,1)S(1)}, f16[256,384]{1,0:T(8,128)(2,1)S(1)}, u32[]{:S(2)}, u32[]{:S(2)}) collective-permute-start(f16[256,384]{1,0:T(8,128)(2,1)S(1)} %collective-permute-done.13), channel_id=1, source_target_pairs={{0,4},{4,0},{8,12},{12,8},{16,20},{20,16},{24,28},{28,24},{1,5},{5... | collective-permute-start | bytes 589832 | tf_op jit(solution)/shard_map/ppermute | solution.py:16
  149.3 9.6 %collective-permute-start.16 = (f16[256,384]{1,0:T(8,128)(2,1)S(1)}, f16[256,384]{1,0:T(8,128)(2,1)S(1)}, u32[]{:S(2)}, u32[]{:S(2)}) collective-permute-start(f16[256,384]{1,0:T(8,128)(2,1)S(1)} %collective-permute-done.15), channel_id=1, source_target_pairs={{0,4},{4,0},{8,12},{12,8},{16,20},{20,16},{24,28},{28,24},{1,5},{5... | collective-permute-start | bytes 589832 | tf_op jit(solution)/shard_map/ppermute | solution.py:16

commit v2 on v0

v2 whole, which is shorter than its diff:
```python
import jax
import jax.numpy as jnp
from jax import lax
from jax.experimental import pallas as pl
from jax.experimental.pallas import tpu as pltpu
from jax.sharding import PartitionSpec as P

TRACE_SCALE = 2.0**13
RESULT_SCALE = 2.0
MIB = 2**20
ROWS = 16


def exchange(block, axis, offset):
    count = lax.axis_size(axis)
    return lax.ppermute(block, axis, [(i, i ^ offset) for i in range(count)])


def after(value, *others):
    return lax.optimization_barrier((value, *others))[0]


def gather_blocks(block, early, late):
    count = lax.axis_size("wide")
    held = {0: block}
    held[4] = exchange(block, "wide", 4)
    held[2] = exchange(block, "wide", 2)
    held[1] = exchange(block, "wide", 1)
    held[6] = exchange(block, "wide", 6)
    held[3] = exchange(held[2], "wide", 1)
    done = early(held)
    held[4] = after(held[4], done)
    held[5] = exchange(held[4], "wide", 1)
    held[7] = exchange(held[6], "wide", 1)
    done = late(held, done)
    held[5], held[7], done = lax.optimization_barrier((held[5], held[7], done))
    step = 8
    while step < count:
        for offset in sorted(held):
            held[offset ^ step] = exchange(held[offset], "wide", step)
        step *= 2
    return held, done


def with_ids(values, slab, local):
    slots, images = values.shape
    per = -(-slots // images)
    extra = -(-2 * per // ROWS) * ROWS
    total = jnp.pad(values, ((0, extra), (0, 0)))
    for n, part in enumerate((slab, local)):
        for r in range(per):
            piece = part.reshape(1, slots)[:, r * images : (r + 1) * images].astype(values.dtype)
            row = n * per + r
            total = total + jnp.pad(piece, ((slots + row, extra - row - 1), (0, images - piece.shape[1])))
    return total.astype(jnp.float16)


def ids_of(block, slots, node_dev):
    images = block.shape[1]
    per = -(-slots // images)

    def line(first):
        pieces = [
            block[slots + first + r : slots + first + r + 1, : min(images, slots - r * images)] for r in range(per)
        ]
        return pieces[0] if per == 1 else jnp.concatenate(pieces, axis=1)

    return (line(0) * node_dev + line(per)).astype(jnp.int32)


def store_halves(values, out, first):
    rows, images = values.shape
    high = values.astype(jnp.bfloat16)
    out[first : first + rows, :images] = high
    out[first : first + rows, images:] = (values - high.astype(jnp.float32)).astype(jnp.bfloat16)


def scatter_tile(blocks, both, slots, first_node, tile, node_dev):
    @pl.when(first_node == 0)
    def _():
        for k, block in enumerate(blocks):
            store_halves(block[:slots, :], both, k * slots)

    node = first_node + lax.broadcasted_iota(jnp.int32, (tile, slots), 0)
    picks = [
        jnp.where(ids_of(block, slots, node_dev) == node, 1.0, 0.0).astype(jnp.bfloat16) for block in blocks
    ]
    total = jnp.dot(jnp.concatenate(picks, axis=1), both[...], preferred_element_type=jnp.float32)
    images = total.shape[1] // 2
    return total[:, :images] + total[:, images:]


def cost_of(blocks, slots, nodes, extra=0):
    images = blocks[0].shape[1]
    flops = 4 * len(blocks) * slots * nodes * images + extra
    return pl.CostEstimate(flops=flops, bytes_accessed=8 * nodes * images, transcendentals=0)


def scatter(blocks, slots, before, nodes, node_dev):
    images = blocks[0].shape[1]
    tile = 2 * node_dev

    def body(*refs):
        held, out, both = refs[: len(blocks)], refs[-2], refs[-1]
        total = scatter_tile(held, both, slots, pl.program_id(0) * tile, tile, node_dev)
        if before is not None:
            total = total + refs[len(blocks)][...]
        out[...] = total

    part = pl.BlockSpec((tile, images), lambda s: (s, 0))
    more = [] if before is None else [before]
    return pl.pallas_call(
        body,
        grid=(nodes // tile,),
        in_specs=[pl.BlockSpec(block.shape, lambda s: (0, 0)) for block in blocks] + [part] * len(more),
        out_specs=part,
        out_shape=jax.ShapeDtypeStruct((nodes, images), jnp.float32),
        scratch_shapes=[pltpu.VMEM((len(blocks) * slots, 2 * images), jnp.bfloat16)],
        compiler_params=pltpu.CompilerParams(vmem_limit_bytes=(8 + 4 * len(blocks)) * MIB),
        cost_estimate=cost_of(blocks, slots, nodes),
        name="scatter_traces",
    )(*blocks, *more)


def scatter_and_layer(place, blocks, slots, before, matrix, diagonal, nodes, node_dev, narrow_count):
    images = blocks[0].shape[1]
    tile = 2 * node_dev
    steps = nodes // tile

    def body(place_ref, *refs):
        held = refs[: len(blocks)]
        before_ref, matrix_ref, diagonal_ref = refs[len(blocks) : len(blocks) + 3]
        outs = refs[len(blocks) + 3 : -5]
        both, rounded, own, matrix_held, sem = refs[-5:]
        step = pl.program_id(0)
        fetch = pltpu.make_async_copy(matrix_ref, matrix_held, sem)

        @pl.when(step == 0)
        def _():
            fetch.start()

        total = scatter_tile(held, both, slots, step * tile, tile, node_dev)
        total = (total + before_ref[...]) * (1.0 / TRACE_SCALE)
        for half in range(2):
            @pl.when(2 * step + half == place_ref[0])
            def _():
                own[...] = total[half * node_dev : (half + 1) * node_dev, :]

        rounded[pl.ds(pl.multiple_of(step * tile, tile), tile), :] = total.astype(jnp.bfloat16)

        @pl.when(step == steps - 1)
        def _():
            fetch.wait()
            for k in range(narrow_count):
                first = pl.multiple_of((place_ref[1] ^ k) * node_dev, node_dev)
                layer = jnp.dot(
                    matrix_held[pl.ds(first, node_dev), :], rounded[...], preferred_element_type=jnp.float32
                )
                if k == 0:
                    layer = layer + diagonal_ref[...] * own[...]
                outs[k][...] = layer.astype(outs[k].dtype)

    one = pl.BlockSpec((node_dev, images), lambda s, p: (0, 0))
    limit = 12 + 4 * len(blocks) + (2 * matrix.size + 2 * nodes * images) // MIB
    return pl.pallas_call(
        body,
        grid_spec=pltpu.PrefetchScalarGridSpec(
            num_scalar_prefetch=1,
            grid=(steps,),
            in_specs=[pl.BlockSpec(block.shape, lambda s, p: (0, 0)) for block in blocks]
            + [
                pl.BlockSpec((tile, images), lambda s, p: (s, 0)),
                pl.BlockSpec(memory_space=pl.ANY),
                pl.BlockSpec((node_dev, 1), lambda s, p: (0, 0)),
            ],
            out_specs=[one] * narrow_count,
            scratch_shapes=[
                pltpu.VMEM((len(blocks) * slots, 2 * images), jnp.bfloat16),
                pltpu.VMEM((nodes, images), jnp.bfloat16),
                pltpu.VMEM((node_dev, images), jnp.float32),
                pltpu.VMEM(matrix.shape, matrix.dtype),
                pltpu.SemaphoreType.DMA,
            ],
        ),
        out_shape=[jax.ShapeDtypeStruct((node_dev, images), jnp.float32)]
        + [jax.ShapeDtypeStruct((node_dev, images), jnp.bfloat16)] * (narrow_count - 1),
        compiler_params=pltpu.CompilerParams(vmem_limit_bytes=limit * MIB),
        cost_estimate=cost_of(blocks, slots, nodes, 2 * matrix.shape[0] * nodes * images),
        name="scatter_and_layer",
    )(place, *blocks, before, matrix, diagonal)


def read_back(place, ids, blocks, keys, before):
    slots = ids.shape[0]
    node_dev, images = blocks[0].shape

    def body(place_ref, ids_ref, *refs):
        out, both = refs[-2:]
        lane = lax.broadcasted_iota(jnp.int32, (slots, node_dev), 1)
        picks = []
        for row, key in enumerate(keys):
            store_halves(refs[row][...], both, row * node_dev)
            node = (place_ref[0] ^ key) * node_dev + lane
            picks.append(jnp.where(ids_ref[...] == node, 1.0, 0.0).astype(jnp.bfloat16))
        total = jnp.dot(jnp.concatenate(picks, axis=1), both[...], preferred_element_type=jnp.float32)
        total = (total[:, :images] + total[:, images:]) * (1.0 / RESULT_SCALE)
        if before is not None:
            total = total + refs[len(blocks)][...]
        out[...] = total

    more = [] if before is None else [before]
    vmem = pl.BlockSpec(memory_space=pltpu.VMEM)
    return pl.pallas_call(
        body,
        in_specs=[pl.BlockSpec(memory_space=pltpu.SMEM)] + [vmem] * (1 + len(blocks) + len(more)),
        out_shape=jax.ShapeDtypeStruct((slots, images), jnp.float32),
        scratch_shapes=[pltpu.VMEM((len(blocks) * node_dev, 2 * images), jnp.bfloat16)],
        compiler_params=pltpu.CompilerParams(vmem_limit_bytes=(10 + 2 * len(blocks)) * MIB),
        cost_estimate=cost_of(blocks, node_dev, slots),
        name="read_back",
    )(place, ids, *blocks, *more)


def on_device(trace_parts, node_slab, node_local, solid_fraction, influence):
    node_dev = solid_fraction.shape[1]
    slots, images = trace_parts.shape
    wide_count = lax.axis_size("wide")
    narrow_count = lax.axis_size("narrow")
    nodes = wide_count * node_dev
    place = jnp.stack([lax.axis_index("wide"), lax.axis_index("narrow")]).astype(jnp.int32)
    ids = (node_slab[:, 0] * node_dev + node_local).reshape(-1, 1)
    diagonal = (solid_fraction - 1.0).reshape(-1, 1)
    first, second, last = (0, 1, 2), (3, 4, 6), (5, 7)
    others = [tuple(range(k, k + 4)) for k in range(8, wide_count, 4)]

    def add_up(held, keys, before):
        return scatter([held[k].astype(jnp.float32) for k in keys], slots, before, nodes, node_dev)

    sent = with_ids(trace_parts * TRACE_SCALE, node_slab, node_local)
    held, sums = gather_blocks(
        sent, lambda held: add_up(held, first, None), lambda held, sums: add_up(held, second, sums)
    )
    for keys in others:
        sums = add_up(held, keys, sums)
    matrix = influence.reshape(narrow_count * node_dev, nodes)
    potential, *shares = scatter_and_layer(
        place, [held[k].astype(jnp.float32) for k in last], slots, sums, matrix, diagonal, nodes, node_dev, narrow_count
    )
    for k, share in enumerate(shares, 1):
        potential = potential + exchange(share, "narrow", k).astype(jnp.float32)

    def look_up(held, keys, before):
        return read_back(place, ids, [held[k].astype(jnp.float32) for k in keys], keys, before)

    spread, dirichlet = gather_blocks(
        (potential * RESULT_SCALE).astype(jnp.float16),
        lambda held: look_up(held, first, None),
        lambda held, found: look_up(held, second, found),
    )
    for keys in others + [last]:
        dirichlet = look_up(spread, keys, dirichlet)
    return (potential[None], dirichlet)


def solution(mesh):
    placed = (
        P(("wide", "narrow"), None),
        P(("wide", "narrow"), None),
        P(("wide", "narrow")),
        P("narrow", "wide"),
        P(None, "wide", "narrow", None),
    )
    return jax.shard_map(
        on_device,
        mesh=mesh,
        in_specs=placed,
        out_specs=(P("narrow", "wide", None), P(("wide", "narrow"), None)),
        check_vma=False,
    )
```

time: 283 us -> 104 us (0.37)
  waiting for transfers between devices: 132 us -> 48.2 us
  blocking collectives: 77.9 us -> 0 us
  other arithmetic: 46.6 us -> 4.2 us
  starting transfers between devices: 0.12 us -> 25.1 us
  Pallas kernels: 0 us -> 24.7 us
  between operations: 13.8 us -> 0.86 us
  local copies, waits for them, and re-layouts: 6.24 us -> 0.3 us
  matrix products: 4.5 us -> 0 us
    all_gather x2 -> x0, waiting for transfers between devices: 105 us -> none  [the longest x1 61.6 us: on_device(): lax.all_gather(boundary_potential[0], 'wide', axis=0, tiled=True)]
    all_to_all x1 -> x0, blocking collectives: 77.9 us -> none  [on_device(): lax.all_to_all(spread, 'wide', split_axis=0, concat_axis=0, tiled=True)]
    ppermute x0 -> x17, waiting for transfers between devices: none -> 48.2 us  [exchange(): return lax.ppermute(block, axis, [(i, i ^ offset) for i in range(count)])]
    scatter-add x1 -> x0, other arithmetic: 39.9 us -> none  [on_device(): spread = jnp.zeros((wide_count, node_dev, images), jnp.float32).at[dest_s...]
    reduce_scatter x1 -> x0, waiting for transfers between devices: 27.1 us -> none  [on_device(): lax.psum_scatter(partial_sum.reshape(narrow_count, node_dev, images), 'na...]
    ppermute x0 -> x17, starting transfers between devices: none -> 25.1 us  [exchange(): return lax.ppermute(block, axis, [(i, i ^ offset) for i in range(count)])]
    pallas_call x0 -> x6, Pallas kernels: none -> 24.7 us  [the longest x2 12 us: scatter(): pl.pallas_call(body, grid=(nodes // tile,), in_specs=[pl.BlockSpec(block....]
    dot_general x1 -> x0, matrix products: 4.5 us -> none  [on_device(): jnp.dot(matrix_block, lax.all_gather(trace_round, 'wide', axis=0, tiled=T...]
  transfers between devices with their start and end apart: 3 -> 17, of which waited for: 3 -> 9; matrix products, arithmetic and copies ran while one was open for 0% -> 1% of each run, Pallas kernels for 0% -> 14%
where the time goes in v2:
time: 104 us; the launch traced here: 103 us
  waiting for transfers between devices  48.2 us (46%)
  starting transfers between devices  25.1 us (24%)
  Pallas kernels  24.7 us (24%)
  other arithmetic  4.2 us (4%)
    ppermute x17, waiting for transfers between devices, exchange(): return lax.ppermute(block, axis, [(i, i ^ offset) for i in range(count)])  48.2 us
    ppermute x17, starting transfers between devices, exchange(): return lax.ppermute(block, axis, [(i, i ^ offset) for i in range(count)])  25.1 us
    pallas_call x2, Pallas kernels, scatter(): pl.pallas_call(body, grid=(nodes // tile,), in_specs=[pl.BlockSpec(block....  12 us
    pallas_call x1, Pallas kernels, scatter_and_layer(): pl.pallas_call(body, grid_spec=pltpu.PrefetchScalarGridSpec(num_scalar_pr...  7.73 us
    pallas_call x3, Pallas kernels, read_back(): pl.pallas_call(body, in_specs=[pl.BlockSpec(memory_space=pltpu.SMEM)] + [...  4.97 us
  transfers between devices with their start and end apart: 17, of which 9 were waited for; matrix products, arithmetic and copies ran while one was open for 1% of the time, Pallas kernels for 14%

profile of v2, /device:TPU:0, one launch (start us, length us, event | category | flops | bytes accessed | tf_op | source)
XLA Modules:
  0.0 103.4 jit_solution(1043019756743586583)
XLA Ops:
  3.3 3.1 %collective-permute-start.2 = (f16[528,384]{1,0:T(8,128)(2,1)S(1)}, f16[528,384]{1,0:T(8,128)(2,1)S(1)}, u32[]{:S(2)}, u32[]{:S(2)}) collective-permute-start(f16[528,384]{1,0:T(8,128)(2,1)S(1)} %get-tuple-element.29), channel_id=1, source_target_pairs={{0,8},{4,12},{8,0},{12,4},{16,24},{20,28},{24,16},{28,20},{1,9},{5... | collective-permute-start | bytes 1216520 | tf_op jit(solution)/shard_map/ppermute | solution.py:16
  6.4 1.5 %collective-permute-start.1 = (f16[528,384]{1,0:T(8,128)(2,1)S(1)}, f16[528,384]{1,0:T(8,128)(2,1)S(1)}, u32[]{:S(2)}, u32[]{:S(2)}) collective-permute-start(f16[528,384]{1,0:T(8,128)(2,1)S(1)} %get-tuple-element.29), channel_id=1, source_target_pairs={{0,4},{4,0},{8,12},{12,8},{16,20},{20,16},{24,28},{28,24},{1,5},{5... | collective-permute-start | bytes 1216520 | tf_op jit(solution)/shard_map/ppermute | solution.py:16
  7.9 2.6 %collective-permute-start = (f16[528,384]{1,0:T(8,128)(2,1)S(1)}, f16[528,384]{1,0:T(8,128)(2,1)S(1)}, u32[]{:S(2)}, u32[]{:S(2)}) collective-permute-start(f16[528,384]{1,0:T(8,128)(2,1)S(1)} %get-tuple-element.29), channel_id=1, source_target_pairs={{0,16},{4,20},{8,24},{12,28},{16,0},{20,4},{24,8},{28,12},{1,17},{... | collective-permute-start | bytes 1216520 | tf_op jit(solution)/shard_map/ppermute | solution.py:16
  11.0 12.0 %collective-permute-done.2 = f16[528,384]{1,0:T(8,128)(2,1)S(1)} collective-permute-done((f16[528,384]{1,0:T(8,128)(2,1)S(1)}, f16[528,384]{1,0:T(8,128)(2,1)S(1)}, u32[]{:S(2)}, u32[]{:S(2)}) %collective-permute-start.2) | collective-permute-done | bytes 405536 | tf_op jit(solution)/shard_map/ppermute | solution.py:16
  23.0 2.3 %collective-permute-start.6 = (f16[528,384]{1,0:T(8,128)(2,1)S(1)}, f16[528,384]{1,0:T(8,128)(2,1)S(1)}, u32[]{:S(2)}, u32[]{:S(2)}) collective-permute-start(f16[528,384]{1,0:T(8,128)(2,1)S(1)} %collective-permute-done.2), channel_id=1, source_target_pairs={{0,4},{4,0},{8,12},{12,8},{16,20},{20,16},{24,28},{28,24},{1,5},{5... | collective-permute-start | bytes 1216520 | tf_op jit(solution)/shard_map/ppermute | solution.py:16
  25.3 6.0 %scatter_traces.2.refs_3_ = f32[2048,384]{1,0:T(8,128)S(1)} custom-call(f32[528,384]{1,0:T(8,128)S(1)} %get-tuple-element.28.refs_0_, f32[528,384]{1,0:T(8,128)S(1)} %convert_element_type.91.refs_1_, f32[528,384]{1,0:T(8,128)S(1)} %convert_element_type.92.refs_2_), custom_call_target="tpu_custom_call" | custom-call | flops 4831838208 | bytes 6291456 | tf_op jit(solution)/shard_map/scatter_traces/pallas_call | solution.py:112
  31.3 7.2 %collective-permute-done = f16[528,384]{1,0:T(8,128)(2,1)S(1)} collective-permute-done((f16[528,384]{1,0:T(8,128)(2,1)S(1)}, f16[528,384]{1,0:T(8,128)(2,1)S(1)}, u32[]{:S(2)}, u32[]{:S(2)}) %collective-permute-start) | collective-permute-done | bytes 405536 | tf_op jit(solution)/shard_map/ppermute | solution.py:16
  39.2 1.6 %collective-permute-start.5 = (f16[528,384]{1,0:T(8,128)(2,1)S(1)}, f16[528,384]{1,0:T(8,128)(2,1)S(1)}, u32[]{:S(2)}, u32[]{:S(2)}) collective-permute-start(f16[528,384]{1,0:T(8,128)(2,1)S(1)} %collective-permute-done.4), channel_id=1, source_target_pairs={{0,4},{4,0},{8,12},{12,8},{16,20},{20,16},{24,28},{28,24},{1,5},{5... | collective-permute-start | bytes 1216520 | tf_op jit(solution)/shard_map/ppermute | solution.py:16
  40.9 6.0 %scatter_traces.3.refs_2_ = f32[2048,384]{1,0:T(8,128)S(1)} custom-call(f32[528,384]{1,0:T(8,128)S(1)} %convert_element_type.93.refs_0_, f32[528,384]{1,0:T(8,128)S(1)} %convert_element_type.94.refs_1_, f32[528,384]{1,0:T(8,128)S(1)} %convert_element_type.95.refs_2_, f32[2048,384]{1,0:T(8,128)S(1)} %scatter_traces.2.refs_3_), custom_call_target="tpu_custom_call" | custom-call | flops 4831838208 | bytes 6291456 | tf_op jit(solution)/shard_map/scatter_traces/pallas_call | solution.py:112
  46.9 4.2 %collective-permute-done.5 = f16[528,384]{1,0:T(8,128)(2,1)S(1)} collective-permute-done((f16[528,384]{1,0:T(8,128)(2,1)S(1)}, f16[528,384]{1,0:T(8,128)(2,1)S(1)}, u32[]{:S(2)}, u32[]{:S(2)}) %collective-permute-start.5) | collective-permute-done | bytes 405536 | tf_op jit(solution)/shard_map/ppermute | solution.py:16
  51.3 7.7 %scatter_and_layer.1 = (f32[256,384]{1,0:T(8,128)S(1)}, bf16[256,384]{1,0:T(8,128)(2,1)S(1)}, bf16[256,384]{1,0:T(8,128)(2,1)S(1)}, bf16[256,384]{1,0:T(8,128)(2,1)S(1)}) custom-call(s32[2]{0:T(128)S(1)} %pad_add_fusion.place_ref, f32[528,384]{1,0:T(8,128)S(1)} %convert_element_type.96.refs_0_, f32[528,384]{1,0:T(8,128)S(1)} %convert_element_type.97.refs_1_, ...), custom_call_target="tpu_custom_call" | custom-call | flops 4831838208 | bytes 6291456 | tf_op jit(solution)/shard_map/scatter_and_layer/pallas_call | solution.py:165
  59.1 1.6 %collective-permute-start.8 = (bf16[256,384]{1,0:T(8,128)(2,1)S(1)}, bf16[256,384]{1,0:T(8,128)(2,1)S(1)}, u32[]{:S(2)}, u32[]{:S(2)}) collective-permute-start(bf16[256,384]{1,0:T(8,128)(2,1)S(1)} %get-tuple-element.20), channel_id=1, source_target_pairs={{0,2},{1,3},{2,0},{3,1},{4,6},{5,7},{6,4},{7,5},{8,10},{9,11},{10,... | collective-permute-start | bytes 589832 | tf_op jit(solution)/shard_map/ppermute | solution.py:16
  61.0 5.9 %collective-permute-done.8 = bf16[256,384]{1,0:T(8,128)(2,1)S(1)} collective-permute-done((bf16[256,384]{1,0:T(8,128)(2,1)S(1)}, bf16[256,384]{1,0:T(8,128)(2,1)S(1)}, u32[]{:S(2)}, u32[]{:S(2)}) %collective-permute-start.8) | collective-permute-done | bytes 196640 | tf_op jit(solution)/shard_map/ppermute | solution.py:16
  66.9 3.3 %collective-permute-done.9 = bf16[256,384]{1,0:T(8,128)(2,1)S(1)} collective-permute-done((bf16[256,384]{1,0:T(8,128)(2,1)S(1)}, bf16[256,384]{1,0:T(8,128)(2,1)S(1)}, u32[]{:S(2)}, u32[]{:S(2)}) %collective-permute-start.9) | collective-permute-done | bytes 196640 | tf_op jit(solution)/shard_map/ppermute | solution.py:16
  71.1 1.7 %collective-permute-start.11 = (f16[256,384]{1,0:T(8,128)(2,1)S(1)}, f16[256,384]{1,0:T(8,128)(2,1)S(1)}, u32[]{:S(2)}, u32[]{:S(2)}) collective-permute-start(f16[256,384]{1,0:T(8,128)(2,1)S(1)} %get-tuple-element.27), channel_id=1, source_target_pairs={{0,4},{4,0},{8,12},{12,8},{16,20},{20,16},{24,28},{28,24},{1,5},{5... | collective-permute-start | bytes 589832 | tf_op jit(solution)/shard_map/ppermute | solution.py:16
  72.8 3.5 %collective-permute-start.12 = (f16[256,384]{1,0:T(8,128)(2,1)S(1)}, f16[256,384]{1,0:T(8,128)(2,1)S(1)}, u32[]{:S(2)}, u32[]{:S(2)}) collective-permute-start(f16[256,384]{1,0:T(8,128)(2,1)S(1)} %get-tuple-element.27), channel_id=1, source_target_pairs={{0,8},{4,12},{8,0},{12,4},{16,24},{20,28},{24,16},{28,20},{1,9},{5... | collective-permute-start | bytes 589832 | tf_op jit(solution)/shard_map/ppermute | solution.py:16
  76.3 2.2 %collective-permute-start.10 = (f16[256,384]{1,0:T(8,128)(2,1)S(1)}, f16[256,384]{1,0:T(8,128)(2,1)S(1)}, u32[]{:S(2)}, u32[]{:S(2)}) collective-permute-start(f16[256,384]{1,0:T(8,128)(2,1)S(1)} %get-tuple-element.27), channel_id=1, source_target_pairs={{0,16},{4,20},{8,24},{12,28},{16,0},{20,4},{24,8},{28,12},{1,17},{... | collective-permute-start | bytes 589832 | tf_op jit(solution)/shard_map/ppermute | solution.py:16
  78.9 5.9 %collective-permute-done.12 = f16[256,384]{1,0:T(8,128)(2,1)S(1)} collective-permute-done((f16[256,384]{1,0:T(8,128)(2,1)S(1)}, f16[256,384]{1,0:T(8,128)(2,1)S(1)}, u32[]{:S(2)}, u32[]{:S(2)}) %collective-permute-start.12) | collective-permute-done | bytes 196640 | tf_op jit(solution)/shard_map/ppermute | solution.py:16
  84.9 1.6 %collective-permute-start.16 = (f16[256,384]{1,0:T(8,128)(2,1)S(1)}, f16[256,384]{1,0:T(8,128)(2,1)S(1)}, u32[]{:S(2)}, u32[]{:S(2)}) collective-permute-start(f16[256,384]{1,0:T(8,128)(2,1)S(1)} %collective-permute-done.12), channel_id=1, source_target_pairs={{0,4},{4,0},{8,12},{12,8},{16,20},{20,16},{24,28},{28,24},{1,5},{5... | collective-permute-start | bytes 589832 | tf_op jit(solution)/shard_map/ppermute | solution.py:16
  88.0 5.4 %collective-permute-done.10 = f16[256,384]{1,0:T(8,128)(2,1)S(1)} collective-permute-done((f16[256,384]{1,0:T(8,128)(2,1)S(1)}, f16[256,384]{1,0:T(8,128)(2,1)S(1)}, u32[]{:S(2)}, u32[]{:S(2)}) %collective-permute-start.10) | collective-permute-done | bytes 196640 | tf_op jit(solution)/shard_map/ppermute | solution.py:16
  93.4 1.5 %collective-permute-start.13 = (f16[256,384]{1,0:T(8,128)(2,1)S(1)}, f16[256,384]{1,0:T(8,128)(2,1)S(1)}, u32[]{:S(2)}, u32[]{:S(2)}) collective-permute-start(f16[256,384]{1,0:T(8,128)(2,1)S(1)} %collective-permute-done.10), channel_id=1, source_target_pairs={{0,4},{4,0},{8,12},{12,8},{16,20},{20,16},{24,28},{28,24},{1,5},{5... | collective-permute-start | bytes 589832 | tf_op jit(solution)/shard_map/ppermute | solution.py:16
  97.0 2.1 %collective-permute-done.13 = f16[256,384]{1,0:T(8,128)(2,1)S(1)} collective-permute-done((f16[256,384]{1,0:T(8,128)(2,1)S(1)}, f16[256,384]{1,0:T(8,128)(2,1)S(1)}, u32[]{:S(2)}, u32[]{:S(2)}) %collective-permute-start.13) | collective-permute-done | bytes 196640 | tf_op jit(solution)/shard_map/ppermute | solution.py:16
  99.1 2.1 %collective-permute-done.15 = f16[256,384]{1,0:T(8,128)(2,1)S(1)} collective-permute-done((f16[256,384]{1,0:T(8,128)(2,1)S(1)}, f16[256,384]{1,0:T(8,128)(2,1)S(1)}, u32[]{:S(2)}, u32[]{:S(2)}) %collective-permute-start.15) | collective-permute-done | bytes 196640 | tf_op jit(solution)/shard_map/ppermute | solution.py:16
  101.3 2.1 %read_back.5 = f32[512,384]{1,0:T(8,128)} custom-call(s32[2]{0:T(128)S(1)} %pad_add_fusion.place_ref, s32[512,1]{1,0:T(8,128)S(1)} %copy.10.ids_ref, f32[256,384]{1,0:T(8,128)S(1)} %convert_element_type.108.refs_0_, f32[256,384]{1,0:T(8,128)S(1)} %convert_element_type.109.refs_1_, f32[512,384]{1,0:T(8,128)S(1)} %read_back.4.refs_2_), custom_call_target="tpu_custom_call" | custom-call | flops 402653184 | bytes 1572864 | tf_op jit(solution)/shard_map/read_back/pallas_call | solution.py:213
  (49 shorter events, 9.3 us)
Async XLA Ops:
  0.6 10.1 %copy-start.3 = (f32[1,256]{1,0:T(1,128)S(1)}, f32[1,256]{1,0:T(1,128)}, u32[]{:S(2)}) copy-start(f32[1,256]{1,0:T(1,128)} %param.8) | copy-start | bytes 3076
  3.3 19.6 %collective-permute-start.2 = (f16[528,384]{1,0:T(8,128)(2,1)S(1)}, f16[528,384]{1,0:T(8,128)(2,1)S(1)}, u32[]{:S(2)}, u32[]{:S(2)}) collective-permute-start(f16[528,384]{1,0:T(8,128)(2,1)S(1)} %get-tuple-element.29), channel_id=1, source_target_pairs={{0,8},{4,12},{8,0},{12,4},{16,24},{20,28},{24,16},{28,20},{1,9},{5... | collective-permute-start | bytes 1216520 | tf_op jit(solution)/shard_map/ppermute | solution.py:16
  6.4 18.9 %collective-permute-start.1 = (f16[528,384]{1,0:T(8,128)(2,1)S(1)}, f16[528,384]{1,0:T(8,128)(2,1)S(1)}, u32[]{:S(2)}, u32[]{:S(2)}) collective-permute-start(f16[528,384]{1,0:T(8,128)(2,1)S(1)} %get-tuple-element.29), channel_id=1, source_target_pairs={{0,4},{4,0},{8,12},{12,8},{16,20},{20,16},{24,28},{28,24},{1,5},{5... | collective-permute-start | bytes 1216520 | tf_op jit(solution)/shard_map/ppermute | solution.py:16
  7.9 30.6 %collective-permute-start = (f16[528,384]{1,0:T(8,128)(2,1)S(1)}, f16[528,384]{1,0:T(8,128)(2,1)S(1)}, u32[]{:S(2)}, u32[]{:S(2)}) collective-permute-start(f16[528,384]{1,0:T(8,128)(2,1)S(1)} %get-tuple-element.29), channel_id=1, source_target_pairs={{0,16},{4,20},{8,24},{12,28},{16,0},{20,4},{24,8},{28,12},{1,17},{... | collective-permute-start | bytes 1216520 | tf_op jit(solution)/shard_map/ppermute | solution.py:16
  10.5 28.6 %collective-permute-start.4 = (f16[528,384]{1,0:T(8,128)(2,1)S(1)}, f16[528,384]{1,0:T(8,128)(2,1)S(1)}, u32[]{:S(2)}, u32[]{:S(2)}) collective-permute-start(f16[528,384]{1,0:T(8,128)(2,1)S(1)} %get-tuple-element.29), channel_id=1, source_target_pairs={{0,24},{4,28},{8,16},{12,20},{16,8},{20,12},{24,0},{28,4},{1,25},{... | collective-permute-start | bytes 1216520 | tf_op jit(solution)/shard_map/ppermute | solution.py:16
  23.0 17.8 %collective-permute-start.6 = (f16[528,384]{1,0:T(8,128)(2,1)S(1)}, f16[528,384]{1,0:T(8,128)(2,1)S(1)}, u32[]{:S(2)}, u32[]{:S(2)}) collective-permute-start(f16[528,384]{1,0:T(8,128)(2,1)S(1)} %collective-permute-done.2), channel_id=1, source_target_pairs={{0,4},{4,0},{8,12},{12,8},{16,20},{20,16},{24,28},{28,24},{1,5},{5... | collective-permute-start | bytes 1216520 | tf_op jit(solution)/shard_map/ppermute | solution.py:16
  38.6 8.3 %collective-permute-start.3 = (f16[528,384]{1,0:T(8,128)(2,1)S(1)}, f16[528,384]{1,0:T(8,128)(2,1)S(1)}, u32[]{:S(2)}, u32[]{:S(2)}) collective-permute-start(f16[528,384]{1,0:T(8,128)(2,1)S(1)} %collective-permute-done), channel_id=1, source_target_pairs={{0,4},{4,0},{8,12},{12,8},{16,20},{20,16},{24,28},{28,24},{1,5},{5... | collective-permute-start | bytes 1216520 | tf_op jit(solution)/shard_map/ppermute | solution.py:16
  39.2 11.9 %collective-permute-start.5 = (f16[528,384]{1,0:T(8,128)(2,1)S(1)}, f16[528,384]{1,0:T(8,128)(2,1)S(1)}, u32[]{:S(2)}, u32[]{:S(2)}) collective-permute-start(f16[528,384]{1,0:T(8,128)(2,1)S(1)} %collective-permute-done.4), channel_id=1, source_target_pairs={{0,4},{4,0},{8,12},{12,8},{16,20},{20,16},{24,28},{28,24},{1,5},{5... | collective-permute-start | bytes 1216520 | tf_op jit(solution)/shard_map/ppermute | solution.py:16
  40.9 10.4 %copy-start = (bf16[4,256,1,2048]{3,1,2,0:T(8,128)(2,1)S(1)}, bf16[4,256,1,2048]{3,1,2,0:T(8,128)(2,1)}, u32[]{:S(2)}) copy-start(bf16[4,256,1,2048]{3,1,2,0:T(8,128)(2,1)} %param.9) | copy-start | bytes 12582916
  51.3 27.5 %copy-start.2 = (s32[512,1]{0,1:T(1,128)S(1)}, s32[512,1]{0,1:T(1,128)}, u32[]{:S(2)}) copy-start(s32[512,1]{0,1:T(1,128)} %param.6) | copy-start | bytes 6148
  51.3 27.5 %copy-start.1 = (s32[512]{0:T(512)S(1)}, s32[512]{0:T(512)}, u32[]{:S(2)}) copy-start(s32[512]{0:T(512)} %param.7) | copy-start | bytes 6148
  59.0 1.9 %collective-permute-start.7 = (bf16[256,384]{1,0:T(8,128)(2,1)S(1)}, bf16[256,384]{1,0:T(8,128)(2,1)S(1)}, u32[]{:S(2)}, u32[]{:S(2)}) collective-permute-start(bf16[256,384]{1,0:T(8,128)(2,1)S(1)} %get-tuple-element.19), channel_id=1, source_target_pairs={{0,1},{1,0},{2,3},{3,2},{4,5},{5,4},{6,7},{7,6},{8,9},{9,8},{10,11... | collective-permute-start | bytes 589832 | tf_op jit(solution)/shard_map/ppermute | solution.py:16
  59.1 7.8 %collective-permute-start.8 = (bf16[256,384]{1,0:T(8,128)(2,1)S(1)}, bf16[256,384]{1,0:T(8,128)(2,1)S(1)}, u32[]{:S(2)}, u32[]{:S(2)}) collective-permute-start(bf16[256,384]{1,0:T(8,128)(2,1)S(1)} %get-tuple-element.20), channel_id=1, source_target_pairs={{0,2},{1,3},{2,0},{3,1},{4,6},{5,7},{6,4},{7,5},{8,10},{9,11},{10,... | collective-permute-start | bytes 589832 | tf_op jit(solution)/shard_map/ppermute | solution.py:16
  60.7 9.5 %collective-permute-start.9 = (bf16[256,384]{1,0:T(8,128)(2,1)S(1)}, bf16[256,384]{1,0:T(8,128)(2,1)S(1)}, u32[]{:S(2)}, u32[]{:S(2)}) collective-permute-start(bf16[256,384]{1,0:T(8,128)(2,1)S(1)} %get-tuple-element.21), channel_id=1, source_target_pairs={{0,3},{1,2},{2,1},{3,0},{4,7},{5,6},{6,5},{7,4},{8,11},{9,10},{10,... | collective-permute-start | bytes 589832 | tf_op jit(solution)/shard_map/ppermute | solution.py:16
  71.1 15.4 %collective-permute-start.11 = (f16[256,384]{1,0:T(8,128)(2,1)S(1)}, f16[256,384]{1,0:T(8,128)(2,1)S(1)}, u32[]{:S(2)}, u32[]{:S(2)}) collective-permute-start(f16[256,384]{1,0:T(8,128)(2,1)S(1)} %get-tuple-element.27), channel_id=1, source_target_pairs={{0,4},{4,0},{8,12},{12,8},{16,20},{20,16},{24,28},{28,24},{1,5},{5... | collective-permute-start | bytes 589832 | tf_op jit(solution)/shard_map/ppermute | solution.py:16
  72.8 12.1 %collective-permute-start.12 = (f16[256,384]{1,0:T(8,128)(2,1)S(1)}, f16[256,384]{1,0:T(8,128)(2,1)S(1)}, u32[]{:S(2)}, u32[]{:S(2)}) collective-permute-start(f16[256,384]{1,0:T(8,128)(2,1)S(1)} %get-tuple-element.27), channel_id=1, source_target_pairs={{0,8},{4,12},{8,0},{12,4},{16,24},{20,28},{24,16},{28,20},{1,9},{5... | collective-permute-start | bytes 589832 | tf_op jit(solution)/shard_map/ppermute | solution.py:16
  76.3 17.1 %collective-permute-start.10 = (f16[256,384]{1,0:T(8,128)(2,1)S(1)}, f16[256,384]{1,0:T(8,128)(2,1)S(1)}, u32[]{:S(2)}, u32[]{:S(2)}) collective-permute-start(f16[256,384]{1,0:T(8,128)(2,1)S(1)} %get-tuple-element.27), channel_id=1, source_target_pairs={{0,16},{4,20},{8,24},{12,28},{16,0},{20,4},{24,8},{28,12},{1,17},{... | collective-permute-start | bytes 589832 | tf_op jit(solution)/shard_map/ppermute | solution.py:16
  78.5 16.4 %collective-permute-start.14 = (f16[256,384]{1,0:T(8,128)(2,1)S(1)}, f16[256,384]{1,0:T(8,128)(2,1)S(1)}, u32[]{:S(2)}, u32[]{:S(2)}) collective-permute-start(f16[256,384]{1,0:T(8,128)(2,1)S(1)} %get-tuple-element.27), channel_id=1, source_target_pairs={{0,24},{4,28},{8,16},{12,20},{16,8},{20,12},{24,0},{28,4},{1,25},{... | collective-permute-start | bytes 589832 | tf_op jit(solution)/shard_map/ppermute | solution.py:16
  84.9 10.6 %collective-permute-start.16 = (f16[256,384]{1,0:T(8,128)(2,1)S(1)}, f16[256,384]{1,0:T(8,128)(2,1)S(1)}, u32[]{:S(2)}, u32[]{:S(2)}) collective-permute-start(f16[256,384]{1,0:T(8,128)(2,1)S(1)} %collective-permute-done.12), channel_id=1, source_target_pairs={{0,4},{4,0},{8,12},{12,8},{16,20},{20,16},{24,28},{28,24},{1,5},{5... | collective-permute-start | bytes 589832 | tf_op jit(solution)/shard_map/ppermute | solution.py:16
  93.4 5.7 %collective-permute-start.13 = (f16[256,384]{1,0:T(8,128)(2,1)S(1)}, f16[256,384]{1,0:T(8,128)(2,1)S(1)}, u32[]{:S(2)}, u32[]{:S(2)}) collective-permute-start(f16[256,384]{1,0:T(8,128)(2,1)S(1)} %collective-permute-done.10), channel_id=1, source_target_pairs={{0,4},{4,0},{8,12},{12,8},{16,20},{20,16},{24,28},{28,24},{1,5},{5... | collective-permute-start | bytes 589832 | tf_op jit(solution)/shard_map/ppermute | solution.py:16
  94.9 6.3 %collective-permute-start.15 = (f16[256,384]{1,0:T(8,128)(2,1)S(1)}, f16[256,384]{1,0:T(8,128)(2,1)S(1)}, u32[]{:S(2)}, u32[]{:S(2)}) collective-permute-start(f16[256,384]{1,0:T(8,128)(2,1)S(1)} %collective-permute-done.14), channel_id=1, source_target_pairs={{0,4},{4,0},{8,12},{12,8},{16,20},{20,16},{24,28},{28,24},{1,5},{5... | collective-permute-start | bytes 589832 | tf_op jit(solution)/shard_map/ppermute | solution.py:16

commit v3 on v0

v3 whole, which is shorter than its diff:
```python
import jax
import jax.numpy as jnp
from jax import lax
from jax.experimental import pallas as pl
from jax.experimental.pallas import tpu as pltpu
from jax.sharding import PartitionSpec as P

TRACE_SCALE = 2.0**13
RESULT_SCALE = 2.0
MIB = 2**20
ROWS = 16
EXACT = 2048


def exchange(block, axis, offset):
    count = lax.axis_size(axis)
    return lax.ppermute(block, axis, [(i, i ^ offset) for i in range(count)])


def after(value, *others):
    return lax.optimization_barrier((value, *others))[0]


def gather_far(parts, split):
    whole, pieces = parts
    held = {0: [whole]}
    held[4] = [exchange(whole, "wide", 4)]
    held[2] = [exchange(whole, "wide", 2)]
    held[1] = [exchange(whole, "wide", 1)]
    if split:
        held[6] = [exchange(pieces[0], "wide", 6)]
        held[6].append(exchange(after(pieces[1], held[1][0]), "wide", 6))
    else:
        held[6] = [exchange(whole, "wide", 6)]
    return held


def id_parts(slab, local, nodes, node_dev):
    return [slab * node_dev + local] if nodes <= EXACT else [slab, local]


def with_ids(values, parts):
    slots, images = values.shape
    per = -(-slots // images)
    extra = -(-len(parts) * per // ROWS) * ROWS
    total = jnp.pad(values, ((extra, 0), (0, 0)))
    for n, part in enumerate(parts):
        for r in range(per):
            piece = part.reshape(1, slots)[:, r * images : (r + 1) * images].astype(values.dtype)
            row = n * per + r
            total = total + jnp.pad(piece, ((row, extra + slots - row - 1), (0, images - piece.shape[1])))
    return total.astype(jnp.float16)


def ids_of(tail, slots, nodes, node_dev):
    images = tail.shape[1]
    per = -(-slots // images)

    def line(first):
        pieces = [tail[first + r : first + r + 1, : min(images, slots - r * images)] for r in range(per)]
        return pieces[0] if per == 1 else jnp.concatenate(pieces, axis=1)

    return (line(0) if nodes <= EXACT else line(0) * node_dev + line(per)).astype(jnp.int32)


def store_halves(values, out, first):
    rows, images = values.shape
    high = values.astype(jnp.bfloat16)
    out[first : first + rows, :images] = high
    out[first : first + rows, images:] = (values - high.astype(jnp.float32)).astype(jnp.bfloat16)


class Rows:
    def __init__(self, data, tail, first, span):
        self.data, self.tail, self.first, self.span = data, tail, first, span
        self.count = span[1] - span[0]


def row_specs(rows):
    return [pl.BlockSpec(memory_space=pltpu.VMEM)] * (2 * len(rows))


def row_args(rows):
    return [array for part in rows for array in (part.data, part.tail)]


def scatter_tile(rows, refs, both, first_node, tile, slots, nodes, node_dev):
    @pl.when(first_node == 0)
    def _():
        done = 0
        for part, data in zip(rows, refs[::2]):
            store_halves(data[part.first : part.first + part.count, :], both, done)
            done += part.count

    picks = []
    for part, tail in zip(rows, refs[1::2]):
        node = first_node + lax.broadcasted_iota(jnp.int32, (tile, part.count), 0)
        ids = ids_of(tail, slots, nodes, node_dev)[:, part.span[0] : part.span[1]]
        picks.append(jnp.where(ids == node, 1.0, 0.0).astype(jnp.bfloat16))
    total = jnp.dot(jnp.concatenate(picks, axis=1), both[...], preferred_element_type=jnp.float32)
    images = total.shape[1] // 2
    return total[:, :images] + total[:, images:]


def scatter(rows, slots, before, nodes, node_dev):
    images = rows[0].data.shape[1]
    tile = 2 * node_dev
    depth = sum(part.count for part in rows)

    def body(*refs):
        out, both = refs[-2:]
        total = scatter_tile(rows, refs[: 2 * len(rows)], both, pl.program_id(0) * tile, tile, slots, nodes, node_dev)
        if before is not None:
            total = total + refs[2 * len(rows)][...]
        out[...] = total

    part = pl.BlockSpec((tile, images), lambda s: (s, 0))
    more = [] if before is None else [before]
    return pl.pallas_call(
        body,
        grid=(nodes // tile,),
        in_specs=row_specs(rows) + [part] * len(more),
        out_specs=part,
        out_shape=jax.ShapeDtypeStruct((nodes, images), jnp.float32),
        scratch_shapes=[pltpu.VMEM((depth, 2 * images), jnp.bfloat16)],
        compiler_params=pltpu.CompilerParams(vmem_limit_bytes=(8 + 2 * -(-depth // slots)) * MIB),
        cost_estimate=pl.CostEstimate(
            flops=4 * depth * nodes * images, bytes_accessed=8 * nodes * images, transcendentals=0
        ),
        name="scatter_traces",
    )(*row_args(rows), *more)


def row_block(place_ref, job, parts):
    offset, part = job
    return (place_ref[1] ^ offset) * parts + part


def scatter_and_layer(place, rows, slots, before, matrix, jobs, parts, nodes, node_dev):
    images = rows[0].data.shape[1]
    tile = 2 * node_dev
    steps = nodes // tile
    depth = sum(part.count for part in rows)
    count = len(jobs)
    height = node_dev // parts

    def body(place_ref, *refs):
        before_ref, matrix_ref = refs[2 * len(rows) : 2 * len(rows) + 2]
        rounded, own = refs[2 * len(rows) + 2 : 2 * len(rows) + 4]
        outs = refs[2 * len(rows) + 4 : -3]
        both, matrix_held, sems = refs[-3:]
        step = pl.program_id(0)
        fetches = []
        for n, job in enumerate(jobs):
            first = pl.multiple_of(row_block(place_ref, job, parts) * height, height)
            fetches.append(
                pltpu.make_async_copy(matrix_ref.at[pl.ds(first, height), :], matrix_held.at[n], sems.at[n])
            )

        @pl.when(step == 0)
        def _():
            for fetch in fetches:
                fetch.start()

        total = scatter_tile(rows, refs[: 2 * len(rows)], both, step * tile, tile, slots, nodes, node_dev)
        total = (total + before_ref[...]) * (1.0 / TRACE_SCALE)
        for half in range(2):
            @pl.when(2 * step + half == place_ref[0])
            def _():
                own[...] = total[half * node_dev : (half + 1) * node_dev, :]

        rounded[pl.ds(pl.multiple_of(step * tile, tile), tile), :] = total.astype(jnp.bfloat16)

        @pl.when(step == steps - 1)
        def _():
            for n, fetch in enumerate(fetches):
                fetch.wait()
                layer = jnp.dot(matrix_held[n], rounded[...], preferred_element_type=jnp.float32)
                outs[n][...] = layer.astype(outs[n].dtype)

    one = pl.BlockSpec((height, images), lambda s, p: (0, 0))
    limit = 10 + 2 * -(-depth // slots) + (2 * count * height * nodes + 4 * nodes * images) // MIB
    return pl.pallas_call(
        body,
        grid_spec=pltpu.PrefetchScalarGridSpec(
            num_scalar_prefetch=1,
            grid=(steps,),
            in_specs=row_specs(rows)
            + [pl.BlockSpec((tile, images), lambda s, p: (s, 0)), pl.BlockSpec(memory_space=pl.ANY)],
            out_specs=[
                pl.BlockSpec((nodes, images), lambda s, p: (0, 0)),
                pl.BlockSpec((node_dev, images), lambda s, p: (0, 0)),
            ]
            + [one] * count,
            scratch_shapes=[
                pltpu.VMEM((depth, 2 * images), jnp.bfloat16),
                pltpu.VMEM((count, height, nodes), matrix.dtype),
                pltpu.SemaphoreType.DMA((count,)),
            ],
        ),
        out_shape=[
            jax.ShapeDtypeStruct((nodes, images), jnp.bfloat16),
            jax.ShapeDtypeStruct((node_dev, images), jnp.float32),
        ]
        + [jax.ShapeDtypeStruct((height, images), jnp.bfloat16)] * count,
        compiler_params=pltpu.CompilerParams(vmem_limit_bytes=limit * MIB),
        cost_estimate=pl.CostEstimate(
            flops=4 * depth * nodes * images + 2 * count * height * nodes * images,
            bytes_accessed=8 * nodes * images,
            transcendentals=0,
        ),
        name="scatter_and_layer",
    )(place, *row_args(rows), before, matrix)


def layer_more(place, rounded, own, matrix, diagonal, jobs, parts):
    node_dev, images = own.shape
    nodes = rounded.shape[0]
    count = len(jobs)
    height = node_dev // parts

    def body(place_ref, rounded_ref, own_ref, diagonal_ref, *refs):
        for n, (offset, part) in enumerate(jobs):
            layer = jnp.dot(refs[n][...], rounded_ref[...], preferred_element_type=jnp.float32)
            if offset == 0:
                here = slice(part * height, (part + 1) * height)
                layer = layer + diagonal_ref[here, :] * own_ref[here, :]
            refs[count + n][...] = layer.astype(refs[count + n].dtype)

    def spec(array):
        return pl.BlockSpec(array.shape, lambda i, p: (0, 0))

    return pl.pallas_call(
        body,
        grid_spec=pltpu.PrefetchScalarGridSpec(
            num_scalar_prefetch=1,
            grid=(1,),
            in_specs=[spec(rounded), spec(own), spec(diagonal)]
            + [pl.BlockSpec((height, nodes), lambda i, p, job=job: (row_block(p, job, parts), 0)) for job in jobs],
            out_specs=[pl.BlockSpec((height, images), lambda i, p: (0, 0))] * count,
        ),
        out_shape=[
            jax.ShapeDtypeStruct((height, images), jnp.float32 if offset == 0 else jnp.bfloat16)
            for offset, _ in jobs
        ],
        compiler_params=pltpu.CompilerParams(
            vmem_limit_bytes=(8 + (4 * nodes * images + 4 * count * height * nodes) // MIB) * MIB
        ),
        cost_estimate=pl.CostEstimate(
            flops=2 * count * height * nodes * images, bytes_accessed=2 * nodes * images, transcendentals=0
        ),
        name="layer_more",
    )(place, rounded, own, diagonal, *[matrix] * count)


def read_back(place, ids, blocks, keys, parts, node_dev, before, weight=1):
    slots = ids.shape[0]
    height, images = blocks[0].shape

    def body(place_ref, ids_ref, *refs):
        out, both = refs[-2:]
        lane = lax.broadcasted_iota(jnp.int32, (slots, height), 1)
        picks = []
        for row, (key, part) in enumerate(keys):
            store_halves(refs[row][...], both, row * height)
            node = (place_ref[0] ^ key) * node_dev + part * height + lane
            picks.append(jnp.where(ids_ref[...] == node, 1.0, 0.0).astype(jnp.bfloat16))
        total = jnp.dot(jnp.concatenate(picks, axis=1), both[...], preferred_element_type=jnp.float32)
        total = (total[:, :images] + total[:, images:]) * (1.0 / RESULT_SCALE)
        if before is not None:
            total = total + refs[len(blocks)][...]
        out[...] = total

    more = [] if before is None else [before]
    vmem = pl.BlockSpec(memory_space=pltpu.VMEM)
    return pl.pallas_call(
        body,
        in_specs=[pl.BlockSpec(memory_space=pltpu.SMEM)] + [vmem] * (1 + len(blocks) + len(more)),
        out_shape=jax.ShapeDtypeStruct((slots, images), jnp.float32),
        scratch_shapes=[pltpu.VMEM((len(blocks) * height, 2 * images), jnp.bfloat16)],
        compiler_params=pltpu.CompilerParams(vmem_limit_bytes=(8 + 2 * len(blocks)) * MIB),
        cost_estimate=pl.CostEstimate(
            flops=weight * 4 * len(blocks) * height * slots * images,
            bytes_accessed=8 * slots * images,
            transcendentals=0,
        ),
        name="read_back",
    )(place, ids, *blocks, *more)


def on_device(trace_parts, node_slab, node_local, solid_fraction, influence):
    node_dev = solid_fraction.shape[1]
    slots, images = trace_parts.shape
    wide_count = lax.axis_size("wide")
    narrow_count = lax.axis_size("narrow")
    nodes = wide_count * node_dev
    place = jnp.stack([lax.axis_index("wide"), lax.axis_index("narrow")]).astype(jnp.int32)
    ids = (node_slab[:, 0] * node_dev + node_local).reshape(-1, 1)
    diagonal = (solid_fraction - 1.0).reshape(-1, 1)
    matrix = influence.reshape(narrow_count * node_dev, nodes)
    barrier = lax.optimization_barrier

    parts = id_parts(node_slab[:, 0], node_local, nodes, node_dev)
    sent = with_ids(trace_parts * TRACE_SCALE, parts)
    extra = sent.shape[0] - slots
    half = slots // 2
    held = gather_far((sent, (sent[: extra + half], sent[extra + half :])), True)

    held[3] = [exchange(held[2][0], "wide", 1)]

    def rows_of(key, part=None):
        if len(held[key]) == 1:
            data = held[key][0].astype(jnp.float32)
            return Rows(data, data, extra, (0, slots))
        tail = held[key][0].astype(jnp.float32)
        if part == 0:
            return Rows(tail, tail, extra, (0, half))
        return Rows(held[key][1].astype(jnp.float32), tail, 0, (half, slots))

    def add_up(rows, before):
        return scatter(rows, slots, before, nodes, node_dev)

    sums = add_up([rows_of(0), rows_of(1), rows_of(2)], None)
    held[4] = [after(held[4][0], sums)]
    held[5] = [exchange(held[4][0], "wide", 1)]
    held[7] = [exchange(held[6][0], "wide", 1)]
    sums = add_up([rows_of(3), rows_of(4), rows_of(6, 0)], sums)
    held[5], held[6][1], held[7][0], sums = barrier((held[5], held[6][1], held[7][0], sums))
    held[7].append(exchange(held[6][1], "wide", 1))
    sums = add_up([rows_of(5), rows_of(6, 1), rows_of(7, 0)], sums)
    held[7][1], sums = barrier((held[7][1], sums))
    step = 8
    while step < wide_count:
        for key in range(step):
            held[key ^ step] = [exchange(part, "wide", step) for part in held[key]]
        for key in range(step, 2 * step, 2):
            sums = add_up([rows_of(k, p) for k in (key, key + 1) for p in range(len(held[k]))], sums)
        step *= 2
    far = [k for k in range(narrow_count) if k >= 2]
    near = [k for k in range(narrow_count) if k < 2]
    jobs = [(k, 0) for k in far]
    rounded, own, *shares = scatter_and_layer(
        place, [rows_of(7, 1)], slots, sums, matrix, jobs, 2, nodes, node_dev
    )
    crossed = [exchange(share, "narrow", k) for share, (k, _) in zip(shares, jobs)]
    jobs = [(k, 0) for k in near] + [(k, 1) for k in far]
    shares = layer_more(place, rounded, own, matrix, diagonal, jobs, 2)
    *crossed, upper = barrier((*crossed, shares[0]))
    crossed += [exchange(share, "narrow", k) for share, (k, _) in zip(shares[1 : len(near)], jobs[1:])]
    crossed_more = [exchange(share, "narrow", k) for share, (k, _) in zip(shares[len(near) :], jobs[len(near) :])]
    shares = layer_more(place, rounded, own, matrix, diagonal, [(k, 1) for k in near], 2)
    *crossed, lower = barrier((*crossed, shares[0]))
    crossed_more += [exchange(share, "narrow", k) for share, k in zip(shares[1:], near[1:])]
    for part in crossed:
        upper = upper + part.astype(jnp.float32)
    sent = (upper * RESULT_SCALE).astype(jnp.float16)
    first = gather_far((sent, None), False)
    for part in crossed_more:
        lower = lower + part.astype(jnp.float32)
    sent = (lower * RESULT_SCALE).astype(jnp.float16)
    second = gather_far((sent, None), False)

    def look_up(keys, before, weight=1):
        blocks = [(first, second)[part][k][0].astype(jnp.float32) for k, part in keys]
        return read_back(place, ids, blocks, keys, 2, node_dev, before, weight)

    def both_parts(*keys):
        return [(k, part) for part in range(2) for k in keys]

    for held in (first, second):
        held[1], held[2] = [after(held[1][0], first[4][0])], [after(held[2][0], first[4][0])]
        held[3] = [exchange(held[2][0], "wide", 1)]
        held[5] = [exchange(held[4][0], "wide", 1)]
        held[7] = [exchange(held[6][0], "wide", 1)]
    found = look_up(both_parts(0, 1, 2), None, 1)
    found = look_up(both_parts(3, 4, 6), found)
    first[5], first[7], second[5], second[7], found = barrier((first[5], first[7], second[5], second[7], found))
    step = 8
    while step < wide_count:
        for held in (first, second):
            for key in range(step):
                held[key ^ step] = [exchange(held[key][0], "wide", step)]
        for key in range(step, 2 * step, 4):
            found = look_up(both_parts(*range(key, key + 4)), found)
        step *= 2
    dirichlet = look_up(both_parts(5, 7), found)
    potential = jnp.concatenate([upper, lower], axis=0)
    return (potential[None], dirichlet)


def solution(mesh):
    placed = (
        P(("wide", "narrow"), None),
        P(("wide", "narrow"), None),
        P(("wide", "narrow")),
        P("narrow", "wide"),
        P(None, "wide", "narrow", None),
    )
    return jax.shard_map(
        on_device,
        mesh=mesh,
        in_specs=placed,
        out_specs=(P("narrow", "wide", None), P(("wide", "narrow"), None)),
        check_vma=False,
    )
```

time: 283 us -> 97 us (0.34)
  waiting for transfers between devices: 132 us -> 22.9 us
  blocking collectives: 77.9 us -> 0 us
  other arithmetic: 46.6 us -> 4.25 us
  starting transfers between devices: 0.12 us -> 37 us
  Pallas kernels: 0 us -> 27.8 us
  between operations: 13.8 us -> 1 us
  matrix products: 4.5 us -> 0 us
    all_gather x2 -> x0, waiting for transfers between devices: 105 us -> none  [the longest x1 61.6 us: on_device(): lax.all_gather(boundary_potential[0], 'wide', axis=0, tiled=True)]
    all_to_all x1 -> x0, blocking collectives: 77.9 us -> none  [on_device(): lax.all_to_all(spread, 'wide', split_axis=0, concat_axis=0, tiled=True)]
    scatter-add x1 -> x0, other arithmetic: 39.9 us -> none  [on_device(): spread = jnp.zeros((wide_count, node_dev, images), jnp.float32).at[dest_s...]
    ppermute x0 -> x29, starting transfers between devices: none -> 37 us  [exchange(): return lax.ppermute(block, axis, [(i, i ^ offset) for i in range(count)])]
    pallas_call x0 -> x9, Pallas kernels: none -> 27.8 us  [the longest x3 15.4 us: scatter(): pl.pallas_call(body, grid=(nodes // tile,), in_specs=row_specs(rows) + [p...]
    reduce_scatter x1 -> x0, waiting for transfers between devices: 27.1 us -> none  [on_device(): lax.psum_scatter(partial_sum.reshape(narrow_count, node_dev, images), 'na...]
    ppermute x0 -> x29, waiting for transfers between devices: none -> 22.9 us  [exchange(): return lax.ppermute(block, axis, [(i, i ^ offset) for i in range(count)])]
    dot_general x1 -> x0, matrix products: 4.5 us -> none  [on_device(): jnp.dot(matrix_block, lax.all_gather(trace_round, 'wide', axis=0, tiled=T...]
  transfers between devices with their start and end apart: 3 -> 29, of which waited for: 3 -> 8; matrix products, arithmetic and copies ran while one was open for 0% -> 2% of each run, Pallas kernels for 0% -> 23%
where the time goes in v3:
time: 97 us; the launch traced here: 96.7 us
  starting transfers between devices  37 us (38%)
  Pallas kernels  27.8 us (29%)
  waiting for transfers between devices  22.9 us (24%)
  other arithmetic  4.25 us (4%)
  local copies, waits for them, and re-layouts  3.87 us (4%)
  between operations  1 us (1%)
    ppermute x29, starting transfers between devices, exchange(): return lax.ppermute(block, axis, [(i, i ^ offset) for i in range(count)])  37 us
    ppermute x29, waiting for transfers between devices, exchange(): return lax.ppermute(block, axis, [(i, i ^ offset) for i in range(count)])  22.9 us
    pallas_call x3, Pallas kernels, scatter(): pl.pallas_call(body, grid=(nodes // tile,), in_specs=row_specs(rows) + [p...  15.4 us
    pallas_call x3, Pallas kernels, read_back(): pl.pallas_call(body, in_specs=[pl.BlockSpec(memory_space=pltpu.SMEM)] + [...  5.5 us
    pallas_call x1, Pallas kernels, scatter_and_layer(): pl.pallas_call(body, grid_spec=pltpu.PrefetchScalarGridSpec(num_scalar_pr...  3.71 us
    unnamed x8, local copies, waits for them, and re-layouts  3.52 us
    pallas_call x2, Pallas kernels, layer_more(): pl.pallas_call(body, grid_spec=pltpu.PrefetchScalarGridSpec(num_scalar_pr...  3.14 us
  transfers between devices with their start and end apart: 29, of which 8 were waited for; matrix products, arithmetic and copies ran while one was open for 2% of the time, Pallas kernels for 23%

profile of v3, /device:TPU:0, one launch (start us, length us, event | category | flops | bytes accessed | tf_op | source)
XLA Modules:
  0.0 96.7 jit_solution(3601921930900699912)
XLA Ops:
  3.3 3.1 %collective-permute-start.2 = (f16[528,384]{1,0:T(8,128)(2,1)S(1)}, f16[528,384]{1,0:T(8,128)(2,1)S(1)}, u32[]{:S(2)}, u32[]{:S(2)}) collective-permute-start(f16[528,384]{1,0:T(8,128)(2,1)S(1)} %get-tuple-element.77), channel_id=1, source_target_pairs={{0,8},{4,12},{8,0},{12,4},{16,24},{20,28},{24,16},{28,20},{1,9},{5... | collective-permute-start | bytes 1216520 | tf_op jit(solution)/shard_map/ppermute | solution.py:17
  7.9 2.6 %collective-permute-start = (f16[528,384]{1,0:T(8,128)(2,1)S(1)}, f16[528,384]{1,0:T(8,128)(2,1)S(1)}, u32[]{:S(2)}, u32[]{:S(2)}) collective-permute-start(f16[528,384]{1,0:T(8,128)(2,1)S(1)} %get-tuple-element.77), channel_id=1, source_target_pairs={{0,16},{4,20},{8,24},{12,28},{16,0},{20,4},{24,8},{28,12},{1,17},{... | collective-permute-start | bytes 1216520 | tf_op jit(solution)/shard_map/ppermute | solution.py:17
  10.8 12.1 %collective-permute-done.2 = f16[528,384]{1,0:T(8,128)(2,1)S(1)} collective-permute-done((f16[528,384]{1,0:T(8,128)(2,1)S(1)}, f16[528,384]{1,0:T(8,128)(2,1)S(1)}, u32[]{:S(2)}, u32[]{:S(2)}) %collective-permute-start.2) | collective-permute-done | bytes 405536 | tf_op jit(solution)/shard_map/ppermute | solution.py:17
  23.0 2.3 %collective-permute-start.7 = (f16[528,384]{1,0:T(8,128)(2,1)S(1)}, f16[528,384]{1,0:T(8,128)(2,1)S(1)}, u32[]{:S(2)}, u32[]{:S(2)}) collective-permute-start(f16[528,384]{1,0:T(8,128)(2,1)S(1)} %collective-permute-done.2), channel_id=1, source_target_pairs={{0,4},{4,0},{8,12},{12,8},{16,20},{20,16},{24,28},{28,24},{1,5},{5... | collective-permute-start | bytes 1216520 | tf_op jit(solution)/shard_map/ppermute | solution.py:17
  25.3 6.0 %scatter_traces.3.refs_6_ = f32[2048,384]{1,0:T(8,128)S(1)} custom-call(f32[528,384]{1,0:T(8,128)S(1)} %get-tuple-element.76.refs_0_.refs_1_, f32[528,384]{1,0:T(8,128)S(1)} %get-tuple-element.76.refs_0_.refs_1_, f32[528,384]{1,0:T(8,128)S(1)} %convert_element_type.123.refs_2_.refs_3_, f32[528,384]{1,0:T(8,128)S(1)} %convert_element_type.123.refs_2_.refs_3_, ...), custom_call_target="tpu_custom_call" | custom-call | flops 4831838208 | bytes 6291456 | tf_op jit(solution)/shard_map/scatter_traces/pallas_call | solution.py:119
  31.3 1.6 %copy-done.1 = f32[2048,384]{1,0:T(8,128)} copy-done((f32[2048,384]{1,0:T(8,128)}, f32[2048,384]{1,0:T(8,128)S(1)}, u32[]{:S(2)}) %copy-start.1) | copy-done | bytes 3145752
  35.1 1.6 %collective-permute-start.6 = (f16[272,384]{1,0:T(8,128)(2,1)S(1)}, f16[272,384]{1,0:T(8,128)(2,1)S(1)}, u32[]{:S(2)}, u32[]{:S(2)}) collective-permute-start(f16[272,384]{1,0:T(8,128)(2,1)S(1)} %collective-permute-done.5), channel_id=1, source_target_pairs={{0,4},{4,0},{8,12},{12,8},{16,20},{20,16},{24,28},{28,24},{1,5},{5... | collective-permute-start | bytes 626696 | tf_op jit(solution)/shard_map/ppermute | solution.py:17
  36.8 2.5 %collective-permute-start.4 = (f16[256,384]{1,0:T(8,128)(2,1)S(1)}, f16[256,384]{1,0:T(8,128)(2,1)S(1)}, u32[]{:S(2)}, u32[]{:S(2)}) collective-permute-start(f16[256,384]{1,0:T(8,128)(2,1)S(1)} %slice.18), channel_id=1, source_target_pairs={{0,24},{4,28},{8,16},{12,20},{16,8},{20,12},{24,0},{28,4},{1,25},{... | collective-permute-start | bytes 589832 | tf_op jit(solution)/shard_map/ppermute | solution.py:17
  39.4 1.9 %copy-done.2 = f32[2048,384]{1,0:T(8,128)S(1)} copy-done((f32[2048,384]{1,0:T(8,128)S(1)}, f32[2048,384]{1,0:T(8,128)}, u32[]{:S(2)}) %copy-start.2) | copy-done | bytes 3145752
  41.3 5.1 %scatter_traces.4.refs_6_ = f32[2048,384]{1,0:T(8,128)S(1)} custom-call(f32[528,384]{1,0:T(8,128)S(1)} %convert_element_type.125.refs_0_.refs_1_, f32[528,384]{1,0:T(8,128)S(1)} %convert_element_type.125.refs_0_.refs_1_, f32[528,384]{1,0:T(8,128)S(1)} %convert_element_type.126.refs_2_.refs_3_, f32[528,384]{1,0:T(8,128)S(1)} %convert_element_type.126.refs_2_.refs_3_, ...), custom_call_target="tpu_custom_call" | custom-call | flops 4026531840 | bytes 6291456 | tf_op jit(solution)/shard_map/scatter_traces/pallas_call | solution.py:119
  46.4 1.6 %collective-permute-done.6 = f16[272,384]{1,0:T(8,128)(2,1)S(1)} collective-permute-done((f16[272,384]{1,0:T(8,128)(2,1)S(1)}, f16[272,384]{1,0:T(8,128)(2,1)S(1)}, u32[]{:S(2)}, u32[]{:S(2)}) %collective-permute-start.6) | collective-permute-done | bytes 208928 | tf_op jit(solution)/shard_map/ppermute | solution.py:17
  49.0 4.3 %scatter_traces.5.refs_2_ = f32[2048,384]{1,0:T(8,128)S(1)} custom-call(f32[528,384]{1,0:T(8,128)S(1)} %convert_element_type.128.refs_0_.refs_1_, f32[528,384]{1,0:T(8,128)S(1)} %convert_element_type.128.refs_0_.refs_1_, f32[256,384]{1,0:T(8,128)S(1)} %convert_element_type.129.refs_2_, f32[272,384]{1,0:T(8,128)S(1)} %convert_element_type.127.refs_4_.refs_5_.refs_3_, ...), custom_call_target="tpu_custom_call" | custom-call | flops 3221225472 | bytes 6291456 | tf_op jit(solution)/shard_map/scatter_traces/pallas_call | solution.py:119
  53.7 3.7 %scatter_and_layer.1 = (bf16[2048,384]{1,0:T(8,128)(2,1)S(1)}, f32[256,384]{1,0:T(8,128)S(1)}, bf16[128,384]{1,0:T(8,128)(2,1)S(1)}, bf16[128,384]{1,0:T(8,128)(2,1)S(1)}) custom-call(s32[2]{0:T(128)S(1)} %pad_add_fusion.place_ref, f32[256,384]{1,0:T(8,128)S(1)} %convert_element_type.131.refs_0_, ...), custom_call_target="tpu_custom_call" | custom-call | flops 1207959552 | bytes 6291456 | tf_op jit(solution)/shard_map/scatter_and_layer/pallas_call | solution.py:183
  57.4 1.6 %collective-permute-start.9 = (bf16[128,384]{1,0:T(8,128)(2,1)S(1)}, bf16[128,384]{1,0:T(8,128)(2,1)S(1)}, u32[]{:S(2)}, u32[]{:S(2)}) collective-permute-start(bf16[128,384]{1,0:T(8,128)(2,1)S(1)} %get-tuple-element.44), channel_id=1, source_target_pairs={{0,2},{1,3},{2,0},{3,1},{4,6},{5,7},{6,4},{7,5},{8,10},{9,11},{10,... | collective-permute-start | bytes 294920 | tf_op jit(solution)/shard_map/ppermute | solution.py:17
  59.0 1.9 %layer_more.2 = (f32[128,384]{1,0:T(8,128)S(1)}, bf16[128,384]{1,0:T(8,128)(2,1)S(1)}, bf16[128,384]{1,0:T(8,128)(2,1)S(1)}, bf16[128,384]{1,0:T(8,128)(2,1)S(1)}) custom-call(s32[2]{0:T(128)S(1)} %pad_add_fusion.place_ref, bf16[2048,384]{1,0:T(8,128)(2,1)S(1)} %get-tuple-element.46.rounded_ref, f32[256,384]{1,0:T(8,128)S(1)} %get-tuple-element.47.own_ref, ...), custom_call_target="tpu_custom_call" | custom-call | flops 805306368 | bytes 1572864 | tf_op jit(solution)/shard_map/layer_more/pallas_call | solution.py:233
  62.9 1.6 %collective-permute-start.13 = (bf16[128,384]{1,0:T(8,128)(2,1)S(1)}, bf16[128,384]{1,0:T(8,128)(2,1)S(1)}, u32[]{:S(2)}, u32[]{:S(2)}) collective-permute-start(bf16[128,384]{1,0:T(8,128)(2,1)S(1)} %get-tuple-element.59), channel_id=1, source_target_pairs={{0,3},{1,2},{2,1},{3,0},{4,7},{5,6},{6,5},{7,4},{8,11},{9,10},{10,... | collective-permute-start | bytes 294920 | tf_op jit(solution)/shard_map/ppermute | solution.py:17
  66.1 2.2 %collective-permute-start.23 = (f16[128,384]{1,0:T(8,128)(2,1)S(1)}, f16[128,384]{1,0:T(8,128)(2,1)S(1)}, u32[]{:S(2)}, u32[]{:S(2)}) collective-permute-start(f16[128,384]{1,0:T(8,128)(2,1)S(1)} %get-tuple-element.74), channel_id=1, source_target_pairs={{0,8},{4,12},{8,0},{12,4},{16,24},{20,28},{24,16},{28,20},{1,9},{5... | collective-permute-start | bytes 294920 | tf_op jit(solution)/shard_map/ppermute | solution.py:17
  68.3 1.9 %collective-permute-done.12 = bf16[128,384]{1,0:T(8,128)(2,1)S(1)} collective-permute-done((bf16[128,384]{1,0:T(8,128)(2,1)S(1)}, bf16[128,384]{1,0:T(8,128)(2,1)S(1)}, u32[]{:S(2)}, u32[]{:S(2)}) %collective-permute-start.12) | collective-permute-done | bytes 98336 | tf_op jit(solution)/shard_map/ppermute | solution.py:17
  72.7 2.5 %collective-permute-start.17 = (f16[128,384]{1,0:T(8,128)(2,1)S(1)}, f16[128,384]{1,0:T(8,128)(2,1)S(1)}, u32[]{:S(2)}, u32[]{:S(2)}) collective-permute-start(f16[128,384]{1,0:T(8,128)(2,1)S(1)} %get-tuple-element.74), channel_id=1, source_target_pairs={{0,24},{4,28},{8,16},{12,20},{16,8},{20,12},{24,0},{28,4},{1,25},{... | collective-permute-start | bytes 294920 | tf_op jit(solution)/shard_map/ppermute | solution.py:17
  76.1 2.5 %collective-permute-start.21 = (f16[128,384]{1,0:T(8,128)(2,1)S(1)}, f16[128,384]{1,0:T(8,128)(2,1)S(1)}, u32[]{:S(2)}, u32[]{:S(2)}) collective-permute-start(f16[128,384]{1,0:T(8,128)(2,1)S(1)} %get-tuple-element.71), channel_id=1, source_target_pairs={{0,24},{4,28},{8,16},{12,20},{16,8},{20,12},{24,0},{28,4},{1,25},{... | collective-permute-start | bytes 294920 | tf_op jit(solution)/shard_map/ppermute | solution.py:17
  82.8 4.8 %collective-permute-done.19 = f16[128,384]{1,0:T(8,128)(2,1)S(1)} collective-permute-done((f16[128,384]{1,0:T(8,128)(2,1)S(1)}, f16[128,384]{1,0:T(8,128)(2,1)S(1)}, u32[]{:S(2)}, u32[]{:S(2)}) %collective-permute-start.19) | collective-permute-done | bytes 98336 | tf_op jit(solution)/shard_map/ppermute | solution.py:17
  90.5 1.6 %read_back.3.refs_6_ = f32[512,384]{1,0:T(8,128)S(1)} custom-call(s32[2]{0:T(128)S(1)} %pad_add_fusion.place_ref, s32[512,1]{1,0:T(8,128)S(1)} %copy.11.ids_ref, f32[128,384]{1,0:T(8,128)S(1)} %get-tuple-element.73.refs_0_, f32[128,384]{1,0:T(8,128)S(1)} %convert_element_type.147.refs_1_, f32[128,384]{1,0:T(8,128)S(1)} %convert_element_type.148.refs_2_, ...), custom_call_target="tpu_custom_call" | custom-call | flops 603979776 | bytes 1572864 | tf_op jit(solution)/shard_map/read_back/pallas_call | solution.py:276
  92.2 1.6 %read_back.4.refs_4_ = f32[512,384]{1,0:T(8,128)S(1)} custom-call(s32[2]{0:T(128)S(1)} %pad_add_fusion.place_ref, s32[512,1]{1,0:T(8,128)S(1)} %copy.11.ids_ref, f32[128,384]{1,0:T(8,128)S(1)} %convert_element_type.140.refs_0_, f32[128,384]{1,0:T(8,128)S(1)} %convert_element_type.141.refs_1_, f32[128,384]{1,0:T(8,128)S(1)} %convert_element_type.142.refs_2_, ...), custom_call_target="tpu_custom_call" | custom-call | flops 603979776 | bytes 1572864 | tf_op jit(solution)/shard_map/read_back/pallas_call | solution.py:276
  94.5 2.2 %read_back.5 = f32[512,384]{1,0:T(8,128)} custom-call(s32[2]{0:T(128)S(1)} %pad_add_fusion.place_ref, s32[512,1]{1,0:T(8,128)S(1)} %copy.11.ids_ref, f32[128,384]{1,0:T(8,128)S(1)} %convert_element_type.152.refs_0_, f32[128,384]{1,0:T(8,128)S(1)} %convert_element_type.153.refs_1_, f32[128,384]{1,0:T(8,128)S(1)} %convert_element_type.154.refs_2_, ...), custom_call_target="tpu_custom_call" | custom-call | flops 402653184 | bytes 1572864 | tf_op jit(solution)/shard_map/read_back/pallas_call | solution.py:276
  (89 shorter events, 22.9 us)
Async XLA Ops:
  3.3 19.6 %collective-permute-start.2 = (f16[528,384]{1,0:T(8,128)(2,1)S(1)}, f16[528,384]{1,0:T(8,128)(2,1)S(1)}, u32[]{:S(2)}, u32[]{:S(2)}) collective-permute-start(f16[528,384]{1,0:T(8,128)(2,1)S(1)} %get-tuple-element.77), channel_id=1, source_target_pairs={{0,8},{4,12},{8,0},{12,4},{16,24},{20,28},{24,16},{28,20},{1,9},{5... | collective-permute-start | bytes 1216520 | tf_op jit(solution)/shard_map/ppermute | solution.py:17
  6.4 18.9 %collective-permute-start.1 = (f16[528,384]{1,0:T(8,128)(2,1)S(1)}, f16[528,384]{1,0:T(8,128)(2,1)S(1)}, u32[]{:S(2)}, u32[]{:S(2)}) collective-permute-start(f16[528,384]{1,0:T(8,128)(2,1)S(1)} %get-tuple-element.77), channel_id=1, source_target_pairs={{0,4},{4,0},{8,12},{12,8},{16,20},{20,16},{24,28},{28,24},{1,5},{5... | collective-permute-start | bytes 1216520 | tf_op jit(solution)/shard_map/ppermute | solution.py:17
  7.9 26.4 %collective-permute-start = (f16[528,384]{1,0:T(8,128)(2,1)S(1)}, f16[528,384]{1,0:T(8,128)(2,1)S(1)}, u32[]{:S(2)}, u32[]{:S(2)}) collective-permute-start(f16[528,384]{1,0:T(8,128)(2,1)S(1)} %get-tuple-element.77), channel_id=1, source_target_pairs={{0,16},{4,20},{8,24},{12,28},{16,0},{20,4},{24,8},{28,12},{1,17},{... | collective-permute-start | bytes 1216520 | tf_op jit(solution)/shard_map/ppermute | solution.py:17
  10.6 24.5 %collective-permute-start.5 = (f16[272,384]{1,0:T(8,128)(2,1)S(1)}, f16[272,384]{1,0:T(8,128)(2,1)S(1)}, u32[]{:S(2)}, u32[]{:S(2)}) collective-permute-start(f16[272,384]{1,0:T(8,128)(2,1)S(1)} %slice.19), channel_id=1, source_target_pairs={{0,24},{4,28},{8,16},{12,20},{16,8},{20,12},{24,0},{28,4},{1,25},{... | collective-permute-start | bytes 626696 | tf_op jit(solution)/shard_map/ppermute | solution.py:17
  23.0 16.3 %collective-permute-start.7 = (f16[528,384]{1,0:T(8,128)(2,1)S(1)}, f16[528,384]{1,0:T(8,128)(2,1)S(1)}, u32[]{:S(2)}, u32[]{:S(2)}) collective-permute-start(f16[528,384]{1,0:T(8,128)(2,1)S(1)} %collective-permute-done.2), channel_id=1, source_target_pairs={{0,4},{4,0},{8,12},{12,8},{16,20},{20,16},{24,28},{28,24},{1,5},{5... | collective-permute-start | bytes 1216520 | tf_op jit(solution)/shard_map/ppermute | solution.py:17
  34.3 13.7 %collective-permute-start.3 = (f16[528,384]{1,0:T(8,128)(2,1)S(1)}, f16[528,384]{1,0:T(8,128)(2,1)S(1)}, u32[]{:S(2)}, u32[]{:S(2)}) collective-permute-start(f16[528,384]{1,0:T(8,128)(2,1)S(1)} %collective-permute-done), channel_id=1, source_target_pairs={{0,4},{4,0},{8,12},{12,8},{16,20},{20,16},{24,28},{28,24},{1,5},{5... | collective-permute-start | bytes 1216520 | tf_op jit(solution)/shard_map/ppermute | solution.py:17
  35.1 12.9 %collective-permute-start.6 = (f16[272,384]{1,0:T(8,128)(2,1)S(1)}, f16[272,384]{1,0:T(8,128)(2,1)S(1)}, u32[]{:S(2)}, u32[]{:S(2)}) collective-permute-start(f16[272,384]{1,0:T(8,128)(2,1)S(1)} %collective-permute-done.5), channel_id=1, source_target_pairs={{0,4},{4,0},{8,12},{12,8},{16,20},{20,16},{24,28},{28,24},{1,5},{5... | collective-permute-start | bytes 626696 | tf_op jit(solution)/shard_map/ppermute | solution.py:17
  36.8 11.2 %collective-permute-start.4 = (f16[256,384]{1,0:T(8,128)(2,1)S(1)}, f16[256,384]{1,0:T(8,128)(2,1)S(1)}, u32[]{:S(2)}, u32[]{:S(2)}) collective-permute-start(f16[256,384]{1,0:T(8,128)(2,1)S(1)} %slice.18), channel_id=1, source_target_pairs={{0,24},{4,28},{8,16},{12,20},{16,8},{20,12},{24,0},{28,4},{1,25},{... | collective-permute-start | bytes 589832 | tf_op jit(solution)/shard_map/ppermute | solution.py:17
  48.0 5.7 %collective-permute-start.8 = (f16[256,384]{1,0:T(8,128)(2,1)S(1)}, f16[256,384]{1,0:T(8,128)(2,1)S(1)}, u32[]{:S(2)}, u32[]{:S(2)}) collective-permute-start(f16[256,384]{1,0:T(8,128)(2,1)S(1)} %collective-permute-done.4), channel_id=1, source_target_pairs={{0,4},{4,0},{8,12},{12,8},{16,20},{20,16},{24,28},{28,24},{1,5},{5... | collective-permute-start | bytes 589832 | tf_op jit(solution)/shard_map/ppermute | solution.py:17
  57.4 7.1 %collective-permute-start.9 = (bf16[128,384]{1,0:T(8,128)(2,1)S(1)}, bf16[128,384]{1,0:T(8,128)(2,1)S(1)}, u32[]{:S(2)}, u32[]{:S(2)}) collective-permute-start(bf16[128,384]{1,0:T(8,128)(2,1)S(1)} %get-tuple-element.44), channel_id=1, source_target_pairs={{0,2},{1,3},{2,0},{3,1},{4,6},{5,7},{6,4},{7,5},{8,10},{9,11},{10,... | collective-permute-start | bytes 294920 | tf_op jit(solution)/shard_map/ppermute | solution.py:17
  59.0 6.1 %collective-permute-start.10 = (bf16[128,384]{1,0:T(8,128)(2,1)S(1)}, bf16[128,384]{1,0:T(8,128)(2,1)S(1)}, u32[]{:S(2)}, u32[]{:S(2)}) collective-permute-start(bf16[128,384]{1,0:T(8,128)(2,1)S(1)} %get-tuple-element.45), channel_id=1, source_target_pairs={{0,3},{1,2},{2,1},{3,0},{4,7},{5,6},{6,5},{7,4},{8,11},{9,10},{10,... | collective-permute-start | bytes 294920 | tf_op jit(solution)/shard_map/ppermute | solution.py:17
  64.5 5.7 %collective-permute-start.12 = (bf16[128,384]{1,0:T(8,128)(2,1)S(1)}, bf16[128,384]{1,0:T(8,128)(2,1)S(1)}, u32[]{:S(2)}, u32[]{:S(2)}) collective-permute-start(bf16[128,384]{1,0:T(8,128)(2,1)S(1)} %get-tuple-element.58), channel_id=1, source_target_pairs={{0,2},{1,3},{2,0},{3,1},{4,6},{5,7},{6,4},{7,5},{8,10},{9,11},{10,... | collective-permute-start | bytes 294920 | tf_op jit(solution)/shard_map/ppermute | solution.py:17
  65.2 7.6 %collective-permute-start.15 = (f16[128,384]{1,0:T(8,128)(2,1)S(1)}, f16[128,384]{1,0:T(8,128)(2,1)S(1)}, u32[]{:S(2)}, u32[]{:S(2)}) collective-permute-start(f16[128,384]{1,0:T(8,128)(2,1)S(1)} %get-tuple-element.74), channel_id=1, source_target_pairs={{0,16},{4,20},{8,24},{12,28},{16,0},{20,4},{24,8},{28,12},{1,17},{... | collective-permute-start | bytes 294920 | tf_op jit(solution)/shard_map/ppermute | solution.py:17
  66.1 9.1 %collective-permute-start.23 = (f16[128,384]{1,0:T(8,128)(2,1)S(1)}, f16[128,384]{1,0:T(8,128)(2,1)S(1)}, u32[]{:S(2)}, u32[]{:S(2)}) collective-permute-start(f16[128,384]{1,0:T(8,128)(2,1)S(1)} %get-tuple-element.74), channel_id=1, source_target_pairs={{0,8},{4,12},{8,0},{12,4},{16,24},{20,28},{24,16},{28,20},{1,9},{5... | collective-permute-start | bytes 294920 | tf_op jit(solution)/shard_map/ppermute | solution.py:17
  70.3 5.8 %collective-permute-start.25 = (f16[128,384]{1,0:T(8,128)(2,1)S(1)}, f16[128,384]{1,0:T(8,128)(2,1)S(1)}, u32[]{:S(2)}, u32[]{:S(2)}) collective-permute-start(f16[128,384]{1,0:T(8,128)(2,1)S(1)} %get-tuple-element.71), channel_id=1, source_target_pairs={{0,8},{4,12},{8,0},{12,4},{16,24},{20,28},{24,16},{28,20},{1,9},{5... | collective-permute-start | bytes 294920 | tf_op jit(solution)/shard_map/ppermute | solution.py:17
  70.3 8.3 %collective-permute-start.27 = (f16[128,384]{1,0:T(8,128)(2,1)S(1)}, f16[128,384]{1,0:T(8,128)(2,1)S(1)}, u32[]{:S(2)}, u32[]{:S(2)}) collective-permute-start(f16[128,384]{1,0:T(8,128)(2,1)S(1)} %get-tuple-element.74), channel_id=1, source_target_pairs={{0,4},{4,0},{8,12},{12,8},{16,20},{20,16},{24,28},{28,24},{1,5},{5... | collective-permute-start | bytes 294920 | tf_op jit(solution)/shard_map/ppermute | solution.py:17
  71.3 8.5 %collective-permute-start.28 = (f16[128,384]{1,0:T(8,128)(2,1)S(1)}, f16[128,384]{1,0:T(8,128)(2,1)S(1)}, u32[]{:S(2)}, u32[]{:S(2)}) collective-permute-start(f16[128,384]{1,0:T(8,128)(2,1)S(1)} %get-tuple-element.71), channel_id=1, source_target_pairs={{0,4},{4,0},{8,12},{12,8},{16,20},{20,16},{24,28},{28,24},{1,5},{5... | collective-permute-start | bytes 294920 | tf_op jit(solution)/shard_map/ppermute | solution.py:17
  72.7 8.8 %collective-permute-start.17 = (f16[128,384]{1,0:T(8,128)(2,1)S(1)}, f16[128,384]{1,0:T(8,128)(2,1)S(1)}, u32[]{:S(2)}, u32[]{:S(2)}) collective-permute-start(f16[128,384]{1,0:T(8,128)(2,1)S(1)} %get-tuple-element.74), channel_id=1, source_target_pairs={{0,24},{4,28},{8,16},{12,20},{16,8},{20,12},{24,0},{28,4},{1,25},{... | collective-permute-start | bytes 294920 | tf_op jit(solution)/shard_map/ppermute | solution.py:17
  75.2 12.4 %collective-permute-start.19 = (f16[128,384]{1,0:T(8,128)(2,1)S(1)}, f16[128,384]{1,0:T(8,128)(2,1)S(1)}, u32[]{:S(2)}, u32[]{:S(2)}) collective-permute-start(f16[128,384]{1,0:T(8,128)(2,1)S(1)} %get-tuple-element.71), channel_id=1, source_target_pairs={{0,16},{4,20},{8,24},{12,28},{16,0},{20,4},{24,8},{28,12},{1,17},{... | collective-permute-start | bytes 294920 | tf_op jit(solution)/shard_map/ppermute | solution.py:17
  76.1 12.2 %collective-permute-start.21 = (f16[128,384]{1,0:T(8,128)(2,1)S(1)}, f16[128,384]{1,0:T(8,128)(2,1)S(1)}, u32[]{:S(2)}, u32[]{:S(2)}) collective-permute-start(f16[128,384]{1,0:T(8,128)(2,1)S(1)} %get-tuple-element.71), channel_id=1, source_target_pairs={{0,24},{4,28},{8,16},{12,20},{16,8},{20,12},{24,0},{28,4},{1,25},{... | collective-permute-start | bytes 294920 | tf_op jit(solution)/shard_map/ppermute | solution.py:17
  78.6 11.1 %collective-permute-start.24 = (f16[128,384]{1,0:T(8,128)(2,1)S(1)}, f16[128,384]{1,0:T(8,128)(2,1)S(1)}, u32[]{:S(2)}, u32[]{:S(2)}) collective-permute-start(f16[128,384]{1,0:T(8,128)(2,1)S(1)} %collective-permute-done.23), channel_id=1, source_target_pairs={{0,4},{4,0},{8,12},{12,8},{16,20},{20,16},{24,28},{28,24},{1,5},{5... | collective-permute-start | bytes 294920 | tf_op jit(solution)/shard_map/ppermute | solution.py:17
  79.8 12.4 %collective-permute-start.26 = (f16[128,384]{1,0:T(8,128)(2,1)S(1)}, f16[128,384]{1,0:T(8,128)(2,1)S(1)}, u32[]{:S(2)}, u32[]{:S(2)}) collective-permute-start(f16[128,384]{1,0:T(8,128)(2,1)S(1)} %collective-permute-done.25), channel_id=1, source_target_pairs={{0,4},{4,0},{8,12},{12,8},{16,20},{20,16},{24,28},{28,24},{1,5},{5... | collective-permute-start | bytes 294920 | tf_op jit(solution)/shard_map/ppermute | solution.py:17
  81.5 12.3 %collective-permute-start.16 = (f16[128,384]{1,0:T(8,128)(2,1)S(1)}, f16[128,384]{1,0:T(8,128)(2,1)S(1)}, u32[]{:S(2)}, u32[]{:S(2)}) collective-permute-start(f16[128,384]{1,0:T(8,128)(2,1)S(1)} %collective-permute-done.15), channel_id=1, source_target_pairs={{0,4},{4,0},{8,12},{12,8},{16,20},{20,16},{24,28},{28,24},{1,5},{5... | collective-permute-start | bytes 294920 | tf_op jit(solution)/shard_map/ppermute | solution.py:17
  87.6 6.3 %collective-permute-start.18 = (f16[128,384]{1,0:T(8,128)(2,1)S(1)}, f16[128,384]{1,0:T(8,128)(2,1)S(1)}, u32[]{:S(2)}, u32[]{:S(2)}) collective-permute-start(f16[128,384]{1,0:T(8,128)(2,1)S(1)} %collective-permute-done.17), channel_id=1, source_target_pairs={{0,4},{4,0},{8,12},{12,8},{16,20},{20,16},{24,28},{28,24},{1,5},{5... | collective-permute-start | bytes 294920 | tf_op jit(solution)/shard_map/ppermute | solution.py:17
  (9 other events, 43.8 us)

commit v4 on v3

--- a/solution.py
+++ b/solution.py
@@ -8,7 +8,7 @@
 TRACE_SCALE = 2.0**13
 RESULT_SCALE = 2.0
 MIB = 2**20
-ROWS = 16
+ROWS = 8
 EXACT = 2048
 
 
@@ -28,8 +28,7 @@
     held[2] = [exchange(whole, "wide", 2)]
     held[1] = [exchange(whole, "wide", 1)]
     if split:
-        held[6] = [exchange(pieces[0], "wide", 6)]
-        held[6].append(exchange(after(pieces[1], held[1][0]), "wide", 6))
+        held[6] = [exchange(pieces[0], "wide", 6), exchange(after(pieces[1], held[2][0]), "wide", 6)]
     else:
         held[6] = [exchange(whole, "wide", 6)]
     return held
@@ -70,6 +69,10 @@
     out[first : first + rows, images:] = (values - high.astype(jnp.float32)).astype(jnp.bfloat16)
 
 
+def cost(flops, moved, weight):
+    return pl.CostEstimate(flops=int(flops * weight) + 1, bytes_accessed=int(moved * weight) + 1, transcendentals=0)
+
+
 class Rows:
     def __init__(self, data, tail, first, span):
         self.data, self.tail, self.first, self.span = data, tail, first, span
@@ -102,7 +105,7 @@
     return total[:, :images] + total[:, images:]
 
 
-def scatter(rows, slots, before, nodes, node_dev):
+def scatter(rows, slots, before, nodes, node_dev, weight):
     images = rows[0].data.shape[1]
     tile = 2 * node_dev
     depth = sum(part.count for part in rows)
@@ -124,9 +127,7 @@
         out_shape=jax.ShapeDtypeStruct((nodes, images), jnp.float32),
         scratch_shapes=[pltpu.VMEM((depth, 2 * images), jnp.bfloat16)],
         compiler_params=pltpu.CompilerParams(vmem_limit_bytes=(8 + 2 * -(-depth // slots)) * MIB),
-        cost_estimate=pl.CostEstimate(
-            flops=4 * depth * nodes * images, bytes_accessed=8 * nodes * images, transcendentals=0
-        ),
+        cost_estimate=cost(4 * depth * nodes * images, 8 * nodes * images, weight),
         name="scatter_traces",
     )(*row_args(rows), *more)
 
@@ -136,7 +137,7 @@
     return (place_ref[1] ^ offset) * parts + part
 
 
-def scatter_and_layer(place, rows, slots, before, matrix, jobs, parts, nodes, node_dev):
+def scatter_and_layer(place, rows, slots, before, matrix, jobs, parts, nodes, node_dev, weight):
     images = rows[0].data.shape[1]
     tile = 2 * node_dev
     steps = nodes // tile
@@ -204,16 +205,14 @@
         ]
         + [jax.ShapeDtypeStruct((height, images), jnp.bfloat16)] * count,
         compiler_params=pltpu.CompilerParams(vmem_limit_bytes=limit * MIB),
-        cost_estimate=pl.CostEstimate(
-            flops=4 * depth * nodes * images + 2 * count * height * nodes * images,
-            bytes_accessed=8 * nodes * images,
-            transcendentals=0,
+        cost_estimate=cost(
+            (4 * depth + 2 * count * height) * nodes * images, 8 * nodes * images, weight
         ),
         name="scatter_and_layer",
     )(place, *row_args(rows), before, matrix)
 
 
-def layer_more(place, rounded, own, matrix, diagonal, jobs, parts):
+def layer_more(place, rounded, own, matrix, diagonal, jobs, parts, weight):
     node_dev, images = own.shape
     nodes = rounded.shape[0]
     count = len(jobs)
@@ -246,14 +245,12 @@
         compiler_params=pltpu.CompilerParams(
             vmem_limit_bytes=(8 + (4 * nodes * images + 4 * count * height * nodes) // MIB) * MIB
         ),
-        cost_estimate=pl.CostEstimate(
-            flops=2 * count * height * nodes * images, bytes_accessed=2 * nodes * images, transcendentals=0
-        ),
+        cost_estimate=cost(2 * count * height * nodes * images, 2 * nodes * images, weight),
         name="layer_more",
     )(place, rounded, own, diagonal, *[matrix] * count)
 
 
-def read_back(place, ids, blocks, keys, parts, node_dev, before, weight=1):
+def read_back(place, ids, blocks, keys, parts, node_dev, before, weight):
     slots = ids.shape[0]
     height, images = blocks[0].shape
 
@@ -279,11 +276,7 @@
         out_shape=jax.ShapeDtypeStruct((slots, images), jnp.float32),
         scratch_shapes=[pltpu.VMEM((len(blocks) * height, 2 * images), jnp.bfloat16)],
         compiler_params=pltpu.CompilerParams(vmem_limit_bytes=(8 + 2 * len(blocks)) * MIB),
-        cost_estimate=pl.CostEstimate(
-            flops=weight * 4 * len(blocks) * height * slots * images,
-            bytes_accessed=8 * slots * images,
-            transcendentals=0,
-        ),
+        cost_estimate=cost(4 * len(blocks) * height * slots * images, 8 * slots * images, weight),
         name="read_back",
     )(place, ids, *blocks, *more)
 
@@ -295,12 +288,12 @@
     narrow_count = lax.axis_size("narrow")
     nodes = wide_count * node_dev
     place = jnp.stack([lax.axis_index("wide"), lax.axis_index("narrow")]).astype(jnp.int32)
-    ids = (node_slab[:, 0] * node_dev + node_local).reshape(-1, 1)
     diagonal = (solid_fraction - 1.0).reshape(-1, 1)
     matrix = influence.reshape(narrow_count * node_dev, nodes)
     barrier = lax.optimization_barrier
 
-    parts = id_parts(node_slab[:, 0], node_local, nodes, node_dev)
+    slab = barrier(node_slab.reshape(slots))
+    parts = id_parts(slab, node_local, nodes, node_dev)
     sent = with_ids(trace_parts * TRACE_SCALE, parts)
     extra = sent.shape[0] - slots
     half = slots // 2
@@ -317,17 +310,17 @@
             return Rows(tail, tail, extra, (0, half))
         return Rows(held[key][1].astype(jnp.float32), tail, 0, (half, slots))
 
-    def add_up(rows, before):
-        return scatter(rows, slots, before, nodes, node_dev)
-
-    sums = add_up([rows_of(0), rows_of(1), rows_of(2)], None)
+    def add_up(rows, before, weight=1):
+        return scatter(rows, slots, before, nodes, node_dev, weight)
+
+    sums = add_up([rows_of(0), rows_of(1), rows_of(2)], None, 1)
     held[4] = [after(held[4][0], sums)]
     held[5] = [exchange(held[4][0], "wide", 1)]
     held[7] = [exchange(held[6][0], "wide", 1)]
-    sums = add_up([rows_of(3), rows_of(4), rows_of(6, 0)], sums)
+    sums = add_up([rows_of(3), rows_of(4), rows_of(6, 0)], sums, 1)
     held[5], held[6][1], held[7][0], sums = barrier((held[5], held[6][1], held[7][0], sums))
     held[7].append(exchange(held[6][1], "wide", 1))
-    sums = add_up([rows_of(5), rows_of(6, 1), rows_of(7, 0)], sums)
+    sums = add_up([rows_of(5), rows_of(6, 1), rows_of(7, 0)], sums, 1)
     held[7][1], sums = barrier((held[7][1], sums))
     step = 8
     while step < wide_count:
@@ -336,19 +329,21 @@
         for key in range(step, 2 * step, 2):
             sums = add_up([rows_of(k, p) for k in (key, key + 1) for p in range(len(held[k]))], sums)
         step *= 2
+    slab, local, sums = barrier((slab, node_local, sums))
+    ids = (slab * node_dev + local).reshape(-1, 1)
     far = [k for k in range(narrow_count) if k >= 2]
     near = [k for k in range(narrow_count) if k < 2]
     jobs = [(k, 0) for k in far]
     rounded, own, *shares = scatter_and_layer(
-        place, [rows_of(7, 1)], slots, sums, matrix, jobs, 2, nodes, node_dev
+        place, [rows_of(7, 1)], slots, sums, matrix, jobs, 2, nodes, node_dev, 1
     )
     crossed = [exchange(share, "narrow", k) for share, (k, _) in zip(shares, jobs)]
     jobs = [(k, 0) for k in near] + [(k, 1) for k in far]
-    shares = layer_more(place, rounded, own, matrix, diagonal, jobs, 2)
+    shares = layer_more(place, rounded, own, matrix, diagonal, jobs, 2, 1)
     *crossed, upper = barrier((*crossed, shares[0]))
     crossed += [exchange(share, "narrow", k) for share, (k, _) in zip(shares[1 : len(near)], jobs[1:])]
     crossed_more = [exchange(share, "narrow", k) for share, (k, _) in zip(shares[len(near) :], jobs[len(near) :])]
-    shares = layer_more(place, rounded, own, matrix, diagonal, [(k, 1) for k in near], 2)
+    shares = layer_more(place, rounded, own, matrix, diagonal, [(k, 1) for k in near], 2, 1)
     *crossed, lower = barrier((*crossed, shares[0]))
     crossed_more += [exchange(share, "narrow", k) for share, k in zip(shares[1:], near[1:])]
     for part in crossed:
@@ -367,14 +362,16 @@
     def both_parts(*keys):
         return [(k, part) for part in range(2) for k in keys]
 
+    far4, far6 = first[4][0], first[6][0]
+    first[4] = [after(far4, first[1][0], second[1][0])]
+    first[2], second[2] = [after(first[2][0], far4, far6)], [after(second[2][0], far4, far6)]
     for held in (first, second):
-        held[1], held[2] = [after(held[1][0], first[4][0])], [after(held[2][0], first[4][0])]
         held[3] = [exchange(held[2][0], "wide", 1)]
         held[5] = [exchange(held[4][0], "wide", 1)]
         held[7] = [exchange(held[6][0], "wide", 1)]
-    found = look_up(both_parts(0, 1, 2), None, 1)
-    found = look_up(both_parts(3, 4, 6), found)
-    first[5], first[7], second[5], second[7], found = barrier((first[5], first[7], second[5], second[7], found))
+    found = look_up(both_parts(0, 1, 2), None, 0)
+    found = look_up(both_parts(3, 4, 6) + [(5, 0), (7, 0)], found, 0)
+    second[5], second[7], found = barrier((second[5], second[7], found))
     step = 8
     while step < wide_count:
         for held in (first, second):
@@ -383,7 +380,7 @@
         for key in range(step, 2 * step, 4):
             found = look_up(both_parts(*range(key, key + 4)), found)
         step *= 2
-    dirichlet = look_up(both_parts(5, 7), found)
+    dirichlet = look_up([(5, 1), (7, 1)], found)
     potential = jnp.concatenate([upper, lower], axis=0)
     return (potential[None], dirichlet)
 

time: 97 us -> 94.5 us (0.974)
  starting transfers between devices: 37 us -> 35.4 us
    ppermute x29, starting transfers between devices: 37 us -> 35.4 us  [exchange(): return lax.ppermute(block, axis, [(i, i ^ offset) for i in range(count)])]
    unnamed x8 -> x12, local copies, waits for them, and re-layouts: 3.52 us -> 3.53 us
  transfers between devices with their start and end apart: 29 -> 29, of which waited for: 8 -> 7; matrix products, arithmetic and copies ran while one was open for 2% -> 2% of each run, Pallas kernels for 23% -> 23%
where the time goes in v4:
time: 94.5 us; the launch traced here: 94.3 us
  starting transfers between devices  35.4 us (37%)
  Pallas kernels  27.7 us (29%)
  waiting for transfers between devices  22.6 us (24%)
  local copies, waits for them, and re-layouts  3.88 us (4%)
  other arithmetic  3.58 us (4%)
  between operations  1.03 us (1%)
    ppermute x29, starting transfers between devices, exchange(): return lax.ppermute(block, axis, [(i, i ^ offset) for i in range(count)])  35.4 us
    ppermute x29, waiting for transfers between devices, exchange(): return lax.ppermute(block, axis, [(i, i ^ offset) for i in range(count)])  22.6 us
    pallas_call x3, Pallas kernels, scatter(): pl.pallas_call(body, grid=(nodes // tile,), in_specs=row_specs(rows) + [p...  15.4 us
    pallas_call x3, Pallas kernels, read_back(): pl.pallas_call(body, in_specs=[pl.BlockSpec(memory_space=pltpu.SMEM)] + [...  5.5 us
    pallas_call x1, Pallas kernels, scatter_and_layer(): pl.pallas_call(body, grid_spec=pltpu.PrefetchScalarGridSpec(num_scalar_pr...  3.63 us
    unnamed x12, local copies, waits for them, and re-layouts  3.53 us
    pallas_call x2, Pallas kernels, layer_more(): pl.pallas_call(body, grid_spec=pltpu.PrefetchScalarGridSpec(num_scalar_pr...  3.16 us
  transfers between devices with their start and end apart: 29, of which 7 were waited for; matrix products, arithmetic and copies ran while one was open for 2% of the time, Pallas kernels for 23%

profile of v4, /device:TPU:0, one launch (start us, length us, event | category | flops | bytes accessed | tf_op | source)
XLA Modules:
  0.0 94.3 jit_solution(5844314924318464645)
XLA Ops:
  2.6 3.1 %collective-permute-start.2 = (f16[520,384]{1,0:T(8,128)(2,1)S(1)}, f16[520,384]{1,0:T(8,128)(2,1)S(1)}, u32[]{:S(2)}, u32[]{:S(2)}) collective-permute-start(f16[520,384]{1,0:T(8,128)(2,1)S(1)} %get-tuple-element.77), channel_id=1, source_target_pairs={{0,8},{4,12},{8,0},{12,4},{16,24},{20,28},{24,16},{28,20},{1,9},{5... | collective-permute-start | bytes 1198088 | tf_op jit(solution)/shard_map/ppermute | solution.py:17
  7.3 2.6 %collective-permute-start = (f16[520,384]{1,0:T(8,128)(2,1)S(1)}, f16[520,384]{1,0:T(8,128)(2,1)S(1)}, u32[]{:S(2)}, u32[]{:S(2)}) collective-permute-start(f16[520,384]{1,0:T(8,128)(2,1)S(1)} %get-tuple-element.77), channel_id=1, source_target_pairs={{0,16},{4,20},{8,24},{12,28},{16,0},{20,4},{24,8},{28,12},{1,17},{... | collective-permute-start | bytes 1198088 | tf_op jit(solution)/shard_map/ppermute | solution.py:17
  10.2 11.8 %collective-permute-done.2 = f16[520,384]{1,0:T(8,128)(2,1)S(1)} collective-permute-done((f16[520,384]{1,0:T(8,128)(2,1)S(1)}, f16[520,384]{1,0:T(8,128)(2,1)S(1)}, u32[]{:S(2)}, u32[]{:S(2)}) %collective-permute-start.2) | collective-permute-done | bytes 399392 | tf_op jit(solution)/shard_map/ppermute | solution.py:17
  22.1 2.3 %collective-permute-start.7 = (f16[520,384]{1,0:T(8,128)(2,1)S(1)}, f16[520,384]{1,0:T(8,128)(2,1)S(1)}, u32[]{:S(2)}, u32[]{:S(2)}) collective-permute-start(f16[520,384]{1,0:T(8,128)(2,1)S(1)} %collective-permute-done.2), channel_id=1, source_target_pairs={{0,4},{4,0},{8,12},{12,8},{16,20},{20,16},{24,28},{28,24},{1,5},{5... | collective-permute-start | bytes 1198088 | tf_op jit(solution)/shard_map/ppermute | solution.py:17
  24.4 6.0 %scatter_traces.3.refs_6_ = f32[2048,384]{1,0:T(8,128)S(1)} custom-call(f32[520,384]{1,0:T(8,128)S(1)} %get-tuple-element.76.refs_0_.refs_1_, f32[520,384]{1,0:T(8,128)S(1)} %get-tuple-element.76.refs_0_.refs_1_, f32[520,384]{1,0:T(8,128)S(1)} %convert_element_type.123.refs_2_.refs_3_, f32[520,384]{1,0:T(8,128)S(1)} %convert_element_type.123.refs_2_.refs_3_, ...), custom_call_target="tpu_custom_call" | custom-call | flops 4831838208 | bytes 6291457 | tf_op jit(solution)/shard_map/scatter_traces/pallas_call | solution.py:122
  30.4 1.6 %copy-done.1 = f32[2048,384]{1,0:T(8,128)} copy-done((f32[2048,384]{1,0:T(8,128)}, f32[2048,384]{1,0:T(8,128)S(1)}, u32[]{:S(2)}) %copy-start.1) | copy-done | bytes 3145752
  34.0 1.6 %collective-permute-start.6 = (f16[264,384]{1,0:T(8,128)(2,1)S(1)}, f16[264,384]{1,0:T(8,128)(2,1)S(1)}, u32[]{:S(2)}, u32[]{:S(2)}) collective-permute-start(f16[264,384]{1,0:T(8,128)(2,1)S(1)} %collective-permute-done.5), channel_id=1, source_target_pairs={{0,4},{4,0},{8,12},{12,8},{16,20},{20,16},{24,28},{28,24},{1,5},{5... | collective-permute-start | bytes 608264 | tf_op jit(solution)/shard_map/ppermute | solution.py:17
  35.7 2.5 %collective-permute-start.4 = (f16[256,384]{1,0:T(8,128)(2,1)S(1)}, f16[256,384]{1,0:T(8,128)(2,1)S(1)}, u32[]{:S(2)}, u32[]{:S(2)}) collective-permute-start(f16[256,384]{1,0:T(8,128)(2,1)S(1)} %slice.18), channel_id=1, source_target_pairs={{0,24},{4,28},{8,16},{12,20},{16,8},{20,12},{24,0},{28,4},{1,25},{... | collective-permute-start | bytes 589832 | tf_op jit(solution)/shard_map/ppermute | solution.py:17
  38.3 1.9 %copy-done.2 = f32[2048,384]{1,0:T(8,128)S(1)} copy-done((f32[2048,384]{1,0:T(8,128)S(1)}, f32[2048,384]{1,0:T(8,128)}, u32[]{:S(2)}) %copy-start.2) | copy-done | bytes 3145752
  40.2 5.1 %scatter_traces.4.refs_6_ = f32[2048,384]{1,0:T(8,128)S(1)} custom-call(f32[520,384]{1,0:T(8,128)S(1)} %convert_element_type.125.refs_0_.refs_1_, f32[520,384]{1,0:T(8,128)S(1)} %convert_element_type.125.refs_0_.refs_1_, f32[520,384]{1,0:T(8,128)S(1)} %convert_element_type.126.refs_2_.refs_3_, f32[520,384]{1,0:T(8,128)S(1)} %convert_element_type.126.refs_2_.refs_3_, ...), custom_call_target="tpu_custom_call" | custom-call | flops 4026531840 | bytes 6291457 | tf_op jit(solution)/shard_map/scatter_traces/pallas_call | solution.py:122
  45.3 1.6 %collective-permute-done.6 = f16[264,384]{1,0:T(8,128)(2,1)S(1)} collective-permute-done((f16[264,384]{1,0:T(8,128)(2,1)S(1)}, f16[264,384]{1,0:T(8,128)(2,1)S(1)}, u32[]{:S(2)}, u32[]{:S(2)}) %collective-permute-start.6) | collective-permute-done | bytes 202784 | tf_op jit(solution)/shard_map/ppermute | solution.py:17
  47.6 4.3 %scatter_traces.5.refs_2_ = f32[2048,384]{1,0:T(8,128)S(1)} custom-call(f32[520,384]{1,0:T(8,128)S(1)} %convert_element_type.128.refs_0_.refs_1_, f32[520,384]{1,0:T(8,128)S(1)} %convert_element_type.128.refs_0_.refs_1_, f32[256,384]{1,0:T(8,128)S(1)} %convert_element_type.129.refs_2_, f32[264,384]{1,0:T(8,128)S(1)} %convert_element_type.127.refs_4_.refs_5_.refs_3_, ...), custom_call_target="tpu_custom_call" | custom-call | flops 3221225472 | bytes 6291457 | tf_op jit(solution)/shard_map/scatter_traces/pallas_call | solution.py:122
  52.7 3.6 %scatter_and_layer.1 = (bf16[2048,384]{1,0:T(8,128)(2,1)S(1)}, f32[256,384]{1,0:T(8,128)S(1)}, bf16[128,384]{1,0:T(8,128)(2,1)S(1)}, bf16[128,384]{1,0:T(8,128)(2,1)S(1)}) custom-call(s32[2]{0:T(128)S(1)} %pad_add_fusion.place_ref, f32[256,384]{1,0:T(8,128)S(1)} %convert_element_type.131.refs_0_, ...), custom_call_target="tpu_custom_call" | custom-call | flops 1207959552 | bytes 6291457 | tf_op jit(solution)/shard_map/scatter_and_layer/pallas_call | solution.py:184
  56.3 1.6 %collective-permute-start.9 = (bf16[128,384]{1,0:T(8,128)(2,1)S(1)}, bf16[128,384]{1,0:T(8,128)(2,1)S(1)}, u32[]{:S(2)}, u32[]{:S(2)}) collective-permute-start(bf16[128,384]{1,0:T(8,128)(2,1)S(1)} %get-tuple-element.45), channel_id=1, source_target_pairs={{0,2},{1,3},{2,0},{3,1},{4,6},{5,7},{6,4},{7,5},{8,10},{9,11},{10,... | collective-permute-start | bytes 294920 | tf_op jit(solution)/shard_map/ppermute | solution.py:17
  57.9 1.9 %layer_more.2 = (f32[128,384]{1,0:T(8,128)S(1)}, bf16[128,384]{1,0:T(8,128)(2,1)S(1)}, bf16[128,384]{1,0:T(8,128)(2,1)S(1)}, bf16[128,384]{1,0:T(8,128)(2,1)S(1)}) custom-call(s32[2]{0:T(128)S(1)} %pad_add_fusion.place_ref, bf16[2048,384]{1,0:T(8,128)(2,1)S(1)} %get-tuple-element.47.rounded_ref, f32[256,384]{1,0:T(8,128)S(1)} %get-tuple-element.48.own_ref, ...), custom_call_target="tpu_custom_call" | custom-call | flops 805306368 | bytes 1572865 | tf_op jit(solution)/shard_map/layer_more/pallas_call | solution.py:232
  61.8 1.6 %collective-permute-start.13 = (bf16[128,384]{1,0:T(8,128)(2,1)S(1)}, bf16[128,384]{1,0:T(8,128)(2,1)S(1)}, u32[]{:S(2)}, u32[]{:S(2)}) collective-permute-start(bf16[128,384]{1,0:T(8,128)(2,1)S(1)} %get-tuple-element.60), channel_id=1, source_target_pairs={{0,3},{1,2},{2,1},{3,0},{4,7},{5,6},{6,5},{7,4},{8,11},{9,10},{10,... | collective-permute-start | bytes 294920 | tf_op jit(solution)/shard_map/ppermute | solution.py:17
  64.1 3.0 %collective-permute-start.20 = (f16[128,384]{1,0:T(8,128)(2,1)S(1)}, f16[128,384]{1,0:T(8,128)(2,1)S(1)}, u32[]{:S(2)}, u32[]{:S(2)}) collective-permute-start(f16[128,384]{1,0:T(8,128)(2,1)S(1)} %get-tuple-element.74), channel_id=1, source_target_pairs={{0,16},{4,20},{8,24},{12,28},{16,0},{20,4},{24,8},{28,12},{1,17},{... | collective-permute-start | bytes 294920 | tf_op jit(solution)/shard_map/ppermute | solution.py:17
  70.7 4.6 %collective-permute-done.20 = f16[128,384]{1,0:T(8,128)(2,1)S(1)} collective-permute-done((f16[128,384]{1,0:T(8,128)(2,1)S(1)}, f16[128,384]{1,0:T(8,128)(2,1)S(1)}, u32[]{:S(2)}, u32[]{:S(2)}) %collective-permute-start.20) | collective-permute-done | bytes 98336 | tf_op jit(solution)/shard_map/ppermute | solution.py:17
  75.3 4.3 %collective-permute-start.17 = (f16[128,384]{1,0:T(8,128)(2,1)S(1)}, f16[128,384]{1,0:T(8,128)(2,1)S(1)}, u32[]{:S(2)}, u32[]{:S(2)}) collective-permute-start(f16[128,384]{1,0:T(8,128)(2,1)S(1)} %get-tuple-element.71), channel_id=1, source_target_pairs={{0,24},{4,28},{8,16},{12,20},{16,8},{20,12},{24,0},{28,4},{1,25},{... | collective-permute-start | bytes 294920 | tf_op jit(solution)/shard_map/ppermute | solution.py:17
  79.7 2.0 %collective-permute-start.26 = (f16[128,384]{1,0:T(8,128)(2,1)S(1)}, f16[128,384]{1,0:T(8,128)(2,1)S(1)}, u32[]{:S(2)}, u32[]{:S(2)}) collective-permute-start(f16[128,384]{1,0:T(8,128)(2,1)S(1)} %collective-permute-done.25), channel_id=1, source_target_pairs={{0,4},{4,0},{8,12},{12,8},{16,20},{20,16},{24,28},{28,24},{1,5},{5... | collective-permute-start | bytes 294920 | tf_op jit(solution)/shard_map/ppermute | solution.py:17
  81.8 1.6 %collective-permute-done.15 = f16[128,384]{1,0:T(8,128)(2,1)S(1)} collective-permute-done((f16[128,384]{1,0:T(8,128)(2,1)S(1)}, f16[128,384]{1,0:T(8,128)(2,1)S(1)}, u32[]{:S(2)}, u32[]{:S(2)}) %collective-permute-start.15) | collective-permute-done | bytes 98336 | tf_op jit(solution)/shard_map/ppermute | solution.py:17
  84.6 1.6 %read_back.3.refs_8_ = f32[512,384]{1,0:T(8,128)S(1)} custom-call(s32[2]{0:T(128)S(1)} %pad_add_fusion.place_ref, s32[512,1]{1,0:T(8,128)S(1)} %copy.11.ids_ref, f32[128,384]{1,0:T(8,128)S(1)} %get-tuple-element.73.refs_0_, f32[128,384]{1,0:T(8,128)S(1)} %convert_element_type.149.refs_1_, f32[128,384]{1,0:T(8,128)S(1)} %convert_element_type.150.refs_2_, ...), custom_call_target="tpu_custom_call" | custom-call | flops 1 | bytes 1 | tf_op jit(solution)/shard_map/read_back/pallas_call | solution.py:273
  90.3 1.9 %read_back.4.refs_2_ = f32[512,384]{1,0:T(8,128)S(1)} custom-call(s32[2]{0:T(128)S(1)} %pad_add_fusion.place_ref, s32[512,1]{1,0:T(8,128)S(1)} %copy.11.ids_ref, f32[128,384]{1,0:T(8,128)S(1)} %convert_element_type.140.refs_0_, f32[128,384]{1,0:T(8,128)S(1)} %convert_element_type.141.refs_1_, f32[128,384]{1,0:T(8,128)S(1)} %convert_element_type.142.refs_2_, ...), custom_call_target="tpu_custom_call" | custom-call | flops 1 | bytes 1 | tf_op jit(solution)/shard_map/read_back/pallas_call | solution.py:273
  92.3 1.9 %read_back.5 = f32[512,384]{1,0:T(8,128)} custom-call(s32[2]{0:T(128)S(1)} %pad_add_fusion.place_ref, s32[512,1]{1,0:T(8,128)S(1)} %copy.11.ids_ref, f32[128,384]{1,0:T(8,128)S(1)} %convert_element_type.154.refs_0_, f32[128,384]{1,0:T(8,128)S(1)} %convert_element_type.155.refs_1_, f32[512,384]{1,0:T(8,128)S(1)} %read_back.4.refs_2_), custom_call_target="tpu_custom_call" | custom-call | flops 201326592 | bytes 1572865 | tf_op jit(solution)/shard_map/read_back/pallas_call | solution.py:273
  (93 shorter events, 19.0 us)
Async XLA Ops:
  2.6 19.4 %collective-permute-start.2 = (f16[520,384]{1,0:T(8,128)(2,1)S(1)}, f16[520,384]{1,0:T(8,128)(2,1)S(1)}, u32[]{:S(2)}, u32[]{:S(2)}) collective-permute-start(f16[520,384]{1,0:T(8,128)(2,1)S(1)} %get-tuple-element.77), channel_id=1, source_target_pairs={{0,8},{4,12},{8,0},{12,4},{16,24},{20,28},{24,16},{28,20},{1,9},{5... | collective-permute-start | bytes 1198088 | tf_op jit(solution)/shard_map/ppermute | solution.py:17
  5.7 18.6 %collective-permute-start.1 = (f16[520,384]{1,0:T(8,128)(2,1)S(1)}, f16[520,384]{1,0:T(8,128)(2,1)S(1)}, u32[]{:S(2)}, u32[]{:S(2)}) collective-permute-start(f16[520,384]{1,0:T(8,128)(2,1)S(1)} %get-tuple-element.77), channel_id=1, source_target_pairs={{0,4},{4,0},{8,12},{12,8},{16,20},{20,16},{24,28},{28,24},{1,5},{5... | collective-permute-start | bytes 1198088 | tf_op jit(solution)/shard_map/ppermute | solution.py:17
  7.3 26.0 %collective-permute-start = (f16[520,384]{1,0:T(8,128)(2,1)S(1)}, f16[520,384]{1,0:T(8,128)(2,1)S(1)}, u32[]{:S(2)}, u32[]{:S(2)}) collective-permute-start(f16[520,384]{1,0:T(8,128)(2,1)S(1)} %get-tuple-element.77), channel_id=1, source_target_pairs={{0,16},{4,20},{8,24},{12,28},{16,0},{20,4},{24,8},{28,12},{1,17},{... | collective-permute-start | bytes 1198088 | tf_op jit(solution)/shard_map/ppermute | solution.py:17
  9.9 24.1 %collective-permute-start.5 = (f16[264,384]{1,0:T(8,128)(2,1)S(1)}, f16[264,384]{1,0:T(8,128)(2,1)S(1)}, u32[]{:S(2)}, u32[]{:S(2)}) collective-permute-start(f16[264,384]{1,0:T(8,128)(2,1)S(1)} %slice.19), channel_id=1, source_target_pairs={{0,24},{4,28},{8,16},{12,20},{16,8},{20,12},{24,0},{28,4},{1,25},{... | collective-permute-start | bytes 608264 | tf_op jit(solution)/shard_map/ppermute | solution.py:17
  22.1 16.2 %collective-permute-start.7 = (f16[520,384]{1,0:T(8,128)(2,1)S(1)}, f16[520,384]{1,0:T(8,128)(2,1)S(1)}, u32[]{:S(2)}, u32[]{:S(2)}) collective-permute-start(f16[520,384]{1,0:T(8,128)(2,1)S(1)} %collective-permute-done.2), channel_id=1, source_target_pairs={{0,4},{4,0},{8,12},{12,8},{16,20},{20,16},{24,28},{28,24},{1,5},{5... | collective-permute-start | bytes 1198088 | tf_op jit(solution)/shard_map/ppermute | solution.py:17
  33.2 13.7 %collective-permute-start.3 = (f16[520,384]{1,0:T(8,128)(2,1)S(1)}, f16[520,384]{1,0:T(8,128)(2,1)S(1)}, u32[]{:S(2)}, u32[]{:S(2)}) collective-permute-start(f16[520,384]{1,0:T(8,128)(2,1)S(1)} %collective-permute-done), channel_id=1, source_target_pairs={{0,4},{4,0},{8,12},{12,8},{16,20},{20,16},{24,28},{28,24},{1,5},{5... | collective-permute-start | bytes 1198088 | tf_op jit(solution)/shard_map/ppermute | solution.py:17
  34.0 12.9 %collective-permute-start.6 = (f16[264,384]{1,0:T(8,128)(2,1)S(1)}, f16[264,384]{1,0:T(8,128)(2,1)S(1)}, u32[]{:S(2)}, u32[]{:S(2)}) collective-permute-start(f16[264,384]{1,0:T(8,128)(2,1)S(1)} %collective-permute-done.5), channel_id=1, source_target_pairs={{0,4},{4,0},{8,12},{12,8},{16,20},{20,16},{24,28},{28,24},{1,5},{5... | collective-permute-start | bytes 608264 | tf_op jit(solution)/shard_map/ppermute | solution.py:17
  35.7 11.2 %collective-permute-start.4 = (f16[256,384]{1,0:T(8,128)(2,1)S(1)}, f16[256,384]{1,0:T(8,128)(2,1)S(1)}, u32[]{:S(2)}, u32[]{:S(2)}) collective-permute-start(f16[256,384]{1,0:T(8,128)(2,1)S(1)} %slice.18), channel_id=1, source_target_pairs={{0,24},{4,28},{8,16},{12,20},{16,8},{20,12},{24,0},{28,4},{1,25},{... | collective-permute-start | bytes 589832 | tf_op jit(solution)/shard_map/ppermute | solution.py:17
  56.3 7.2 %collective-permute-start.9 = (bf16[128,384]{1,0:T(8,128)(2,1)S(1)}, bf16[128,384]{1,0:T(8,128)(2,1)S(1)}, u32[]{:S(2)}, u32[]{:S(2)}) collective-permute-start(bf16[128,384]{1,0:T(8,128)(2,1)S(1)} %get-tuple-element.45), channel_id=1, source_target_pairs={{0,2},{1,3},{2,0},{3,1},{4,6},{5,7},{6,4},{7,5},{8,10},{9,11},{10,... | collective-permute-start | bytes 294920 | tf_op jit(solution)/shard_map/ppermute | solution.py:17
  57.9 6.1 %collective-permute-start.10 = (bf16[128,384]{1,0:T(8,128)(2,1)S(1)}, bf16[128,384]{1,0:T(8,128)(2,1)S(1)}, u32[]{:S(2)}, u32[]{:S(2)}) collective-permute-start(bf16[128,384]{1,0:T(8,128)(2,1)S(1)} %get-tuple-element.46), channel_id=1, source_target_pairs={{0,3},{1,2},{2,1},{3,0},{4,7},{5,6},{6,5},{7,4},{8,11},{9,10},{10,... | collective-permute-start | bytes 294920 | tf_op jit(solution)/shard_map/ppermute | solution.py:17
  61.8 6.7 %collective-permute-start.13 = (bf16[128,384]{1,0:T(8,128)(2,1)S(1)}, bf16[128,384]{1,0:T(8,128)(2,1)S(1)}, u32[]{:S(2)}, u32[]{:S(2)}) collective-permute-start(bf16[128,384]{1,0:T(8,128)(2,1)S(1)} %get-tuple-element.60), channel_id=1, source_target_pairs={{0,3},{1,2},{2,1},{3,0},{4,7},{5,6},{6,5},{7,4},{8,11},{9,10},{10,... | collective-permute-start | bytes 294920 | tf_op jit(solution)/shard_map/ppermute | solution.py:17
  64.1 6.6 %collective-permute-start.19 = (f16[128,384]{1,0:T(8,128)(2,1)S(1)}, f16[128,384]{1,0:T(8,128)(2,1)S(1)}, u32[]{:S(2)}, u32[]{:S(2)}) collective-permute-start(f16[128,384]{1,0:T(8,128)(2,1)S(1)} %get-tuple-element.74), channel_id=1, source_target_pairs={{0,8},{4,12},{8,0},{12,4},{16,24},{20,28},{24,16},{28,20},{1,9},{5... | collective-permute-start | bytes 294920 | tf_op jit(solution)/shard_map/ppermute | solution.py:17
  64.1 11.2 %collective-permute-start.20 = (f16[128,384]{1,0:T(8,128)(2,1)S(1)}, f16[128,384]{1,0:T(8,128)(2,1)S(1)}, u32[]{:S(2)}, u32[]{:S(2)}) collective-permute-start(f16[128,384]{1,0:T(8,128)(2,1)S(1)} %get-tuple-element.74), channel_id=1, source_target_pairs={{0,16},{4,20},{8,24},{12,28},{16,0},{20,4},{24,8},{28,12},{1,17},{... | collective-permute-start | bytes 294920 | tf_op jit(solution)/shard_map/ppermute | solution.py:17
  67.2 8.2 %collective-permute-start.21 = (f16[128,384]{1,0:T(8,128)(2,1)S(1)}, f16[128,384]{1,0:T(8,128)(2,1)S(1)}, u32[]{:S(2)}, u32[]{:S(2)}) collective-permute-start(f16[128,384]{1,0:T(8,128)(2,1)S(1)} %get-tuple-element.74), channel_id=1, source_target_pairs={{0,24},{4,28},{8,16},{12,20},{16,8},{20,12},{24,0},{28,4},{1,25},{... | collective-permute-start | bytes 294920 | tf_op jit(solution)/shard_map/ppermute | solution.py:17
  68.5 11.1 %collective-permute-start.23 = (f16[128,384]{1,0:T(8,128)(2,1)S(1)}, f16[128,384]{1,0:T(8,128)(2,1)S(1)}, u32[]{:S(2)}, u32[]{:S(2)}) collective-permute-start(f16[128,384]{1,0:T(8,128)(2,1)S(1)} %get-tuple-element.74), channel_id=1, source_target_pairs={{0,4},{4,0},{8,12},{12,8},{16,20},{20,16},{24,28},{28,24},{1,5},{5... | collective-permute-start | bytes 294920 | tf_op jit(solution)/shard_map/ppermute | solution.py:17
  69.4 10.2 %collective-permute-start.24 = (f16[128,384]{1,0:T(8,128)(2,1)S(1)}, f16[128,384]{1,0:T(8,128)(2,1)S(1)}, u32[]{:S(2)}, u32[]{:S(2)}) collective-permute-start(f16[128,384]{1,0:T(8,128)(2,1)S(1)} %get-tuple-element.71), channel_id=1, source_target_pairs={{0,4},{4,0},{8,12},{12,8},{16,20},{20,16},{24,28},{28,24},{1,5},{5... | collective-permute-start | bytes 294920 | tf_op jit(solution)/shard_map/ppermute | solution.py:17
  70.7 9.0 %collective-permute-start.25 = (f16[128,384]{1,0:T(8,128)(2,1)S(1)}, f16[128,384]{1,0:T(8,128)(2,1)S(1)}, u32[]{:S(2)}, u32[]{:S(2)}) collective-permute-start(f16[128,384]{1,0:T(8,128)(2,1)S(1)} %get-tuple-element.71), channel_id=1, source_target_pairs={{0,8},{4,12},{8,0},{12,4},{16,24},{20,28},{24,16},{28,20},{1,9},{5... | collective-permute-start | bytes 294920 | tf_op jit(solution)/shard_map/ppermute | solution.py:17
  75.3 8.1 %collective-permute-start.15 = (f16[128,384]{1,0:T(8,128)(2,1)S(1)}, f16[128,384]{1,0:T(8,128)(2,1)S(1)}, u32[]{:S(2)}, u32[]{:S(2)}) collective-permute-start(f16[128,384]{1,0:T(8,128)(2,1)S(1)} %get-tuple-element.71), channel_id=1, source_target_pairs={{0,16},{4,20},{8,24},{12,28},{16,0},{20,4},{24,8},{28,12},{1,17},{... | collective-permute-start | bytes 294920 | tf_op jit(solution)/shard_map/ppermute | solution.py:17
  75.3 11.0 %collective-permute-start.17 = (f16[128,384]{1,0:T(8,128)(2,1)S(1)}, f16[128,384]{1,0:T(8,128)(2,1)S(1)}, u32[]{:S(2)}, u32[]{:S(2)}) collective-permute-start(f16[128,384]{1,0:T(8,128)(2,1)S(1)} %get-tuple-element.71), channel_id=1, source_target_pairs={{0,24},{4,28},{8,16},{12,20},{16,8},{20,12},{24,0},{28,4},{1,25},{... | collective-permute-start | bytes 294920 | tf_op jit(solution)/shard_map/ppermute | solution.py:17
  79.6 7.8 %collective-permute-start.22 = (f16[128,384]{1,0:T(8,128)(2,1)S(1)}, f16[128,384]{1,0:T(8,128)(2,1)S(1)}, u32[]{:S(2)}, u32[]{:S(2)}) collective-permute-start(f16[128,384]{1,0:T(8,128)(2,1)S(1)} %collective-permute-done.19), channel_id=1, source_target_pairs={{0,4},{4,0},{8,12},{12,8},{16,20},{20,16},{24,28},{28,24},{1,5},{5... | collective-permute-start | bytes 294920 | tf_op jit(solution)/shard_map/ppermute | solution.py:17
  79.7 8.8 %collective-permute-start.26 = (f16[128,384]{1,0:T(8,128)(2,1)S(1)}, f16[128,384]{1,0:T(8,128)(2,1)S(1)}, u32[]{:S(2)}, u32[]{:S(2)}) collective-permute-start(f16[128,384]{1,0:T(8,128)(2,1)S(1)} %collective-permute-done.25), channel_id=1, source_target_pairs={{0,4},{4,0},{8,12},{12,8},{16,20},{20,16},{24,28},{28,24},{1,5},{5... | collective-permute-start | bytes 294920 | tf_op jit(solution)/shard_map/ppermute | solution.py:17
  81.7 6.8 %collective-permute-start.27 = (f16[128,384]{1,0:T(8,128)(2,1)S(1)}, f16[128,384]{1,0:T(8,128)(2,1)S(1)}, u32[]{:S(2)}, u32[]{:S(2)}) collective-permute-start(f16[128,384]{1,0:T(8,128)(2,1)S(1)} %collective-permute-done.20), channel_id=1, source_target_pairs={{0,4},{4,0},{8,12},{12,8},{16,20},{20,16},{24,28},{28,24},{1,5},{5... | collective-permute-start | bytes 294920 | tf_op jit(solution)/shard_map/ppermute | solution.py:17
  83.4 6.1 %collective-permute-start.28 = (f16[128,384]{1,0:T(8,128)(2,1)S(1)}, f16[128,384]{1,0:T(8,128)(2,1)S(1)}, u32[]{:S(2)}, u32[]{:S(2)}) collective-permute-start(f16[128,384]{1,0:T(8,128)(2,1)S(1)} %collective-permute-done.21), channel_id=1, source_target_pairs={{0,4},{4,0},{8,12},{12,8},{16,20},{20,16},{24,28},{28,24},{1,5},{5... | collective-permute-start | bytes 294920 | tf_op jit(solution)/shard_map/ppermute | solution.py:17
  86.3 6.0 %collective-permute-start.16 = (f16[128,384]{1,0:T(8,128)(2,1)S(1)}, f16[128,384]{1,0:T(8,128)(2,1)S(1)}, u32[]{:S(2)}, u32[]{:S(2)}) collective-permute-start(f16[128,384]{1,0:T(8,128)(2,1)S(1)} %collective-permute-done.15), channel_id=1, source_target_pairs={{0,4},{4,0},{8,12},{12,8},{16,20},{20,16},{24,28},{28,24},{1,5},{5... | collective-permute-start | bytes 294920 | tf_op jit(solution)/shard_map/ppermute | solution.py:17
  (11 other events, 93.2 us)

commit v5 on v4

--- a/solution.py
+++ b/solution.py
@@ -107,7 +107,7 @@
 
 def scatter(rows, slots, before, nodes, node_dev, weight):
     images = rows[0].data.shape[1]
-    tile = 2 * node_dev
+    tile = 4 * node_dev
     depth = sum(part.count for part in rows)
 
     def body(*refs):
@@ -126,7 +126,7 @@
         out_specs=part,
         out_shape=jax.ShapeDtypeStruct((nodes, images), jnp.float32),
         scratch_shapes=[pltpu.VMEM((depth, 2 * images), jnp.bfloat16)],
-        compiler_params=pltpu.CompilerParams(vmem_limit_bytes=(8 + 2 * -(-depth // slots)) * MIB),
+        compiler_params=pltpu.CompilerParams(vmem_limit_bytes=(14 + 2 * -(-depth // slots)) * MIB),
         cost_estimate=cost(4 * depth * nodes * images, 8 * nodes * images, weight),
         name="scatter_traces",
     )(*row_args(rows), *more)
@@ -139,7 +139,7 @@
 
 def scatter_and_layer(place, rows, slots, before, matrix, jobs, parts, nodes, node_dev, weight):
     images = rows[0].data.shape[1]
-    tile = 2 * node_dev
+    tile = 4 * node_dev
     steps = nodes // tile
     depth = sum(part.count for part in rows)
     count = len(jobs)
@@ -165,10 +165,10 @@
 
         total = scatter_tile(rows, refs[: 2 * len(rows)], both, step * tile, tile, slots, nodes, node_dev)
         total = (total + before_ref[...]) * (1.0 / TRACE_SCALE)
-        for half in range(2):
-            @pl.when(2 * step + half == place_ref[0])
+        for slab in range(tile // node_dev):
+            @pl.when(tile // node_dev * step + slab == place_ref[0])
             def _():
-                own[...] = total[half * node_dev : (half + 1) * node_dev, :]
+                own[...] = total[slab * node_dev : (slab + 1) * node_dev, :]
 
         rounded[pl.ds(pl.multiple_of(step * tile, tile), tile), :] = total.astype(jnp.bfloat16)
 
@@ -180,7 +180,7 @@
                 outs[n][...] = layer.astype(outs[n].dtype)
 
     one = pl.BlockSpec((height, images), lambda s, p: (0, 0))
-    limit = 10 + 2 * -(-depth // slots) + (2 * count * height * nodes + 4 * nodes * images) // MIB
+    limit = 16 + 2 * -(-depth // slots) + (2 * count * height * nodes + 4 * nodes * images) // MIB
     return pl.pallas_call(
         body,
         grid_spec=pltpu.PrefetchScalarGridSpec(

time: 94.5 us -> 93.9 us (level)
  starting transfers between devices: 35.4 us -> 38.5 us
  waiting for transfers between devices: 22.6 us -> 20.6 us
  Pallas kernels: 27.7 us -> 26.1 us
    ppermute x29, starting transfers between devices: 35.4 us -> 38.5 us  [exchange(): return lax.ppermute(block, axis, [(i, i ^ offset) for i in range(count)])]
    ppermute x29, waiting for transfers between devices: 22.6 us -> 20.6 us  [exchange(): return lax.ppermute(block, axis, [(i, i ^ offset) for i in range(count)])]
    pallas_call x3, Pallas kernels: 15.4 us -> 14.2 us  [scatter(): pl.pallas_call(body, grid=(nodes // tile,), in_specs=row_specs(rows) + [p...]
  transfers between devices with their start and end apart: 29 -> 29, of which waited for: 7 -> 7; matrix products, arithmetic and copies ran while one was open for 2% -> 2% of each run, Pallas kernels for 23% -> 22%
where the time goes in v5:
time: 93.9 us; the launch traced here: 93.6 us
  starting transfers between devices  38.5 us (41%)
  Pallas kernels  26.1 us (28%)
  waiting for transfers between devices  20.6 us (22%)
  local copies, waits for them, and re-layouts  3.88 us (4%)
  other arithmetic  3.59 us (4%)
  between operations  1.02 us (1%)
    ppermute x29, starting transfers between devices, exchange(): return lax.ppermute(block, axis, [(i, i ^ offset) for i in range(count)])  38.5 us
    ppermute x29, waiting for transfers between devices, exchange(): return lax.ppermute(block, axis, [(i, i ^ offset) for i in range(count)])  20.6 us
    pallas_call x3, Pallas kernels, scatter(): pl.pallas_call(body, grid=(nodes // tile,), in_specs=row_specs(rows) + [p...  14.2 us
    pallas_call x3, Pallas kernels, read_back(): pl.pallas_call(body, in_specs=[pl.BlockSpec(memory_space=pltpu.SMEM)] + [...  5.5 us
    unnamed x12, local copies, waits for them, and re-layouts  3.53 us
    pallas_call x1, Pallas kernels, scatter_and_layer(): pl.pallas_call(body, grid_spec=pltpu.PrefetchScalarGridSpec(num_scalar_pr...  3.27 us
    pallas_call x2, Pallas kernels, layer_more(): pl.pallas_call(body, grid_spec=pltpu.PrefetchScalarGridSpec(num_scalar_pr...  3.05 us
  transfers between devices with their start and end apart: 29, of which 7 were waited for; matrix products, arithmetic and copies ran while one was open for 2% of the time, Pallas kernels for 22%

profile of v5, /device:TPU:0, one launch (start us, length us, event | category | flops | bytes accessed | tf_op | source)
XLA Modules:
  0.0 93.6 jit_solution(13142836030590088753)
XLA Ops:
  2.6 3.1 %collective-permute-start.2 = (f16[520,384]{1,0:T(8,128)(2,1)S(1)}, f16[520,384]{1,0:T(8,128)(2,1)S(1)}, u32[]{:S(2)}, u32[]{:S(2)}) collective-permute-start(f16[520,384]{1,0:T(8,128)(2,1)S(1)} %get-tuple-element.77), channel_id=1, source_target_pairs={{0,8},{4,12},{8,0},{12,4},{16,24},{20,28},{24,16},{28,20},{1,9},{5... | collective-permute-start | bytes 1198088 | tf_op jit(solution)/shard_map/ppermute | solution.py:17
  7.3 2.6 %collective-permute-start = (f16[520,384]{1,0:T(8,128)(2,1)S(1)}, f16[520,384]{1,0:T(8,128)(2,1)S(1)}, u32[]{:S(2)}, u32[]{:S(2)}) collective-permute-start(f16[520,384]{1,0:T(8,128)(2,1)S(1)} %get-tuple-element.77), channel_id=1, source_target_pairs={{0,16},{4,20},{8,24},{12,28},{16,0},{20,4},{24,8},{28,12},{1,17},{... | collective-permute-start | bytes 1198088 | tf_op jit(solution)/shard_map/ppermute | solution.py:17
  10.2 11.8 %collective-permute-done.2 = f16[520,384]{1,0:T(8,128)(2,1)S(1)} collective-permute-done((f16[520,384]{1,0:T(8,128)(2,1)S(1)}, f16[520,384]{1,0:T(8,128)(2,1)S(1)}, u32[]{:S(2)}, u32[]{:S(2)}) %collective-permute-start.2) | collective-permute-done | bytes 399392 | tf_op jit(solution)/shard_map/ppermute | solution.py:17
  22.1 2.3 %collective-permute-start.7 = (f16[520,384]{1,0:T(8,128)(2,1)S(1)}, f16[520,384]{1,0:T(8,128)(2,1)S(1)}, u32[]{:S(2)}, u32[]{:S(2)}) collective-permute-start(f16[520,384]{1,0:T(8,128)(2,1)S(1)} %collective-permute-done.2), channel_id=1, source_target_pairs={{0,4},{4,0},{8,12},{12,8},{16,20},{20,16},{24,28},{28,24},{1,5},{5... | collective-permute-start | bytes 1198088 | tf_op jit(solution)/shard_map/ppermute | solution.py:17
  24.4 5.6 %scatter_traces.3.refs_6_ = f32[2048,384]{1,0:T(8,128)S(1)} custom-call(f32[520,384]{1,0:T(8,128)S(1)} %get-tuple-element.76.refs_0_.refs_1_, f32[520,384]{1,0:T(8,128)S(1)} %get-tuple-element.76.refs_0_.refs_1_, f32[520,384]{1,0:T(8,128)S(1)} %convert_element_type.123.refs_2_.refs_3_, f32[520,384]{1,0:T(8,128)S(1)} %convert_element_type.123.refs_2_.refs_3_, ...), custom_call_target="tpu_custom_call" | custom-call | flops 4831838208 | bytes 6291457 | tf_op jit(solution)/shard_map/scatter_traces/pallas_call | solution.py:122
  30.0 1.6 %copy-done.1 = f32[2048,384]{1,0:T(8,128)} copy-done((f32[2048,384]{1,0:T(8,128)}, f32[2048,384]{1,0:T(8,128)S(1)}, u32[]{:S(2)}) %copy-start.1) | copy-done | bytes 3145752
  31.6 1.6 %collective-permute-done = f16[520,384]{1,0:T(8,128)(2,1)S(1)} collective-permute-done((f16[520,384]{1,0:T(8,128)(2,1)S(1)}, f16[520,384]{1,0:T(8,128)(2,1)S(1)}, u32[]{:S(2)}, u32[]{:S(2)}) %collective-permute-start) | collective-permute-done | bytes 399392 | tf_op jit(solution)/shard_map/ppermute | solution.py:17
  34.0 1.6 %collective-permute-start.6 = (f16[264,384]{1,0:T(8,128)(2,1)S(1)}, f16[264,384]{1,0:T(8,128)(2,1)S(1)}, u32[]{:S(2)}, u32[]{:S(2)}) collective-permute-start(f16[264,384]{1,0:T(8,128)(2,1)S(1)} %collective-permute-done.5), channel_id=1, source_target_pairs={{0,4},{4,0},{8,12},{12,8},{16,20},{20,16},{24,28},{28,24},{1,5},{5... | collective-permute-start | bytes 608264 | tf_op jit(solution)/shard_map/ppermute | solution.py:17
  35.7 2.5 %collective-permute-start.4 = (f16[256,384]{1,0:T(8,128)(2,1)S(1)}, f16[256,384]{1,0:T(8,128)(2,1)S(1)}, u32[]{:S(2)}, u32[]{:S(2)}) collective-permute-start(f16[256,384]{1,0:T(8,128)(2,1)S(1)} %slice.18), channel_id=1, source_target_pairs={{0,24},{4,28},{8,16},{12,20},{16,8},{20,12},{24,0},{28,4},{1,25},{... | collective-permute-start | bytes 589832 | tf_op jit(solution)/shard_map/ppermute | solution.py:17
  38.3 1.9 %copy-done.2 = f32[2048,384]{1,0:T(8,128)S(1)} copy-done((f32[2048,384]{1,0:T(8,128)S(1)}, f32[2048,384]{1,0:T(8,128)}, u32[]{:S(2)}) %copy-start.2) | copy-done | bytes 3145752
  40.2 4.7 %scatter_traces.4.refs_6_ = f32[2048,384]{1,0:T(8,128)S(1)} custom-call(f32[520,384]{1,0:T(8,128)S(1)} %convert_element_type.125.refs_0_.refs_1_, f32[520,384]{1,0:T(8,128)S(1)} %convert_element_type.125.refs_0_.refs_1_, f32[520,384]{1,0:T(8,128)S(1)} %convert_element_type.126.refs_2_.refs_3_, f32[520,384]{1,0:T(8,128)S(1)} %convert_element_type.126.refs_2_.refs_3_, ...), custom_call_target="tpu_custom_call" | custom-call | flops 4026531840 | bytes 6291457 | tf_op jit(solution)/shard_map/scatter_traces/pallas_call | solution.py:122
  47.6 3.9 %scatter_traces.5.refs_2_ = f32[2048,384]{1,0:T(8,128)S(1)} custom-call(f32[520,384]{1,0:T(8,128)S(1)} %convert_element_type.128.refs_0_.refs_1_, f32[520,384]{1,0:T(8,128)S(1)} %convert_element_type.128.refs_0_.refs_1_, f32[256,384]{1,0:T(8,128)S(1)} %convert_element_type.129.refs_2_, f32[264,384]{1,0:T(8,128)S(1)} %convert_element_type.127.refs_4_.refs_5_.refs_3_, ...), custom_call_target="tpu_custom_call" | custom-call | flops 3221225472 | bytes 6291457 | tf_op jit(solution)/shard_map/scatter_traces/pallas_call | solution.py:122
  51.9 3.3 %scatter_and_layer.1 = (bf16[2048,384]{1,0:T(8,128)(2,1)S(1)}, f32[256,384]{1,0:T(8,128)S(1)}, bf16[128,384]{1,0:T(8,128)(2,1)S(1)}, bf16[128,384]{1,0:T(8,128)(2,1)S(1)}) custom-call(s32[2]{0:T(128)S(1)} %pad_add_fusion.place_ref, f32[256,384]{1,0:T(8,128)S(1)} %convert_element_type.131.refs_0_, ...), custom_call_target="tpu_custom_call" | custom-call | flops 1207959552 | bytes 6291457 | tf_op jit(solution)/shard_map/scatter_and_layer/pallas_call | solution.py:184
  56.7 1.8 %layer_more.2 = (f32[128,384]{1,0:T(8,128)S(1)}, bf16[128,384]{1,0:T(8,128)(2,1)S(1)}, bf16[128,384]{1,0:T(8,128)(2,1)S(1)}, bf16[128,384]{1,0:T(8,128)(2,1)S(1)}) custom-call(s32[2]{0:T(128)S(1)} %pad_add_fusion.place_ref, bf16[2048,384]{1,0:T(8,128)(2,1)S(1)} %get-tuple-element.47.rounded_ref, f32[256,384]{1,0:T(8,128)S(1)} %get-tuple-element.48.own_ref, ...), custom_call_target="tpu_custom_call" | custom-call | flops 805306368 | bytes 1572865 | tf_op jit(solution)/shard_map/layer_more/pallas_call | solution.py:232
  60.6 1.6 %collective-permute-start.13 = (bf16[128,384]{1,0:T(8,128)(2,1)S(1)}, bf16[128,384]{1,0:T(8,128)(2,1)S(1)}, u32[]{:S(2)}, u32[]{:S(2)}) collective-permute-start(bf16[128,384]{1,0:T(8,128)(2,1)S(1)} %get-tuple-element.60), channel_id=1, source_target_pairs={{0,3},{1,2},{2,1},{3,0},{4,7},{5,6},{6,5},{7,4},{8,11},{9,10},{10,... | collective-permute-start | bytes 294920 | tf_op jit(solution)/shard_map/ppermute | solution.py:17
  62.9 3.2 %collective-permute-start.20 = (f16[128,384]{1,0:T(8,128)(2,1)S(1)}, f16[128,384]{1,0:T(8,128)(2,1)S(1)}, u32[]{:S(2)}, u32[]{:S(2)}) collective-permute-start(f16[128,384]{1,0:T(8,128)(2,1)S(1)} %get-tuple-element.74), channel_id=1, source_target_pairs={{0,16},{4,20},{8,24},{12,28},{16,0},{20,4},{24,8},{28,12},{1,17},{... | collective-permute-start | bytes 294920 | tf_op jit(solution)/shard_map/ppermute | solution.py:17
  69.5 4.6 %collective-permute-done.20 = f16[128,384]{1,0:T(8,128)(2,1)S(1)} collective-permute-done((f16[128,384]{1,0:T(8,128)(2,1)S(1)}, f16[128,384]{1,0:T(8,128)(2,1)S(1)}, u32[]{:S(2)}, u32[]{:S(2)}) %collective-permute-start.20) | collective-permute-done | bytes 98336 | tf_op jit(solution)/shard_map/ppermute | solution.py:17
  74.0 2.6 %collective-permute-start.17 = (f16[128,384]{1,0:T(8,128)(2,1)S(1)}, f16[128,384]{1,0:T(8,128)(2,1)S(1)}, u32[]{:S(2)}, u32[]{:S(2)}) collective-permute-start(f16[128,384]{1,0:T(8,128)(2,1)S(1)} %get-tuple-element.71), channel_id=1, source_target_pairs={{0,24},{4,28},{8,16},{12,20},{16,8},{20,12},{24,0},{28,4},{1,25},{... | collective-permute-start | bytes 294920 | tf_op jit(solution)/shard_map/ppermute | solution.py:17
  76.7 3.4 %collective-permute-start.22 = (f16[128,384]{1,0:T(8,128)(2,1)S(1)}, f16[128,384]{1,0:T(8,128)(2,1)S(1)}, u32[]{:S(2)}, u32[]{:S(2)}) collective-permute-start(f16[128,384]{1,0:T(8,128)(2,1)S(1)} %collective-permute-done.19), channel_id=1, source_target_pairs={{0,4},{4,0},{8,12},{12,8},{16,20},{20,16},{24,28},{28,24},{1,5},{5... | collective-permute-start | bytes 294920 | tf_op jit(solution)/shard_map/ppermute | solution.py:17
  80.2 1.9 %collective-permute-start.27 = (f16[128,384]{1,0:T(8,128)(2,1)S(1)}, f16[128,384]{1,0:T(8,128)(2,1)S(1)}, u32[]{:S(2)}, u32[]{:S(2)}) collective-permute-start(f16[128,384]{1,0:T(8,128)(2,1)S(1)} %collective-permute-done.20), channel_id=1, source_target_pairs={{0,4},{4,0},{8,12},{12,8},{16,20},{20,16},{24,28},{28,24},{1,5},{5... | collective-permute-start | bytes 294920 | tf_op jit(solution)/shard_map/ppermute | solution.py:17
  84.1 1.6 %read_back.3.refs_8_ = f32[512,384]{1,0:T(8,128)S(1)} custom-call(s32[2]{0:T(128)S(1)} %pad_add_fusion.place_ref, s32[512,1]{1,0:T(8,128)S(1)} %copy.11.ids_ref, f32[128,384]{1,0:T(8,128)S(1)} %get-tuple-element.73.refs_0_, f32[128,384]{1,0:T(8,128)S(1)} %convert_element_type.149.refs_1_, f32[128,384]{1,0:T(8,128)S(1)} %convert_element_type.150.refs_2_, ...), custom_call_target="tpu_custom_call" | custom-call | flops 1 | bytes 1 | tf_op jit(solution)/shard_map/read_back/pallas_call | solution.py:273
  86.4 1.6 %collective-permute-start.18 = (f16[128,384]{1,0:T(8,128)(2,1)S(1)}, f16[128,384]{1,0:T(8,128)(2,1)S(1)}, u32[]{:S(2)}, u32[]{:S(2)}) collective-permute-start(f16[128,384]{1,0:T(8,128)(2,1)S(1)} %collective-permute-done.17), channel_id=1, source_target_pairs={{0,4},{4,0},{8,12},{12,8},{16,20},{20,16},{24,28},{28,24},{1,5},{5... | collective-permute-start | bytes 294920 | tf_op jit(solution)/shard_map/ppermute | solution.py:17
  89.7 1.9 %read_back.4.refs_2_ = f32[512,384]{1,0:T(8,128)S(1)} custom-call(s32[2]{0:T(128)S(1)} %pad_add_fusion.place_ref, s32[512,1]{1,0:T(8,128)S(1)} %copy.11.ids_ref, f32[128,384]{1,0:T(8,128)S(1)} %convert_element_type.140.refs_0_, f32[128,384]{1,0:T(8,128)S(1)} %convert_element_type.141.refs_1_, f32[128,384]{1,0:T(8,128)S(1)} %convert_element_type.142.refs_2_, ...), custom_call_target="tpu_custom_call" | custom-call | flops 1 | bytes 1 | tf_op jit(solution)/shard_map/read_back/pallas_call | solution.py:273
  91.7 1.9 %read_back.5 = f32[512,384]{1,0:T(8,128)} custom-call(s32[2]{0:T(128)S(1)} %pad_add_fusion.place_ref, s32[512,1]{1,0:T(8,128)S(1)} %copy.11.ids_ref, f32[128,384]{1,0:T(8,128)S(1)} %convert_element_type.154.refs_0_, f32[128,384]{1,0:T(8,128)S(1)} %convert_element_type.155.refs_1_, f32[512,384]{1,0:T(8,128)S(1)} %read_back.4.refs_2_), custom_call_target="tpu_custom_call" | custom-call | flops 201326592 | bytes 1572865 | tf_op jit(solution)/shard_map/read_back/pallas_call | solution.py:273
  (93 shorter events, 19.8 us)
Async XLA Ops:
  2.6 19.4 %collective-permute-start.2 = (f16[520,384]{1,0:T(8,128)(2,1)S(1)}, f16[520,384]{1,0:T(8,128)(2,1)S(1)}, u32[]{:S(2)}, u32[]{:S(2)}) collective-permute-start(f16[520,384]{1,0:T(8,128)(2,1)S(1)} %get-tuple-element.77), channel_id=1, source_target_pairs={{0,8},{4,12},{8,0},{12,4},{16,24},{20,28},{24,16},{28,20},{1,9},{5... | collective-permute-start | bytes 1198088 | tf_op jit(solution)/shard_map/ppermute | solution.py:17
  5.7 18.6 %collective-permute-start.1 = (f16[520,384]{1,0:T(8,128)(2,1)S(1)}, f16[520,384]{1,0:T(8,128)(2,1)S(1)}, u32[]{:S(2)}, u32[]{:S(2)}) collective-permute-start(f16[520,384]{1,0:T(8,128)(2,1)S(1)} %get-tuple-element.77), channel_id=1, source_target_pairs={{0,4},{4,0},{8,12},{12,8},{16,20},{20,16},{24,28},{28,24},{1,5},{5... | collective-permute-start | bytes 1198088 | tf_op jit(solution)/shard_map/ppermute | solution.py:17
  7.3 26.0 %collective-permute-start = (f16[520,384]{1,0:T(8,128)(2,1)S(1)}, f16[520,384]{1,0:T(8,128)(2,1)S(1)}, u32[]{:S(2)}, u32[]{:S(2)}) collective-permute-start(f16[520,384]{1,0:T(8,128)(2,1)S(1)} %get-tuple-element.77), channel_id=1, source_target_pairs={{0,16},{4,20},{8,24},{12,28},{16,0},{20,4},{24,8},{28,12},{1,17},{... | collective-permute-start | bytes 1198088 | tf_op jit(solution)/shard_map/ppermute | solution.py:17
  9.9 24.1 %collective-permute-start.5 = (f16[264,384]{1,0:T(8,128)(2,1)S(1)}, f16[264,384]{1,0:T(8,128)(2,1)S(1)}, u32[]{:S(2)}, u32[]{:S(2)}) collective-permute-start(f16[264,384]{1,0:T(8,128)(2,1)S(1)} %slice.19), channel_id=1, source_target_pairs={{0,24},{4,28},{8,16},{12,20},{16,8},{20,12},{24,0},{28,4},{1,25},{... | collective-permute-start | bytes 608264 | tf_op jit(solution)/shard_map/ppermute | solution.py:17
  22.1 16.2 %collective-permute-start.7 = (f16[520,384]{1,0:T(8,128)(2,1)S(1)}, f16[520,384]{1,0:T(8,128)(2,1)S(1)}, u32[]{:S(2)}, u32[]{:S(2)}) collective-permute-start(f16[520,384]{1,0:T(8,128)(2,1)S(1)} %collective-permute-done.2), channel_id=1, source_target_pairs={{0,4},{4,0},{8,12},{12,8},{16,20},{20,16},{24,28},{28,24},{1,5},{5... | collective-permute-start | bytes 1198088 | tf_op jit(solution)/shard_map/ppermute | solution.py:17
  33.2 12.9 %collective-permute-start.3 = (f16[520,384]{1,0:T(8,128)(2,1)S(1)}, f16[520,384]{1,0:T(8,128)(2,1)S(1)}, u32[]{:S(2)}, u32[]{:S(2)}) collective-permute-start(f16[520,384]{1,0:T(8,128)(2,1)S(1)} %collective-permute-done), channel_id=1, source_target_pairs={{0,4},{4,0},{8,12},{12,8},{16,20},{20,16},{24,28},{28,24},{1,5},{5... | collective-permute-start | bytes 1198088 | tf_op jit(solution)/shard_map/ppermute | solution.py:17
  34.0 12.2 %collective-permute-start.6 = (f16[264,384]{1,0:T(8,128)(2,1)S(1)}, f16[264,384]{1,0:T(8,128)(2,1)S(1)}, u32[]{:S(2)}, u32[]{:S(2)}) collective-permute-start(f16[264,384]{1,0:T(8,128)(2,1)S(1)} %collective-permute-done.5), channel_id=1, source_target_pairs={{0,4},{4,0},{8,12},{12,8},{16,20},{20,16},{24,28},{28,24},{1,5},{5... | collective-permute-start | bytes 608264 | tf_op jit(solution)/shard_map/ppermute | solution.py:17
  35.7 10.5 %collective-permute-start.4 = (f16[256,384]{1,0:T(8,128)(2,1)S(1)}, f16[256,384]{1,0:T(8,128)(2,1)S(1)}, u32[]{:S(2)}, u32[]{:S(2)}) collective-permute-start(f16[256,384]{1,0:T(8,128)(2,1)S(1)} %slice.18), channel_id=1, source_target_pairs={{0,24},{4,28},{8,16},{12,20},{16,8},{20,12},{24,0},{28,4},{1,25},{... | collective-permute-start | bytes 589832 | tf_op jit(solution)/shard_map/ppermute | solution.py:17
  55.2 7.0 %collective-permute-start.9 = (bf16[128,384]{1,0:T(8,128)(2,1)S(1)}, bf16[128,384]{1,0:T(8,128)(2,1)S(1)}, u32[]{:S(2)}, u32[]{:S(2)}) collective-permute-start(bf16[128,384]{1,0:T(8,128)(2,1)S(1)} %get-tuple-element.45), channel_id=1, source_target_pairs={{0,2},{1,3},{2,0},{3,1},{4,6},{5,7},{6,4},{7,5},{8,10},{9,11},{10,... | collective-permute-start | bytes 294920 | tf_op jit(solution)/shard_map/ppermute | solution.py:17
  56.7 6.0 %collective-permute-start.10 = (bf16[128,384]{1,0:T(8,128)(2,1)S(1)}, bf16[128,384]{1,0:T(8,128)(2,1)S(1)}, u32[]{:S(2)}, u32[]{:S(2)}) collective-permute-start(bf16[128,384]{1,0:T(8,128)(2,1)S(1)} %get-tuple-element.46), channel_id=1, source_target_pairs={{0,3},{1,2},{2,1},{3,0},{4,7},{5,6},{6,5},{7,4},{8,11},{9,10},{10,... | collective-permute-start | bytes 294920 | tf_op jit(solution)/shard_map/ppermute | solution.py:17
  60.6 6.7 %collective-permute-start.13 = (bf16[128,384]{1,0:T(8,128)(2,1)S(1)}, bf16[128,384]{1,0:T(8,128)(2,1)S(1)}, u32[]{:S(2)}, u32[]{:S(2)}) collective-permute-start(bf16[128,384]{1,0:T(8,128)(2,1)S(1)} %get-tuple-element.60), channel_id=1, source_target_pairs={{0,3},{1,2},{2,1},{3,0},{4,7},{5,6},{6,5},{7,4},{8,11},{9,10},{10,... | collective-permute-start | bytes 294920 | tf_op jit(solution)/shard_map/ppermute | solution.py:17
  62.2 6.4 %collective-permute-start.12 = (bf16[128,384]{1,0:T(8,128)(2,1)S(1)}, bf16[128,384]{1,0:T(8,128)(2,1)S(1)}, u32[]{:S(2)}, u32[]{:S(2)}) collective-permute-start(bf16[128,384]{1,0:T(8,128)(2,1)S(1)} %get-tuple-element.59), channel_id=1, source_target_pairs={{0,2},{1,3},{2,0},{3,1},{4,6},{5,7},{6,4},{7,5},{8,10},{9,11},{10,... | collective-permute-start | bytes 294920 | tf_op jit(solution)/shard_map/ppermute | solution.py:17
  62.8 6.6 %collective-permute-start.19 = (f16[128,384]{1,0:T(8,128)(2,1)S(1)}, f16[128,384]{1,0:T(8,128)(2,1)S(1)}, u32[]{:S(2)}, u32[]{:S(2)}) collective-permute-start(f16[128,384]{1,0:T(8,128)(2,1)S(1)} %get-tuple-element.74), channel_id=1, source_target_pairs={{0,8},{4,12},{8,0},{12,4},{16,24},{20,28},{24,16},{28,20},{1,9},{5... | collective-permute-start | bytes 294920 | tf_op jit(solution)/shard_map/ppermute | solution.py:17
  62.9 11.1 %collective-permute-start.20 = (f16[128,384]{1,0:T(8,128)(2,1)S(1)}, f16[128,384]{1,0:T(8,128)(2,1)S(1)}, u32[]{:S(2)}, u32[]{:S(2)}) collective-permute-start(f16[128,384]{1,0:T(8,128)(2,1)S(1)} %get-tuple-element.74), channel_id=1, source_target_pairs={{0,16},{4,20},{8,24},{12,28},{16,0},{20,4},{24,8},{28,12},{1,17},{... | collective-permute-start | bytes 294920 | tf_op jit(solution)/shard_map/ppermute | solution.py:17
  66.1 7.9 %collective-permute-start.21 = (f16[128,384]{1,0:T(8,128)(2,1)S(1)}, f16[128,384]{1,0:T(8,128)(2,1)S(1)}, u32[]{:S(2)}, u32[]{:S(2)}) collective-permute-start(f16[128,384]{1,0:T(8,128)(2,1)S(1)} %get-tuple-element.74), channel_id=1, source_target_pairs={{0,24},{4,28},{8,16},{12,20},{16,8},{20,12},{24,0},{28,4},{1,25},{... | collective-permute-start | bytes 294920 | tf_op jit(solution)/shard_map/ppermute | solution.py:17
  67.3 9.4 %collective-permute-start.23 = (f16[128,384]{1,0:T(8,128)(2,1)S(1)}, f16[128,384]{1,0:T(8,128)(2,1)S(1)}, u32[]{:S(2)}, u32[]{:S(2)}) collective-permute-start(f16[128,384]{1,0:T(8,128)(2,1)S(1)} %get-tuple-element.74), channel_id=1, source_target_pairs={{0,4},{4,0},{8,12},{12,8},{16,20},{20,16},{24,28},{28,24},{1,5},{5... | collective-permute-start | bytes 294920 | tf_op jit(solution)/shard_map/ppermute | solution.py:17
  68.7 11.4 %collective-permute-start.24 = (f16[128,384]{1,0:T(8,128)(2,1)S(1)}, f16[128,384]{1,0:T(8,128)(2,1)S(1)}, u32[]{:S(2)}, u32[]{:S(2)}) collective-permute-start(f16[128,384]{1,0:T(8,128)(2,1)S(1)} %get-tuple-element.71), channel_id=1, source_target_pairs={{0,4},{4,0},{8,12},{12,8},{16,20},{20,16},{24,28},{28,24},{1,5},{5... | collective-permute-start | bytes 294920 | tf_op jit(solution)/shard_map/ppermute | solution.py:17
  69.5 10.6 %collective-permute-start.25 = (f16[128,384]{1,0:T(8,128)(2,1)S(1)}, f16[128,384]{1,0:T(8,128)(2,1)S(1)}, u32[]{:S(2)}, u32[]{:S(2)}) collective-permute-start(f16[128,384]{1,0:T(8,128)(2,1)S(1)} %get-tuple-element.71), channel_id=1, source_target_pairs={{0,8},{4,12},{8,0},{12,4},{16,24},{20,28},{24,16},{28,20},{1,9},{5... | collective-permute-start | bytes 294920 | tf_op jit(solution)/shard_map/ppermute | solution.py:17
  74.0 8.2 %collective-permute-start.15 = (f16[128,384]{1,0:T(8,128)(2,1)S(1)}, f16[128,384]{1,0:T(8,128)(2,1)S(1)}, u32[]{:S(2)}, u32[]{:S(2)}) collective-permute-start(f16[128,384]{1,0:T(8,128)(2,1)S(1)} %get-tuple-element.71), channel_id=1, source_target_pairs={{0,16},{4,20},{8,24},{12,28},{16,0},{20,4},{24,8},{28,12},{1,17},{... | collective-permute-start | bytes 294920 | tf_op jit(solution)/shard_map/ppermute | solution.py:17
  74.0 11.8 %collective-permute-start.17 = (f16[128,384]{1,0:T(8,128)(2,1)S(1)}, f16[128,384]{1,0:T(8,128)(2,1)S(1)}, u32[]{:S(2)}, u32[]{:S(2)}) collective-permute-start(f16[128,384]{1,0:T(8,128)(2,1)S(1)} %get-tuple-element.71), channel_id=1, source_target_pairs={{0,24},{4,28},{8,16},{12,20},{16,8},{20,12},{24,0},{28,4},{1,25},{... | collective-permute-start | bytes 294920 | tf_op jit(solution)/shard_map/ppermute | solution.py:17
  76.7 9.7 %collective-permute-start.22 = (f16[128,384]{1,0:T(8,128)(2,1)S(1)}, f16[128,384]{1,0:T(8,128)(2,1)S(1)}, u32[]{:S(2)}, u32[]{:S(2)}) collective-permute-start(f16[128,384]{1,0:T(8,128)(2,1)S(1)} %collective-permute-done.19), channel_id=1, source_target_pairs={{0,4},{4,0},{8,12},{12,8},{16,20},{20,16},{24,28},{28,24},{1,5},{5... | collective-permute-start | bytes 294920 | tf_op jit(solution)/shard_map/ppermute | solution.py:17
  80.1 7.9 %collective-permute-start.26 = (f16[128,384]{1,0:T(8,128)(2,1)S(1)}, f16[128,384]{1,0:T(8,128)(2,1)S(1)}, u32[]{:S(2)}, u32[]{:S(2)}) collective-permute-start(f16[128,384]{1,0:T(8,128)(2,1)S(1)} %collective-permute-done.25), channel_id=1, source_target_pairs={{0,4},{4,0},{8,12},{12,8},{16,20},{20,16},{24,28},{28,24},{1,5},{5... | collective-permute-start | bytes 294920 | tf_op jit(solution)/shard_map/ppermute | solution.py:17
  80.2 7.9 %collective-permute-start.27 = (f16[128,384]{1,0:T(8,128)(2,1)S(1)}, f16[128,384]{1,0:T(8,128)(2,1)S(1)}, u32[]{:S(2)}, u32[]{:S(2)}) collective-permute-start(f16[128,384]{1,0:T(8,128)(2,1)S(1)} %collective-permute-done.20), channel_id=1, source_target_pairs={{0,4},{4,0},{8,12},{12,8},{16,20},{20,16},{24,28},{28,24},{1,5},{5... | collective-permute-start | bytes 294920 | tf_op jit(solution)/shard_map/ppermute | solution.py:17
  82.3 6.6 %collective-permute-start.28 = (f16[128,384]{1,0:T(8,128)(2,1)S(1)}, f16[128,384]{1,0:T(8,128)(2,1)S(1)}, u32[]{:S(2)}, u32[]{:S(2)}) collective-permute-start(f16[128,384]{1,0:T(8,128)(2,1)S(1)} %collective-permute-done.21), channel_id=1, source_target_pairs={{0,4},{4,0},{8,12},{12,8},{16,20},{20,16},{24,28},{28,24},{1,5},{5... | collective-permute-start | bytes 294920 | tf_op jit(solution)/shard_map/ppermute | solution.py:17
  (11 other events, 94.5 us)

commit v6 on v5

--- a/solution.py
+++ b/solution.py
@@ -256,12 +256,12 @@
 
     def body(place_ref, ids_ref, *refs):
         out, both = refs[-2:]
-        lane = lax.broadcasted_iota(jnp.int32, (slots, height), 1)
+        place_in = ids_ref[...] - lax.broadcasted_iota(jnp.int32, (slots, height), 1)
         picks = []
         for row, (key, part) in enumerate(keys):
             store_halves(refs[row][...], both, row * height)
-            node = (place_ref[0] ^ key) * node_dev + part * height + lane
-            picks.append(jnp.where(ids_ref[...] == node, 1.0, 0.0).astype(jnp.bfloat16))
+            first = (place_ref[0] ^ key) * node_dev + part * height
+            picks.append(jnp.where(place_in == first, 1.0, 0.0).astype(jnp.bfloat16))
         total = jnp.dot(jnp.concatenate(picks, axis=1), both[...], preferred_element_type=jnp.float32)
         total = (total[:, :images] + total[:, images:]) * (1.0 / RESULT_SCALE)
         if before is not None:

time: 93.9 us -> 93.5 us (level)
  no operation moved by 1% of the time
where the time goes in v6:
time: 93.5 us; the launch traced here: 93.3 us
  starting transfers between devices  38.5 us (41%)
  Pallas kernels  25.5 us (27%)
  waiting for transfers between devices  20.8 us (22%)
  local copies, waits for them, and re-layouts  3.88 us (4%)
  other arithmetic  3.59 us (4%)
  between operations  1.01 us (1%)
    ppermute x29, starting transfers between devices, exchange(): return lax.ppermute(block, axis, [(i, i ^ offset) for i in range(count)])  38.5 us
    ppermute x29, waiting for transfers between devices, exchange(): return lax.ppermute(block, axis, [(i, i ^ offset) for i in range(count)])  20.8 us
    pallas_call x3, Pallas kernels, scatter(): pl.pallas_call(body, grid=(nodes // tile,), in_specs=row_specs(rows) + [p...  14.2 us
    pallas_call x3, Pallas kernels, read_back(): pl.pallas_call(body, in_specs=[pl.BlockSpec(memory_space=pltpu.SMEM)] + [...  4.97 us
    unnamed x12, local copies, waits for them, and re-layouts  3.53 us
    pallas_call x1, Pallas kernels, scatter_and_layer(): pl.pallas_call(body, grid_spec=pltpu.PrefetchScalarGridSpec(num_scalar_pr...  3.27 us
    pallas_call x2, Pallas kernels, layer_more(): pl.pallas_call(body, grid_spec=pltpu.PrefetchScalarGridSpec(num_scalar_pr...  3.05 us
  transfers between devices with their start and end apart: 29, of which 7 were waited for; matrix products, arithmetic and copies ran while one was open for 2% of the time, Pallas kernels for 22%

profile of v6, /device:TPU:0, one launch (start us, length us, event | category | flops | bytes accessed | tf_op | source)
XLA Modules:
  0.0 93.3 jit_solution(14292395318054192485)
XLA Ops:
  2.6 3.1 %collective-permute-start.2 = (f16[520,384]{1,0:T(8,128)(2,1)S(1)}, f16[520,384]{1,0:T(8,128)(2,1)S(1)}, u32[]{:S(2)}, u32[]{:S(2)}) collective-permute-start(f16[520,384]{1,0:T(8,128)(2,1)S(1)} %get-tuple-element.77), channel_id=1, source_target_pairs={{0,8},{4,12},{8,0},{12,4},{16,24},{20,28},{24,16},{28,20},{1,9},{5... | collective-permute-start | bytes 1198088 | tf_op jit(solution)/shard_map/ppermute | solution.py:17
  7.3 2.6 %collective-permute-start = (f16[520,384]{1,0:T(8,128)(2,1)S(1)}, f16[520,384]{1,0:T(8,128)(2,1)S(1)}, u32[]{:S(2)}, u32[]{:S(2)}) collective-permute-start(f16[520,384]{1,0:T(8,128)(2,1)S(1)} %get-tuple-element.77), channel_id=1, source_target_pairs={{0,16},{4,20},{8,24},{12,28},{16,0},{20,4},{24,8},{28,12},{1,17},{... | collective-permute-start | bytes 1198088 | tf_op jit(solution)/shard_map/ppermute | solution.py:17
  10.2 11.8 %collective-permute-done.2 = f16[520,384]{1,0:T(8,128)(2,1)S(1)} collective-permute-done((f16[520,384]{1,0:T(8,128)(2,1)S(1)}, f16[520,384]{1,0:T(8,128)(2,1)S(1)}, u32[]{:S(2)}, u32[]{:S(2)}) %collective-permute-start.2) | collective-permute-done | bytes 399392 | tf_op jit(solution)/shard_map/ppermute | solution.py:17
  22.1 2.3 %collective-permute-start.7 = (f16[520,384]{1,0:T(8,128)(2,1)S(1)}, f16[520,384]{1,0:T(8,128)(2,1)S(1)}, u32[]{:S(2)}, u32[]{:S(2)}) collective-permute-start(f16[520,384]{1,0:T(8,128)(2,1)S(1)} %collective-permute-done.2), channel_id=1, source_target_pairs={{0,4},{4,0},{8,12},{12,8},{16,20},{20,16},{24,28},{28,24},{1,5},{5... | collective-permute-start | bytes 1198088 | tf_op jit(solution)/shard_map/ppermute | solution.py:17
  24.4 5.6 %scatter_traces.3.refs_6_ = f32[2048,384]{1,0:T(8,128)S(1)} custom-call(f32[520,384]{1,0:T(8,128)S(1)} %get-tuple-element.76.refs_0_.refs_1_, f32[520,384]{1,0:T(8,128)S(1)} %get-tuple-element.76.refs_0_.refs_1_, f32[520,384]{1,0:T(8,128)S(1)} %convert_element_type.123.refs_2_.refs_3_, f32[520,384]{1,0:T(8,128)S(1)} %convert_element_type.123.refs_2_.refs_3_, ...), custom_call_target="tpu_custom_call" | custom-call | flops 4831838208 | bytes 6291457 | tf_op jit(solution)/shard_map/scatter_traces/pallas_call | solution.py:122
  30.0 1.6 %copy-done.1 = f32[2048,384]{1,0:T(8,128)} copy-done((f32[2048,384]{1,0:T(8,128)}, f32[2048,384]{1,0:T(8,128)S(1)}, u32[]{:S(2)}) %copy-start.1) | copy-done | bytes 3145752
  31.6 1.6 %collective-permute-done = f16[520,384]{1,0:T(8,128)(2,1)S(1)} collective-permute-done((f16[520,384]{1,0:T(8,128)(2,1)S(1)}, f16[520,384]{1,0:T(8,128)(2,1)S(1)}, u32[]{:S(2)}, u32[]{:S(2)}) %collective-permute-start) | collective-permute-done | bytes 399392 | tf_op jit(solution)/shard_map/ppermute | solution.py:17
  34.0 1.6 %collective-permute-start.6 = (f16[264,384]{1,0:T(8,128)(2,1)S(1)}, f16[264,384]{1,0:T(8,128)(2,1)S(1)}, u32[]{:S(2)}, u32[]{:S(2)}) collective-permute-start(f16[264,384]{1,0:T(8,128)(2,1)S(1)} %collective-permute-done.5), channel_id=1, source_target_pairs={{0,4},{4,0},{8,12},{12,8},{16,20},{20,16},{24,28},{28,24},{1,5},{5... | collective-permute-start | bytes 608264 | tf_op jit(solution)/shard_map/ppermute | solution.py:17
  35.7 2.5 %collective-permute-start.4 = (f16[256,384]{1,0:T(8,128)(2,1)S(1)}, f16[256,384]{1,0:T(8,128)(2,1)S(1)}, u32[]{:S(2)}, u32[]{:S(2)}) collective-permute-start(f16[256,384]{1,0:T(8,128)(2,1)S(1)} %slice.18), channel_id=1, source_target_pairs={{0,24},{4,28},{8,16},{12,20},{16,8},{20,12},{24,0},{28,4},{1,25},{... | collective-permute-start | bytes 589832 | tf_op jit(solution)/shard_map/ppermute | solution.py:17
  38.3 1.9 %copy-done.2 = f32[2048,384]{1,0:T(8,128)S(1)} copy-done((f32[2048,384]{1,0:T(8,128)S(1)}, f32[2048,384]{1,0:T(8,128)}, u32[]{:S(2)}) %copy-start.2) | copy-done | bytes 3145752
  40.2 4.7 %scatter_traces.4.refs_6_ = f32[2048,384]{1,0:T(8,128)S(1)} custom-call(f32[520,384]{1,0:T(8,128)S(1)} %convert_element_type.125.refs_0_.refs_1_, f32[520,384]{1,0:T(8,128)S(1)} %convert_element_type.125.refs_0_.refs_1_, f32[520,384]{1,0:T(8,128)S(1)} %convert_element_type.126.refs_2_.refs_3_, f32[520,384]{1,0:T(8,128)S(1)} %convert_element_type.126.refs_2_.refs_3_, ...), custom_call_target="tpu_custom_call" | custom-call | flops 4026531840 | bytes 6291457 | tf_op jit(solution)/shard_map/scatter_traces/pallas_call | solution.py:122
  47.6 3.9 %scatter_traces.5.refs_2_ = f32[2048,384]{1,0:T(8,128)S(1)} custom-call(f32[520,384]{1,0:T(8,128)S(1)} %convert_element_type.128.refs_0_.refs_1_, f32[520,384]{1,0:T(8,128)S(1)} %convert_element_type.128.refs_0_.refs_1_, f32[256,384]{1,0:T(8,128)S(1)} %convert_element_type.129.refs_2_, f32[264,384]{1,0:T(8,128)S(1)} %convert_element_type.127.refs_4_.refs_5_.refs_3_, ...), custom_call_target="tpu_custom_call" | custom-call | flops 3221225472 | bytes 6291457 | tf_op jit(solution)/shard_map/scatter_traces/pallas_call | solution.py:122
  51.9 3.3 %scatter_and_layer.1 = (bf16[2048,384]{1,0:T(8,128)(2,1)S(1)}, f32[256,384]{1,0:T(8,128)S(1)}, bf16[128,384]{1,0:T(8,128)(2,1)S(1)}, bf16[128,384]{1,0:T(8,128)(2,1)S(1)}) custom-call(s32[2]{0:T(128)S(1)} %pad_add_fusion.place_ref, f32[256,384]{1,0:T(8,128)S(1)} %convert_element_type.131.refs_0_, ...), custom_call_target="tpu_custom_call" | custom-call | flops 1207959552 | bytes 6291457 | tf_op jit(solution)/shard_map/scatter_and_layer/pallas_call | solution.py:184
  55.2 1.6 %collective-permute-start.9 = (bf16[128,384]{1,0:T(8,128)(2,1)S(1)}, bf16[128,384]{1,0:T(8,128)(2,1)S(1)}, u32[]{:S(2)}, u32[]{:S(2)}) collective-permute-start(bf16[128,384]{1,0:T(8,128)(2,1)S(1)} %get-tuple-element.45), channel_id=1, source_target_pairs={{0,2},{1,3},{2,0},{3,1},{4,6},{5,7},{6,4},{7,5},{8,10},{9,11},{10,... | collective-permute-start | bytes 294920 | tf_op jit(solution)/shard_map/ppermute | solution.py:17
  56.7 1.8 %layer_more.2 = (f32[128,384]{1,0:T(8,128)S(1)}, bf16[128,384]{1,0:T(8,128)(2,1)S(1)}, bf16[128,384]{1,0:T(8,128)(2,1)S(1)}, bf16[128,384]{1,0:T(8,128)(2,1)S(1)}) custom-call(s32[2]{0:T(128)S(1)} %pad_add_fusion.place_ref, bf16[2048,384]{1,0:T(8,128)(2,1)S(1)} %get-tuple-element.47.rounded_ref, f32[256,384]{1,0:T(8,128)S(1)} %get-tuple-element.48.own_ref, ...), custom_call_target="tpu_custom_call" | custom-call | flops 805306368 | bytes 1572865 | tf_op jit(solution)/shard_map/layer_more/pallas_call | solution.py:232
  60.6 1.6 %collective-permute-start.13 = (bf16[128,384]{1,0:T(8,128)(2,1)S(1)}, bf16[128,384]{1,0:T(8,128)(2,1)S(1)}, u32[]{:S(2)}, u32[]{:S(2)}) collective-permute-start(bf16[128,384]{1,0:T(8,128)(2,1)S(1)} %get-tuple-element.60), channel_id=1, source_target_pairs={{0,3},{1,2},{2,1},{3,0},{4,7},{5,6},{6,5},{7,4},{8,11},{9,10},{10,... | collective-permute-start | bytes 294920 | tf_op jit(solution)/shard_map/ppermute | solution.py:17
  62.9 3.2 %collective-permute-start.20 = (f16[128,384]{1,0:T(8,128)(2,1)S(1)}, f16[128,384]{1,0:T(8,128)(2,1)S(1)}, u32[]{:S(2)}, u32[]{:S(2)}) collective-permute-start(f16[128,384]{1,0:T(8,128)(2,1)S(1)} %get-tuple-element.74), channel_id=1, source_target_pairs={{0,16},{4,20},{8,24},{12,28},{16,0},{20,4},{24,8},{28,12},{1,17},{... | collective-permute-start | bytes 294920 | tf_op jit(solution)/shard_map/ppermute | solution.py:17
  69.5 4.6 %collective-permute-done.20 = f16[128,384]{1,0:T(8,128)(2,1)S(1)} collective-permute-done((f16[128,384]{1,0:T(8,128)(2,1)S(1)}, f16[128,384]{1,0:T(8,128)(2,1)S(1)}, u32[]{:S(2)}, u32[]{:S(2)}) %collective-permute-start.20) | collective-permute-done | bytes 98336 | tf_op jit(solution)/shard_map/ppermute | solution.py:17
  74.0 2.6 %collective-permute-start.17 = (f16[128,384]{1,0:T(8,128)(2,1)S(1)}, f16[128,384]{1,0:T(8,128)(2,1)S(1)}, u32[]{:S(2)}, u32[]{:S(2)}) collective-permute-start(f16[128,384]{1,0:T(8,128)(2,1)S(1)} %get-tuple-element.71), channel_id=1, source_target_pairs={{0,24},{4,28},{8,16},{12,20},{16,8},{20,12},{24,0},{28,4},{1,25},{... | collective-permute-start | bytes 294920 | tf_op jit(solution)/shard_map/ppermute | solution.py:17
  76.7 3.4 %collective-permute-start.22 = (f16[128,384]{1,0:T(8,128)(2,1)S(1)}, f16[128,384]{1,0:T(8,128)(2,1)S(1)}, u32[]{:S(2)}, u32[]{:S(2)}) collective-permute-start(f16[128,384]{1,0:T(8,128)(2,1)S(1)} %collective-permute-done.19), channel_id=1, source_target_pairs={{0,4},{4,0},{8,12},{12,8},{16,20},{20,16},{24,28},{28,24},{1,5},{5... | collective-permute-start | bytes 294920 | tf_op jit(solution)/shard_map/ppermute | solution.py:17
  80.2 1.9 %collective-permute-start.27 = (f16[128,384]{1,0:T(8,128)(2,1)S(1)}, f16[128,384]{1,0:T(8,128)(2,1)S(1)}, u32[]{:S(2)}, u32[]{:S(2)}) collective-permute-start(f16[128,384]{1,0:T(8,128)(2,1)S(1)} %collective-permute-done.20), channel_id=1, source_target_pairs={{0,4},{4,0},{8,12},{12,8},{16,20},{20,16},{24,28},{28,24},{1,5},{5... | collective-permute-start | bytes 294920 | tf_op jit(solution)/shard_map/ppermute | solution.py:17
  86.2 1.6 %collective-permute-start.18 = (f16[128,384]{1,0:T(8,128)(2,1)S(1)}, f16[128,384]{1,0:T(8,128)(2,1)S(1)}, u32[]{:S(2)}, u32[]{:S(2)}) collective-permute-start(f16[128,384]{1,0:T(8,128)(2,1)S(1)} %collective-permute-done.17), channel_id=1, source_target_pairs={{0,4},{4,0},{8,12},{12,8},{16,20},{20,16},{24,28},{28,24},{1,5},{5... | collective-permute-start | bytes 294920 | tf_op jit(solution)/shard_map/ppermute | solution.py:17
  89.7 1.7 %read_back.4.refs_2_ = f32[512,384]{1,0:T(8,128)S(1)} custom-call(s32[2]{0:T(128)S(1)} %pad_add_fusion.place_ref, s32[512,1]{1,0:T(8,128)S(1)} %copy.11.ids_ref, f32[128,384]{1,0:T(8,128)S(1)} %convert_element_type.140.refs_0_, f32[128,384]{1,0:T(8,128)S(1)} %convert_element_type.141.refs_1_, f32[128,384]{1,0:T(8,128)S(1)} %convert_element_type.142.refs_2_, ...), custom_call_target="tpu_custom_call" | custom-call | flops 1 | bytes 1 | tf_op jit(solution)/shard_map/read_back/pallas_call | solution.py:273
  91.4 1.8 %read_back.5 = f32[512,384]{1,0:T(8,128)} custom-call(s32[2]{0:T(128)S(1)} %pad_add_fusion.place_ref, s32[512,1]{1,0:T(8,128)S(1)} %copy.11.ids_ref, f32[128,384]{1,0:T(8,128)S(1)} %convert_element_type.154.refs_0_, f32[128,384]{1,0:T(8,128)S(1)} %convert_element_type.155.refs_1_, f32[512,384]{1,0:T(8,128)S(1)} %read_back.4.refs_2_), custom_call_target="tpu_custom_call" | custom-call | flops 201326592 | bytes 1572865 | tf_op jit(solution)/shard_map/read_back/pallas_call | solution.py:273
  (93 shorter events, 19.9 us)
Async XLA Ops:
  2.6 19.4 %collective-permute-start.2 = (f16[520,384]{1,0:T(8,128)(2,1)S(1)}, f16[520,384]{1,0:T(8,128)(2,1)S(1)}, u32[]{:S(2)}, u32[]{:S(2)}) collective-permute-start(f16[520,384]{1,0:T(8,128)(2,1)S(1)} %get-tuple-element.77), channel_id=1, source_target_pairs={{0,8},{4,12},{8,0},{12,4},{16,24},{20,28},{24,16},{28,20},{1,9},{5... | collective-permute-start | bytes 1198088 | tf_op jit(solution)/shard_map/ppermute | solution.py:17
  5.7 18.6 %collective-permute-start.1 = (f16[520,384]{1,0:T(8,128)(2,1)S(1)}, f16[520,384]{1,0:T(8,128)(2,1)S(1)}, u32[]{:S(2)}, u32[]{:S(2)}) collective-permute-start(f16[520,384]{1,0:T(8,128)(2,1)S(1)} %get-tuple-element.77), channel_id=1, source_target_pairs={{0,4},{4,0},{8,12},{12,8},{16,20},{20,16},{24,28},{28,24},{1,5},{5... | collective-permute-start | bytes 1198088 | tf_op jit(solution)/shard_map/ppermute | solution.py:17
  7.3 26.0 %collective-permute-start = (f16[520,384]{1,0:T(8,128)(2,1)S(1)}, f16[520,384]{1,0:T(8,128)(2,1)S(1)}, u32[]{:S(2)}, u32[]{:S(2)}) collective-permute-start(f16[520,384]{1,0:T(8,128)(2,1)S(1)} %get-tuple-element.77), channel_id=1, source_target_pairs={{0,16},{4,20},{8,24},{12,28},{16,0},{20,4},{24,8},{28,12},{1,17},{... | collective-permute-start | bytes 1198088 | tf_op jit(solution)/shard_map/ppermute | solution.py:17
  9.9 24.1 %collective-permute-start.5 = (f16[264,384]{1,0:T(8,128)(2,1)S(1)}, f16[264,384]{1,0:T(8,128)(2,1)S(1)}, u32[]{:S(2)}, u32[]{:S(2)}) collective-permute-start(f16[264,384]{1,0:T(8,128)(2,1)S(1)} %slice.19), channel_id=1, source_target_pairs={{0,24},{4,28},{8,16},{12,20},{16,8},{20,12},{24,0},{28,4},{1,25},{... | collective-permute-start | bytes 608264 | tf_op jit(solution)/shard_map/ppermute | solution.py:17
  22.1 16.2 %collective-permute-start.7 = (f16[520,384]{1,0:T(8,128)(2,1)S(1)}, f16[520,384]{1,0:T(8,128)(2,1)S(1)}, u32[]{:S(2)}, u32[]{:S(2)}) collective-permute-start(f16[520,384]{1,0:T(8,128)(2,1)S(1)} %collective-permute-done.2), channel_id=1, source_target_pairs={{0,4},{4,0},{8,12},{12,8},{16,20},{20,16},{24,28},{28,24},{1,5},{5... | collective-permute-start | bytes 1198088 | tf_op jit(solution)/shard_map/ppermute | solution.py:17
  33.2 12.9 %collective-permute-start.3 = (f16[520,384]{1,0:T(8,128)(2,1)S(1)}, f16[520,384]{1,0:T(8,128)(2,1)S(1)}, u32[]{:S(2)}, u32[]{:S(2)}) collective-permute-start(f16[520,384]{1,0:T(8,128)(2,1)S(1)} %collective-permute-done), channel_id=1, source_target_pairs={{0,4},{4,0},{8,12},{12,8},{16,20},{20,16},{24,28},{28,24},{1,5},{5... | collective-permute-start | bytes 1198088 | tf_op jit(solution)/shard_map/ppermute | solution.py:17
  34.0 12.2 %collective-permute-start.6 = (f16[264,384]{1,0:T(8,128)(2,1)S(1)}, f16[264,384]{1,0:T(8,128)(2,1)S(1)}, u32[]{:S(2)}, u32[]{:S(2)}) collective-permute-start(f16[264,384]{1,0:T(8,128)(2,1)S(1)} %collective-permute-done.5), channel_id=1, source_target_pairs={{0,4},{4,0},{8,12},{12,8},{16,20},{20,16},{24,28},{28,24},{1,5},{5... | collective-permute-start | bytes 608264 | tf_op jit(solution)/shard_map/ppermute | solution.py:17
  35.7 10.5 %collective-permute-start.4 = (f16[256,384]{1,0:T(8,128)(2,1)S(1)}, f16[256,384]{1,0:T(8,128)(2,1)S(1)}, u32[]{:S(2)}, u32[]{:S(2)}) collective-permute-start(f16[256,384]{1,0:T(8,128)(2,1)S(1)} %slice.18), channel_id=1, source_target_pairs={{0,24},{4,28},{8,16},{12,20},{16,8},{20,12},{24,0},{28,4},{1,25},{... | collective-permute-start | bytes 589832 | tf_op jit(solution)/shard_map/ppermute | solution.py:17
  55.2 7.0 %collective-permute-start.9 = (bf16[128,384]{1,0:T(8,128)(2,1)S(1)}, bf16[128,384]{1,0:T(8,128)(2,1)S(1)}, u32[]{:S(2)}, u32[]{:S(2)}) collective-permute-start(bf16[128,384]{1,0:T(8,128)(2,1)S(1)} %get-tuple-element.45), channel_id=1, source_target_pairs={{0,2},{1,3},{2,0},{3,1},{4,6},{5,7},{6,4},{7,5},{8,10},{9,11},{10,... | collective-permute-start | bytes 294920 | tf_op jit(solution)/shard_map/ppermute | solution.py:17
  56.7 6.0 %collective-permute-start.10 = (bf16[128,384]{1,0:T(8,128)(2,1)S(1)}, bf16[128,384]{1,0:T(8,128)(2,1)S(1)}, u32[]{:S(2)}, u32[]{:S(2)}) collective-permute-start(bf16[128,384]{1,0:T(8,128)(2,1)S(1)} %get-tuple-element.46), channel_id=1, source_target_pairs={{0,3},{1,2},{2,1},{3,0},{4,7},{5,6},{6,5},{7,4},{8,11},{9,10},{10,... | collective-permute-start | bytes 294920 | tf_op jit(solution)/shard_map/ppermute | solution.py:17
  60.6 6.7 %collective-permute-start.13 = (bf16[128,384]{1,0:T(8,128)(2,1)S(1)}, bf16[128,384]{1,0:T(8,128)(2,1)S(1)}, u32[]{:S(2)}, u32[]{:S(2)}) collective-permute-start(bf16[128,384]{1,0:T(8,128)(2,1)S(1)} %get-tuple-element.60), channel_id=1, source_target_pairs={{0,3},{1,2},{2,1},{3,0},{4,7},{5,6},{6,5},{7,4},{8,11},{9,10},{10,... | collective-permute-start | bytes 294920 | tf_op jit(solution)/shard_map/ppermute | solution.py:17
  62.2 6.4 %collective-permute-start.12 = (bf16[128,384]{1,0:T(8,128)(2,1)S(1)}, bf16[128,384]{1,0:T(8,128)(2,1)S(1)}, u32[]{:S(2)}, u32[]{:S(2)}) collective-permute-start(bf16[128,384]{1,0:T(8,128)(2,1)S(1)} %get-tuple-element.59), channel_id=1, source_target_pairs={{0,2},{1,3},{2,0},{3,1},{4,6},{5,7},{6,4},{7,5},{8,10},{9,11},{10,... | collective-permute-start | bytes 294920 | tf_op jit(solution)/shard_map/ppermute | solution.py:17
  62.8 6.6 %collective-permute-start.19 = (f16[128,384]{1,0:T(8,128)(2,1)S(1)}, f16[128,384]{1,0:T(8,128)(2,1)S(1)}, u32[]{:S(2)}, u32[]{:S(2)}) collective-permute-start(f16[128,384]{1,0:T(8,128)(2,1)S(1)} %get-tuple-element.74), channel_id=1, source_target_pairs={{0,8},{4,12},{8,0},{12,4},{16,24},{20,28},{24,16},{28,20},{1,9},{5... | collective-permute-start | bytes 294920 | tf_op jit(solution)/shard_map/ppermute | solution.py:17
  62.9 11.1 %collective-permute-start.20 = (f16[128,384]{1,0:T(8,128)(2,1)S(1)}, f16[128,384]{1,0:T(8,128)(2,1)S(1)}, u32[]{:S(2)}, u32[]{:S(2)}) collective-permute-start(f16[128,384]{1,0:T(8,128)(2,1)S(1)} %get-tuple-element.74), channel_id=1, source_target_pairs={{0,16},{4,20},{8,24},{12,28},{16,0},{20,4},{24,8},{28,12},{1,17},{... | collective-permute-start | bytes 294920 | tf_op jit(solution)/shard_map/ppermute | solution.py:17
  66.1 7.9 %collective-permute-start.21 = (f16[128,384]{1,0:T(8,128)(2,1)S(1)}, f16[128,384]{1,0:T(8,128)(2,1)S(1)}, u32[]{:S(2)}, u32[]{:S(2)}) collective-permute-start(f16[128,384]{1,0:T(8,128)(2,1)S(1)} %get-tuple-element.74), channel_id=1, source_target_pairs={{0,24},{4,28},{8,16},{12,20},{16,8},{20,12},{24,0},{28,4},{1,25},{... | collective-permute-start | bytes 294920 | tf_op jit(solution)/shard_map/ppermute | solution.py:17
  67.3 9.4 %collective-permute-start.23 = (f16[128,384]{1,0:T(8,128)(2,1)S(1)}, f16[128,384]{1,0:T(8,128)(2,1)S(1)}, u32[]{:S(2)}, u32[]{:S(2)}) collective-permute-start(f16[128,384]{1,0:T(8,128)(2,1)S(1)} %get-tuple-element.74), channel_id=1, source_target_pairs={{0,4},{4,0},{8,12},{12,8},{16,20},{20,16},{24,28},{28,24},{1,5},{5... | collective-permute-start | bytes 294920 | tf_op jit(solution)/shard_map/ppermute | solution.py:17
  68.7 11.4 %collective-permute-start.24 = (f16[128,384]{1,0:T(8,128)(2,1)S(1)}, f16[128,384]{1,0:T(8,128)(2,1)S(1)}, u32[]{:S(2)}, u32[]{:S(2)}) collective-permute-start(f16[128,384]{1,0:T(8,128)(2,1)S(1)} %get-tuple-element.71), channel_id=1, source_target_pairs={{0,4},{4,0},{8,12},{12,8},{16,20},{20,16},{24,28},{28,24},{1,5},{5... | collective-permute-start | bytes 294920 | tf_op jit(solution)/shard_map/ppermute | solution.py:17
  69.5 10.6 %collective-permute-start.25 = (f16[128,384]{1,0:T(8,128)(2,1)S(1)}, f16[128,384]{1,0:T(8,128)(2,1)S(1)}, u32[]{:S(2)}, u32[]{:S(2)}) collective-permute-start(f16[128,384]{1,0:T(8,128)(2,1)S(1)} %get-tuple-element.71), channel_id=1, source_target_pairs={{0,8},{4,12},{8,0},{12,4},{16,24},{20,28},{24,16},{28,20},{1,9},{5... | collective-permute-start | bytes 294920 | tf_op jit(solution)/shard_map/ppermute | solution.py:17
  74.0 8.2 %collective-permute-start.15 = (f16[128,384]{1,0:T(8,128)(2,1)S(1)}, f16[128,384]{1,0:T(8,128)(2,1)S(1)}, u32[]{:S(2)}, u32[]{:S(2)}) collective-permute-start(f16[128,384]{1,0:T(8,128)(2,1)S(1)} %get-tuple-element.71), channel_id=1, source_target_pairs={{0,16},{4,20},{8,24},{12,28},{16,0},{20,4},{24,8},{28,12},{1,17},{... | collective-permute-start | bytes 294920 | tf_op jit(solution)/shard_map/ppermute | solution.py:17
  74.0 11.6 %collective-permute-start.17 = (f16[128,384]{1,0:T(8,128)(2,1)S(1)}, f16[128,384]{1,0:T(8,128)(2,1)S(1)}, u32[]{:S(2)}, u32[]{:S(2)}) collective-permute-start(f16[128,384]{1,0:T(8,128)(2,1)S(1)} %get-tuple-element.71), channel_id=1, source_target_pairs={{0,24},{4,28},{8,16},{12,20},{16,8},{20,12},{24,0},{28,4},{1,25},{... | collective-permute-start | bytes 294920 | tf_op jit(solution)/shard_map/ppermute | solution.py:17
  76.7 9.5 %collective-permute-start.22 = (f16[128,384]{1,0:T(8,128)(2,1)S(1)}, f16[128,384]{1,0:T(8,128)(2,1)S(1)}, u32[]{:S(2)}, u32[]{:S(2)}) collective-permute-start(f16[128,384]{1,0:T(8,128)(2,1)S(1)} %collective-permute-done.19), channel_id=1, source_target_pairs={{0,4},{4,0},{8,12},{12,8},{16,20},{20,16},{24,28},{28,24},{1,5},{5... | collective-permute-start | bytes 294920 | tf_op jit(solution)/shard_map/ppermute | solution.py:17
  80.1 7.8 %collective-permute-start.26 = (f16[128,384]{1,0:T(8,128)(2,1)S(1)}, f16[128,384]{1,0:T(8,128)(2,1)S(1)}, u32[]{:S(2)}, u32[]{:S(2)}) collective-permute-start(f16[128,384]{1,0:T(8,128)(2,1)S(1)} %collective-permute-done.25), channel_id=1, source_target_pairs={{0,4},{4,0},{8,12},{12,8},{16,20},{20,16},{24,28},{28,24},{1,5},{5... | collective-permute-start | bytes 294920 | tf_op jit(solution)/shard_map/ppermute | solution.py:17
  80.2 7.7 %collective-permute-start.27 = (f16[128,384]{1,0:T(8,128)(2,1)S(1)}, f16[128,384]{1,0:T(8,128)(2,1)S(1)}, u32[]{:S(2)}, u32[]{:S(2)}) collective-permute-start(f16[128,384]{1,0:T(8,128)(2,1)S(1)} %collective-permute-done.20), channel_id=1, source_target_pairs={{0,4},{4,0},{8,12},{12,8},{16,20},{20,16},{24,28},{28,24},{1,5},{5... | collective-permute-start | bytes 294920 | tf_op jit(solution)/shard_map/ppermute | solution.py:17
  82.3 6.6 %collective-permute-start.28 = (f16[128,384]{1,0:T(8,128)(2,1)S(1)}, f16[128,384]{1,0:T(8,128)(2,1)S(1)}, u32[]{:S(2)}, u32[]{:S(2)}) collective-permute-start(f16[128,384]{1,0:T(8,128)(2,1)S(1)} %collective-permute-done.21), channel_id=1, source_target_pairs={{0,4},{4,0},{8,12},{12,8},{16,20},{20,16},{24,28},{28,24},{1,5},{5... | collective-permute-start | bytes 294920 | tf_op jit(solution)/shard_map/ppermute | solution.py:17
  (11 other events, 94.2 us)

commit v7 on v6

--- a/solution.py
+++ b/solution.py
@@ -97,8 +97,8 @@
 
     picks = []
     for part, tail in zip(rows, refs[1::2]):
-        node = first_node + lax.broadcasted_iota(jnp.int32, (tile, part.count), 0)
-        ids = ids_of(tail, slots, nodes, node_dev)[:, part.span[0] : part.span[1]]
+        node = lax.broadcasted_iota(jnp.int32, (tile, part.count), 0)
+        ids = ids_of(tail, slots, nodes, node_dev)[:, part.span[0] : part.span[1]] - first_node
         picks.append(jnp.where(ids == node, 1.0, 0.0).astype(jnp.bfloat16))
     total = jnp.dot(jnp.concatenate(picks, axis=1), both[...], preferred_element_type=jnp.float32)
     images = total.shape[1] // 2

time: 93.5 us -> 93.5 us (level)
  no operation moved by 1% of the time
where the time goes in v7:
time: 93.5 us; the launch traced here: 93.2 us
  starting transfers between devices  38.5 us (41%)
  Pallas kernels  25.5 us (27%)
  waiting for transfers between devices  20.8 us (22%)
  local copies, waits for them, and re-layouts  3.88 us (4%)
  other arithmetic  3.59 us (4%)
  between operations  1.01 us (1%)
    ppermute x29, starting transfers between devices, exchange(): return lax.ppermute(block, axis, [(i, i ^ offset) for i in range(count)])  38.5 us
    ppermute x29, waiting for transfers between devices, exchange(): return lax.ppermute(block, axis, [(i, i ^ offset) for i in range(count)])  20.8 us
    pallas_call x3, Pallas kernels, scatter(): pl.pallas_call(body, grid=(nodes // tile,), in_specs=row_specs(rows) + [p...  14.2 us
    pallas_call x3, Pallas kernels, read_back(): pl.pallas_call(body, in_specs=[pl.BlockSpec(memory_space=pltpu.SMEM)] + [...  4.97 us
    unnamed x12, local copies, waits for them, and re-layouts  3.53 us
    pallas_call x1, Pallas kernels, scatter_and_layer(): pl.pallas_call(body, grid_spec=pltpu.PrefetchScalarGridSpec(num_scalar_pr...  3.25 us
    pallas_call x2, Pallas kernels, layer_more(): pl.pallas_call(body, grid_spec=pltpu.PrefetchScalarGridSpec(num_scalar_pr...  3.05 us
  transfers between devices with their start and end apart: 29, of which 7 were waited for; matrix products, arithmetic and copies ran while one was open for 2% of the time, Pallas kernels for 22%

profile of v7, /device:TPU:0, one launch (start us, length us, event | category | flops | bytes accessed | tf_op | source)
XLA Modules:
  0.0 93.2 jit_solution(11780976357901183818)
XLA Ops:
  2.6 3.1 %collective-permute-start.2 = (f16[520,384]{1,0:T(8,128)(2,1)S(1)}, f16[520,384]{1,0:T(8,128)(2,1)S(1)}, u32[]{:S(2)}, u32[]{:S(2)}) collective-permute-start(f16[520,384]{1,0:T(8,128)(2,1)S(1)} %get-tuple-element.77), channel_id=1, source_target_pairs={{0,8},{4,12},{8,0},{12,4},{16,24},{20,28},{24,16},{28,20},{1,9},{5... | collective-permute-start | bytes 1198088 | tf_op jit(solution)/shard_map/ppermute | solution.py:17
  7.3 2.6 %collective-permute-start = (f16[520,384]{1,0:T(8,128)(2,1)S(1)}, f16[520,384]{1,0:T(8,128)(2,1)S(1)}, u32[]{:S(2)}, u32[]{:S(2)}) collective-permute-start(f16[520,384]{1,0:T(8,128)(2,1)S(1)} %get-tuple-element.77), channel_id=1, source_target_pairs={{0,16},{4,20},{8,24},{12,28},{16,0},{20,4},{24,8},{28,12},{1,17},{... | collective-permute-start | bytes 1198088 | tf_op jit(solution)/shard_map/ppermute | solution.py:17
  10.2 11.8 %collective-permute-done.2 = f16[520,384]{1,0:T(8,128)(2,1)S(1)} collective-permute-done((f16[520,384]{1,0:T(8,128)(2,1)S(1)}, f16[520,384]{1,0:T(8,128)(2,1)S(1)}, u32[]{:S(2)}, u32[]{:S(2)}) %collective-permute-start.2) | collective-permute-done | bytes 399392 | tf_op jit(solution)/shard_map/ppermute | solution.py:17
  22.1 2.3 %collective-permute-start.7 = (f16[520,384]{1,0:T(8,128)(2,1)S(1)}, f16[520,384]{1,0:T(8,128)(2,1)S(1)}, u32[]{:S(2)}, u32[]{:S(2)}) collective-permute-start(f16[520,384]{1,0:T(8,128)(2,1)S(1)} %collective-permute-done.2), channel_id=1, source_target_pairs={{0,4},{4,0},{8,12},{12,8},{16,20},{20,16},{24,28},{28,24},{1,5},{5... | collective-permute-start | bytes 1198088 | tf_op jit(solution)/shard_map/ppermute | solution.py:17
  24.4 5.6 %scatter_traces.3.refs_6_ = f32[2048,384]{1,0:T(8,128)S(1)} custom-call(f32[520,384]{1,0:T(8,128)S(1)} %get-tuple-element.76.refs_0_.refs_1_, f32[520,384]{1,0:T(8,128)S(1)} %get-tuple-element.76.refs_0_.refs_1_, f32[520,384]{1,0:T(8,128)S(1)} %convert_element_type.123.refs_2_.refs_3_, f32[520,384]{1,0:T(8,128)S(1)} %convert_element_type.123.refs_2_.refs_3_, ...), custom_call_target="tpu_custom_call" | custom-call | flops 4831838208 | bytes 6291457 | tf_op jit(solution)/shard_map/scatter_traces/pallas_call | solution.py:122
  30.0 1.6 %copy-done.1 = f32[2048,384]{1,0:T(8,128)} copy-done((f32[2048,384]{1,0:T(8,128)}, f32[2048,384]{1,0:T(8,128)S(1)}, u32[]{:S(2)}) %copy-start.1) | copy-done | bytes 3145752
  31.6 1.6 %collective-permute-done = f16[520,384]{1,0:T(8,128)(2,1)S(1)} collective-permute-done((f16[520,384]{1,0:T(8,128)(2,1)S(1)}, f16[520,384]{1,0:T(8,128)(2,1)S(1)}, u32[]{:S(2)}, u32[]{:S(2)}) %collective-permute-start) | collective-permute-done | bytes 399392 | tf_op jit(solution)/shard_map/ppermute | solution.py:17
  34.0 1.6 %collective-permute-start.6 = (f16[264,384]{1,0:T(8,128)(2,1)S(1)}, f16[264,384]{1,0:T(8,128)(2,1)S(1)}, u32[]{:S(2)}, u32[]{:S(2)}) collective-permute-start(f16[264,384]{1,0:T(8,128)(2,1)S(1)} %collective-permute-done.5), channel_id=1, source_target_pairs={{0,4},{4,0},{8,12},{12,8},{16,20},{20,16},{24,28},{28,24},{1,5},{5... | collective-permute-start | bytes 608264 | tf_op jit(solution)/shard_map/ppermute | solution.py:17
  35.7 2.5 %collective-permute-start.4 = (f16[256,384]{1,0:T(8,128)(2,1)S(1)}, f16[256,384]{1,0:T(8,128)(2,1)S(1)}, u32[]{:S(2)}, u32[]{:S(2)}) collective-permute-start(f16[256,384]{1,0:T(8,128)(2,1)S(1)} %slice.18), channel_id=1, source_target_pairs={{0,24},{4,28},{8,16},{12,20},{16,8},{20,12},{24,0},{28,4},{1,25},{... | collective-permute-start | bytes 589832 | tf_op jit(solution)/shard_map/ppermute | solution.py:17
  38.3 1.9 %copy-done.2 = f32[2048,384]{1,0:T(8,128)S(1)} copy-done((f32[2048,384]{1,0:T(8,128)S(1)}, f32[2048,384]{1,0:T(8,128)}, u32[]{:S(2)}) %copy-start.2) | copy-done | bytes 3145752
  40.2 4.7 %scatter_traces.4.refs_6_ = f32[2048,384]{1,0:T(8,128)S(1)} custom-call(f32[520,384]{1,0:T(8,128)S(1)} %convert_element_type.125.refs_0_.refs_1_, f32[520,384]{1,0:T(8,128)S(1)} %convert_element_type.125.refs_0_.refs_1_, f32[520,384]{1,0:T(8,128)S(1)} %convert_element_type.126.refs_2_.refs_3_, f32[520,384]{1,0:T(8,128)S(1)} %convert_element_type.126.refs_2_.refs_3_, ...), custom_call_target="tpu_custom_call" | custom-call | flops 4026531840 | bytes 6291457 | tf_op jit(solution)/shard_map/scatter_traces/pallas_call | solution.py:122
  47.6 3.9 %scatter_traces.5.refs_2_ = f32[2048,384]{1,0:T(8,128)S(1)} custom-call(f32[520,384]{1,0:T(8,128)S(1)} %convert_element_type.128.refs_0_.refs_1_, f32[520,384]{1,0:T(8,128)S(1)} %convert_element_type.128.refs_0_.refs_1_, f32[256,384]{1,0:T(8,128)S(1)} %convert_element_type.129.refs_2_, f32[264,384]{1,0:T(8,128)S(1)} %convert_element_type.127.refs_4_.refs_5_.refs_3_, ...), custom_call_target="tpu_custom_call" | custom-call | flops 3221225472 | bytes 6291457 | tf_op jit(solution)/shard_map/scatter_traces/pallas_call | solution.py:122
  51.9 3.2 %scatter_and_layer.1 = (bf16[2048,384]{1,0:T(8,128)(2,1)S(1)}, f32[256,384]{1,0:T(8,128)S(1)}, bf16[128,384]{1,0:T(8,128)(2,1)S(1)}, bf16[128,384]{1,0:T(8,128)(2,1)S(1)}) custom-call(s32[2]{0:T(128)S(1)} %pad_add_fusion.place_ref, f32[256,384]{1,0:T(8,128)S(1)} %convert_element_type.131.refs_0_, ...), custom_call_target="tpu_custom_call" | custom-call | flops 1207959552 | bytes 6291457 | tf_op jit(solution)/shard_map/scatter_and_layer/pallas_call | solution.py:184
  55.1 1.6 %collective-permute-start.9 = (bf16[128,384]{1,0:T(8,128)(2,1)S(1)}, bf16[128,384]{1,0:T(8,128)(2,1)S(1)}, u32[]{:S(2)}, u32[]{:S(2)}) collective-permute-start(bf16[128,384]{1,0:T(8,128)(2,1)S(1)} %get-tuple-element.45), channel_id=1, source_target_pairs={{0,2},{1,3},{2,0},{3,1},{4,6},{5,7},{6,4},{7,5},{8,10},{9,11},{10,... | collective-permute-start | bytes 294920 | tf_op jit(solution)/shard_map/ppermute | solution.py:17
  56.7 1.8 %layer_more.2 = (f32[128,384]{1,0:T(8,128)S(1)}, bf16[128,384]{1,0:T(8,128)(2,1)S(1)}, bf16[128,384]{1,0:T(8,128)(2,1)S(1)}, bf16[128,384]{1,0:T(8,128)(2,1)S(1)}) custom-call(s32[2]{0:T(128)S(1)} %pad_add_fusion.place_ref, bf16[2048,384]{1,0:T(8,128)(2,1)S(1)} %get-tuple-element.47.rounded_ref, f32[256,384]{1,0:T(8,128)S(1)} %get-tuple-element.48.own_ref, ...), custom_call_target="tpu_custom_call" | custom-call | flops 805306368 | bytes 1572865 | tf_op jit(solution)/shard_map/layer_more/pallas_call | solution.py:232
  60.6 1.6 %collective-permute-start.13 = (bf16[128,384]{1,0:T(8,128)(2,1)S(1)}, bf16[128,384]{1,0:T(8,128)(2,1)S(1)}, u32[]{:S(2)}, u32[]{:S(2)}) collective-permute-start(bf16[128,384]{1,0:T(8,128)(2,1)S(1)} %get-tuple-element.60), channel_id=1, source_target_pairs={{0,3},{1,2},{2,1},{3,0},{4,7},{5,6},{6,5},{7,4},{8,11},{9,10},{10,... | collective-permute-start | bytes 294920 | tf_op jit(solution)/shard_map/ppermute | solution.py:17
  62.9 3.2 %collective-permute-start.20 = (f16[128,384]{1,0:T(8,128)(2,1)S(1)}, f16[128,384]{1,0:T(8,128)(2,1)S(1)}, u32[]{:S(2)}, u32[]{:S(2)}) collective-permute-start(f16[128,384]{1,0:T(8,128)(2,1)S(1)} %get-tuple-element.74), channel_id=1, source_target_pairs={{0,16},{4,20},{8,24},{12,28},{16,0},{20,4},{24,8},{28,12},{1,17},{... | collective-permute-start | bytes 294920 | tf_op jit(solution)/shard_map/ppermute | solution.py:17
  69.4 4.6 %collective-permute-done.20 = f16[128,384]{1,0:T(8,128)(2,1)S(1)} collective-permute-done((f16[128,384]{1,0:T(8,128)(2,1)S(1)}, f16[128,384]{1,0:T(8,128)(2,1)S(1)}, u32[]{:S(2)}, u32[]{:S(2)}) %collective-permute-start.20) | collective-permute-done | bytes 98336 | tf_op jit(solution)/shard_map/ppermute | solution.py:17
  74.0 2.6 %collective-permute-start.17 = (f16[128,384]{1,0:T(8,128)(2,1)S(1)}, f16[128,384]{1,0:T(8,128)(2,1)S(1)}, u32[]{:S(2)}, u32[]{:S(2)}) collective-permute-start(f16[128,384]{1,0:T(8,128)(2,1)S(1)} %get-tuple-element.71), channel_id=1, source_target_pairs={{0,24},{4,28},{8,16},{12,20},{16,8},{20,12},{24,0},{28,4},{1,25},{... | collective-permute-start | bytes 294920 | tf_op jit(solution)/shard_map/ppermute | solution.py:17
  76.6 3.4 %collective-permute-start.22 = (f16[128,384]{1,0:T(8,128)(2,1)S(1)}, f16[128,384]{1,0:T(8,128)(2,1)S(1)}, u32[]{:S(2)}, u32[]{:S(2)}) collective-permute-start(f16[128,384]{1,0:T(8,128)(2,1)S(1)} %collective-permute-done.19), channel_id=1, source_target_pairs={{0,4},{4,0},{8,12},{12,8},{16,20},{20,16},{24,28},{28,24},{1,5},{5... | collective-permute-start | bytes 294920 | tf_op jit(solution)/shard_map/ppermute | solution.py:17
  80.1 1.9 %collective-permute-start.27 = (f16[128,384]{1,0:T(8,128)(2,1)S(1)}, f16[128,384]{1,0:T(8,128)(2,1)S(1)}, u32[]{:S(2)}, u32[]{:S(2)}) collective-permute-start(f16[128,384]{1,0:T(8,128)(2,1)S(1)} %collective-permute-done.20), channel_id=1, source_target_pairs={{0,4},{4,0},{8,12},{12,8},{16,20},{20,16},{24,28},{28,24},{1,5},{5... | collective-permute-start | bytes 294920 | tf_op jit(solution)/shard_map/ppermute | solution.py:17
  86.2 1.6 %collective-permute-start.18 = (f16[128,384]{1,0:T(8,128)(2,1)S(1)}, f16[128,384]{1,0:T(8,128)(2,1)S(1)}, u32[]{:S(2)}, u32[]{:S(2)}) collective-permute-start(f16[128,384]{1,0:T(8,128)(2,1)S(1)} %collective-permute-done.17), channel_id=1, source_target_pairs={{0,4},{4,0},{8,12},{12,8},{16,20},{20,16},{24,28},{28,24},{1,5},{5... | collective-permute-start | bytes 294920 | tf_op jit(solution)/shard_map/ppermute | solution.py:17
  89.7 1.7 %read_back.4.refs_2_ = f32[512,384]{1,0:T(8,128)S(1)} custom-call(s32[2]{0:T(128)S(1)} %pad_add_fusion.place_ref, s32[512,1]{1,0:T(8,128)S(1)} %copy.11.ids_ref, f32[128,384]{1,0:T(8,128)S(1)} %convert_element_type.140.refs_0_, f32[128,384]{1,0:T(8,128)S(1)} %convert_element_type.141.refs_1_, f32[128,384]{1,0:T(8,128)S(1)} %convert_element_type.142.refs_2_, ...), custom_call_target="tpu_custom_call" | custom-call | flops 1 | bytes 1 | tf_op jit(solution)/shard_map/read_back/pallas_call | solution.py:273
  91.4 1.8 %read_back.5 = f32[512,384]{1,0:T(8,128)} custom-call(s32[2]{0:T(128)S(1)} %pad_add_fusion.place_ref, s32[512,1]{1,0:T(8,128)S(1)} %copy.11.ids_ref, f32[128,384]{1,0:T(8,128)S(1)} %convert_element_type.154.refs_0_, f32[128,384]{1,0:T(8,128)S(1)} %convert_element_type.155.refs_1_, f32[512,384]{1,0:T(8,128)S(1)} %read_back.4.refs_2_), custom_call_target="tpu_custom_call" | custom-call | flops 201326592 | bytes 1572865 | tf_op jit(solution)/shard_map/read_back/pallas_call | solution.py:273
  (93 shorter events, 19.9 us)
Async XLA Ops:
  2.6 19.4 %collective-permute-start.2 = (f16[520,384]{1,0:T(8,128)(2,1)S(1)}, f16[520,384]{1,0:T(8,128)(2,1)S(1)}, u32[]{:S(2)}, u32[]{:S(2)}) collective-permute-start(f16[520,384]{1,0:T(8,128)(2,1)S(1)} %get-tuple-element.77), channel_id=1, source_target_pairs={{0,8},{4,12},{8,0},{12,4},{16,24},{20,28},{24,16},{28,20},{1,9},{5... | collective-permute-start | bytes 1198088 | tf_op jit(solution)/shard_map/ppermute | solution.py:17
  5.7 18.6 %collective-permute-start.1 = (f16[520,384]{1,0:T(8,128)(2,1)S(1)}, f16[520,384]{1,0:T(8,128)(2,1)S(1)}, u32[]{:S(2)}, u32[]{:S(2)}) collective-permute-start(f16[520,384]{1,0:T(8,128)(2,1)S(1)} %get-tuple-element.77), channel_id=1, source_target_pairs={{0,4},{4,0},{8,12},{12,8},{16,20},{20,16},{24,28},{28,24},{1,5},{5... | collective-permute-start | bytes 1198088 | tf_op jit(solution)/shard_map/ppermute | solution.py:17
  7.3 26.0 %collective-permute-start = (f16[520,384]{1,0:T(8,128)(2,1)S(1)}, f16[520,384]{1,0:T(8,128)(2,1)S(1)}, u32[]{:S(2)}, u32[]{:S(2)}) collective-permute-start(f16[520,384]{1,0:T(8,128)(2,1)S(1)} %get-tuple-element.77), channel_id=1, source_target_pairs={{0,16},{4,20},{8,24},{12,28},{16,0},{20,4},{24,8},{28,12},{1,17},{... | collective-permute-start | bytes 1198088 | tf_op jit(solution)/shard_map/ppermute | solution.py:17
  9.9 24.1 %collective-permute-start.5 = (f16[264,384]{1,0:T(8,128)(2,1)S(1)}, f16[264,384]{1,0:T(8,128)(2,1)S(1)}, u32[]{:S(2)}, u32[]{:S(2)}) collective-permute-start(f16[264,384]{1,0:T(8,128)(2,1)S(1)} %slice.19), channel_id=1, source_target_pairs={{0,24},{4,28},{8,16},{12,20},{16,8},{20,12},{24,0},{28,4},{1,25},{... | collective-permute-start | bytes 608264 | tf_op jit(solution)/shard_map/ppermute | solution.py:17
  22.1 16.2 %collective-permute-start.7 = (f16[520,384]{1,0:T(8,128)(2,1)S(1)}, f16[520,384]{1,0:T(8,128)(2,1)S(1)}, u32[]{:S(2)}, u32[]{:S(2)}) collective-permute-start(f16[520,384]{1,0:T(8,128)(2,1)S(1)} %collective-permute-done.2), channel_id=1, source_target_pairs={{0,4},{4,0},{8,12},{12,8},{16,20},{20,16},{24,28},{28,24},{1,5},{5... | collective-permute-start | bytes 1198088 | tf_op jit(solution)/shard_map/ppermute | solution.py:17
  33.2 12.9 %collective-permute-start.3 = (f16[520,384]{1,0:T(8,128)(2,1)S(1)}, f16[520,384]{1,0:T(8,128)(2,1)S(1)}, u32[]{:S(2)}, u32[]{:S(2)}) collective-permute-start(f16[520,384]{1,0:T(8,128)(2,1)S(1)} %collective-permute-done), channel_id=1, source_target_pairs={{0,4},{4,0},{8,12},{12,8},{16,20},{20,16},{24,28},{28,24},{1,5},{5... | collective-permute-start | bytes 1198088 | tf_op jit(solution)/shard_map/ppermute | solution.py:17
  34.0 12.1 %collective-permute-start.6 = (f16[264,384]{1,0:T(8,128)(2,1)S(1)}, f16[264,384]{1,0:T(8,128)(2,1)S(1)}, u32[]{:S(2)}, u32[]{:S(2)}) collective-permute-start(f16[264,384]{1,0:T(8,128)(2,1)S(1)} %collective-permute-done.5), channel_id=1, source_target_pairs={{0,4},{4,0},{8,12},{12,8},{16,20},{20,16},{24,28},{28,24},{1,5},{5... | collective-permute-start | bytes 608264 | tf_op jit(solution)/shard_map/ppermute | solution.py:17
  35.7 10.5 %collective-permute-start.4 = (f16[256,384]{1,0:T(8,128)(2,1)S(1)}, f16[256,384]{1,0:T(8,128)(2,1)S(1)}, u32[]{:S(2)}, u32[]{:S(2)}) collective-permute-start(f16[256,384]{1,0:T(8,128)(2,1)S(1)} %slice.18), channel_id=1, source_target_pairs={{0,24},{4,28},{8,16},{12,20},{16,8},{20,12},{24,0},{28,4},{1,25},{... | collective-permute-start | bytes 589832 | tf_op jit(solution)/shard_map/ppermute | solution.py:17
  55.1 7.0 %collective-permute-start.9 = (bf16[128,384]{1,0:T(8,128)(2,1)S(1)}, bf16[128,384]{1,0:T(8,128)(2,1)S(1)}, u32[]{:S(2)}, u32[]{:S(2)}) collective-permute-start(bf16[128,384]{1,0:T(8,128)(2,1)S(1)} %get-tuple-element.45), channel_id=1, source_target_pairs={{0,2},{1,3},{2,0},{3,1},{4,6},{5,7},{6,4},{7,5},{8,10},{9,11},{10,... | collective-permute-start | bytes 294920 | tf_op jit(solution)/shard_map/ppermute | solution.py:17
  56.7 6.0 %collective-permute-start.10 = (bf16[128,384]{1,0:T(8,128)(2,1)S(1)}, bf16[128,384]{1,0:T(8,128)(2,1)S(1)}, u32[]{:S(2)}, u32[]{:S(2)}) collective-permute-start(bf16[128,384]{1,0:T(8,128)(2,1)S(1)} %get-tuple-element.46), channel_id=1, source_target_pairs={{0,3},{1,2},{2,1},{3,0},{4,7},{5,6},{6,5},{7,4},{8,11},{9,10},{10,... | collective-permute-start | bytes 294920 | tf_op jit(solution)/shard_map/ppermute | solution.py:17
  60.6 6.7 %collective-permute-start.13 = (bf16[128,384]{1,0:T(8,128)(2,1)S(1)}, bf16[128,384]{1,0:T(8,128)(2,1)S(1)}, u32[]{:S(2)}, u32[]{:S(2)}) collective-permute-start(bf16[128,384]{1,0:T(8,128)(2,1)S(1)} %get-tuple-element.60), channel_id=1, source_target_pairs={{0,3},{1,2},{2,1},{3,0},{4,7},{5,6},{6,5},{7,4},{8,11},{9,10},{10,... | collective-permute-start | bytes 294920 | tf_op jit(solution)/shard_map/ppermute | solution.py:17
  62.2 6.4 %collective-permute-start.12 = (bf16[128,384]{1,0:T(8,128)(2,1)S(1)}, bf16[128,384]{1,0:T(8,128)(2,1)S(1)}, u32[]{:S(2)}, u32[]{:S(2)}) collective-permute-start(bf16[128,384]{1,0:T(8,128)(2,1)S(1)} %get-tuple-element.59), channel_id=1, source_target_pairs={{0,2},{1,3},{2,0},{3,1},{4,6},{5,7},{6,4},{7,5},{8,10},{9,11},{10,... | collective-permute-start | bytes 294920 | tf_op jit(solution)/shard_map/ppermute | solution.py:17
  62.8 6.6 %collective-permute-start.19 = (f16[128,384]{1,0:T(8,128)(2,1)S(1)}, f16[128,384]{1,0:T(8,128)(2,1)S(1)}, u32[]{:S(2)}, u32[]{:S(2)}) collective-permute-start(f16[128,384]{1,0:T(8,128)(2,1)S(1)} %get-tuple-element.74), channel_id=1, source_target_pairs={{0,8},{4,12},{8,0},{12,4},{16,24},{20,28},{24,16},{28,20},{1,9},{5... | collective-permute-start | bytes 294920 | tf_op jit(solution)/shard_map/ppermute | solution.py:17
  62.9 11.2 %collective-permute-start.20 = (f16[128,384]{1,0:T(8,128)(2,1)S(1)}, f16[128,384]{1,0:T(8,128)(2,1)S(1)}, u32[]{:S(2)}, u32[]{:S(2)}) collective-permute-start(f16[128,384]{1,0:T(8,128)(2,1)S(1)} %get-tuple-element.74), channel_id=1, source_target_pairs={{0,16},{4,20},{8,24},{12,28},{16,0},{20,4},{24,8},{28,12},{1,17},{... | collective-permute-start | bytes 294920 | tf_op jit(solution)/shard_map/ppermute | solution.py:17
  66.1 8.0 %collective-permute-start.21 = (f16[128,384]{1,0:T(8,128)(2,1)S(1)}, f16[128,384]{1,0:T(8,128)(2,1)S(1)}, u32[]{:S(2)}, u32[]{:S(2)}) collective-permute-start(f16[128,384]{1,0:T(8,128)(2,1)S(1)} %get-tuple-element.74), channel_id=1, source_target_pairs={{0,24},{4,28},{8,16},{12,20},{16,8},{20,12},{24,0},{28,4},{1,25},{... | collective-permute-start | bytes 294920 | tf_op jit(solution)/shard_map/ppermute | solution.py:17
  67.2 9.4 %collective-permute-start.23 = (f16[128,384]{1,0:T(8,128)(2,1)S(1)}, f16[128,384]{1,0:T(8,128)(2,1)S(1)}, u32[]{:S(2)}, u32[]{:S(2)}) collective-permute-start(f16[128,384]{1,0:T(8,128)(2,1)S(1)} %get-tuple-element.74), channel_id=1, source_target_pairs={{0,4},{4,0},{8,12},{12,8},{16,20},{20,16},{24,28},{28,24},{1,5},{5... | collective-permute-start | bytes 294920 | tf_op jit(solution)/shard_map/ppermute | solution.py:17
  68.7 11.4 %collective-permute-start.24 = (f16[128,384]{1,0:T(8,128)(2,1)S(1)}, f16[128,384]{1,0:T(8,128)(2,1)S(1)}, u32[]{:S(2)}, u32[]{:S(2)}) collective-permute-start(f16[128,384]{1,0:T(8,128)(2,1)S(1)} %get-tuple-element.71), channel_id=1, source_target_pairs={{0,4},{4,0},{8,12},{12,8},{16,20},{20,16},{24,28},{28,24},{1,5},{5... | collective-permute-start | bytes 294920 | tf_op jit(solution)/shard_map/ppermute | solution.py:17
  69.4 10.6 %collective-permute-start.25 = (f16[128,384]{1,0:T(8,128)(2,1)S(1)}, f16[128,384]{1,0:T(8,128)(2,1)S(1)}, u32[]{:S(2)}, u32[]{:S(2)}) collective-permute-start(f16[128,384]{1,0:T(8,128)(2,1)S(1)} %get-tuple-element.71), channel_id=1, source_target_pairs={{0,8},{4,12},{8,0},{12,4},{16,24},{20,28},{24,16},{28,20},{1,9},{5... | collective-permute-start | bytes 294920 | tf_op jit(solution)/shard_map/ppermute | solution.py:17
  74.0 8.2 %collective-permute-start.15 = (f16[128,384]{1,0:T(8,128)(2,1)S(1)}, f16[128,384]{1,0:T(8,128)(2,1)S(1)}, u32[]{:S(2)}, u32[]{:S(2)}) collective-permute-start(f16[128,384]{1,0:T(8,128)(2,1)S(1)} %get-tuple-element.71), channel_id=1, source_target_pairs={{0,16},{4,20},{8,24},{12,28},{16,0},{20,4},{24,8},{28,12},{1,17},{... | collective-permute-start | bytes 294920 | tf_op jit(solution)/shard_map/ppermute | solution.py:17
  74.0 11.6 %collective-permute-start.17 = (f16[128,384]{1,0:T(8,128)(2,1)S(1)}, f16[128,384]{1,0:T(8,128)(2,1)S(1)}, u32[]{:S(2)}, u32[]{:S(2)}) collective-permute-start(f16[128,384]{1,0:T(8,128)(2,1)S(1)} %get-tuple-element.71), channel_id=1, source_target_pairs={{0,24},{4,28},{8,16},{12,20},{16,8},{20,12},{24,0},{28,4},{1,25},{... | collective-permute-start | bytes 294920 | tf_op jit(solution)/shard_map/ppermute | solution.py:17
  76.6 9.5 %collective-permute-start.22 = (f16[128,384]{1,0:T(8,128)(2,1)S(1)}, f16[128,384]{1,0:T(8,128)(2,1)S(1)}, u32[]{:S(2)}, u32[]{:S(2)}) collective-permute-start(f16[128,384]{1,0:T(8,128)(2,1)S(1)} %collective-permute-done.19), channel_id=1, source_target_pairs={{0,4},{4,0},{8,12},{12,8},{16,20},{20,16},{24,28},{28,24},{1,5},{5... | collective-permute-start | bytes 294920 | tf_op jit(solution)/shard_map/ppermute | solution.py:17
  80.1 7.8 %collective-permute-start.26 = (f16[128,384]{1,0:T(8,128)(2,1)S(1)}, f16[128,384]{1,0:T(8,128)(2,1)S(1)}, u32[]{:S(2)}, u32[]{:S(2)}) collective-permute-start(f16[128,384]{1,0:T(8,128)(2,1)S(1)} %collective-permute-done.25), channel_id=1, source_target_pairs={{0,4},{4,0},{8,12},{12,8},{16,20},{20,16},{24,28},{28,24},{1,5},{5... | collective-permute-start | bytes 294920 | tf_op jit(solution)/shard_map/ppermute | solution.py:17
  80.1 7.7 %collective-permute-start.27 = (f16[128,384]{1,0:T(8,128)(2,1)S(1)}, f16[128,384]{1,0:T(8,128)(2,1)S(1)}, u32[]{:S(2)}, u32[]{:S(2)}) collective-permute-start(f16[128,384]{1,0:T(8,128)(2,1)S(1)} %collective-permute-done.20), channel_id=1, source_target_pairs={{0,4},{4,0},{8,12},{12,8},{16,20},{20,16},{24,28},{28,24},{1,5},{5... | collective-permute-start | bytes 294920 | tf_op jit(solution)/shard_map/ppermute | solution.py:17
  82.2 6.6 %collective-permute-start.28 = (f16[128,384]{1,0:T(8,128)(2,1)S(1)}, f16[128,384]{1,0:T(8,128)(2,1)S(1)}, u32[]{:S(2)}, u32[]{:S(2)}) collective-permute-start(f16[128,384]{1,0:T(8,128)(2,1)S(1)} %collective-permute-done.21), channel_id=1, source_target_pairs={{0,4},{4,0},{8,12},{12,8},{16,20},{20,16},{24,28},{28,24},{1,5},{5... | collective-permute-start | bytes 294920 | tf_op jit(solution)/shard_map/ppermute | solution.py:17
  (11 other events, 94.3 us)
